TPU v7x, 32 devices: a whole 2x2x4 slice. The times are simulated.
32 devices in a mesh: replica: 8 (over z, x), tensor: 4 (over y, core).
Axes of the slice: x: 2, y: 2, z: 4, core: 2. Of those that a mesh axis runs over, the one named last changes fastest.
Arguments:
- hidden_input: bfloat16 [512, 3584], P('replica', 'tensor'), may hold values from -6 to 6
- queries: bfloat16 [512, 2048], P('replica', 'tensor'), may hold values from -8 to 8
- prompt_cache: bfloat16 [32, 2, 2048, 1024], P('replica', None, None, 'tensor'), may hold values from -8 to 8
- suffix_cache: bfloat16 [512, 2, 64, 1024], P('replica', None, None, 'tensor'), may hold values from -6 to 6
- owner_replica: int32 [512, 1], P('replica'), may hold values from 0 to 7; in each aligned block of 64 rows (0 to 63, 64 to 127, ...) at most 16 rows name the same one
- group_slot: int32 [512], P('replica'), may hold values from 0 to 3
- prompt_length: int32 [32], P('replica'), may hold values from 256 to 2048
- suffix_length: int32 [512], P('replica'), may hold values from 1 to 64
- output_weight: bfloat16 [2048, 3584], P('tensor'), may hold values from -0.1875 to 0.1875
- post_gain: float32 [3584], P('tensor'), may hold values from 0.1 to 1.9
Outputs:
- hidden_output: bfloat16 [512, 3584], P('replica', 'tensor')
Inputs may be any that keep to these rules, and one draw needn't show every extreme that they name: `owner_replica`: among the 64 requests of one replica, no owner replica is named more than 16 times.
All inputs are finite; a program needn't handle non-finite values.
Results may differ from a plain program's by a relative error of at most 0.0048.
Values may be sent and summed in bfloat16 or wider, within the bound.
No kernel may reach another device: no remote copies, remote signals or barrier semaphores. Data moves between devices by JAX's collectives and lax.ppermute only.
A program may use at most 128 MiB of HBM per device.

v0:
```python
import jax
import jax.numpy as jnp
from jax import lax
from jax.sharding import PartitionSpec as P

HD = 256


softcap = 50.0
epsilon = 1e-06


def capped_weights(scores, alive):
    capped = softcap * jnp.tanh(scores / softcap)
    return jnp.where(alive, jnp.exp(capped), 0.0)


def prompt_part(flat_queries, select, prompt_cache, prompt_length):
    item_count = flat_queries.shape[0]
    kv_local = prompt_cache.shape[3] // HD
    per_kv = flat_queries.shape[1] // (HD * kv_local)
    prompt_size = prompt_cache.shape[2]
    grouped = flat_queries.reshape(item_count, kv_local, per_kv, HD)
    positions = lax.broadcasted_iota(jnp.int32, (1, 1, 1, prompt_size), 3)
    numerator = jnp.zeros((item_count, kv_local, per_kv, HD), jnp.float32)
    denominator = jnp.zeros((item_count, kv_local, per_kv), jnp.float32)
    for member in range(prompt_cache.shape[0]):
        key_rows = prompt_cache[member, 0].reshape(prompt_size, kv_local, HD)
        value_rows = prompt_cache[member, 1].reshape(prompt_size, kv_local, HD)
        scores = jnp.einsum(
            "mkqd,pkd->mkqp", grouped, key_rows, preferred_element_type=jnp.float32
        ) * HD ** (-0.5)
        weights = capped_weights(scores, positions < prompt_length[member])
        portion = jnp.einsum(
            "mkqp,pkd->mkqd",
            weights.astype(jnp.bfloat16),
            value_rows,
            preferred_element_type=jnp.float32,
        )
        chosen = select[:, member].astype(jnp.float32)
        numerator = numerator + chosen[:, None, None, None] * portion
        denominator = denominator + chosen[:, None, None] * jnp.sum(weights, axis=-1)
    return (numerator, denominator)


def suffix_part(flat_queries, cache_rows, alive):
    item_count = flat_queries.shape[0]
    kv_local = cache_rows.shape[3] // HD
    per_kv = flat_queries.shape[1] // (HD * kv_local)
    window = cache_rows.shape[2]
    grouped = flat_queries.reshape(item_count, kv_local, per_kv, HD)
    key_rows = cache_rows[:, 0].reshape(item_count, window, kv_local, HD)
    value_rows = cache_rows[:, 1].reshape(item_count, window, kv_local, HD)
    scores = jnp.einsum(
        "mkqd,mskd->mkqs", grouped, key_rows, preferred_element_type=jnp.float32
    ) * HD ** (-0.5)
    weights = capped_weights(scores, alive[:, None, None, :])
    numerator = jnp.einsum(
        "mkqs,mskd->mkqd",
        weights.astype(jnp.bfloat16),
        value_rows,
        preferred_element_type=jnp.float32,
    )
    return (numerator, jnp.sum(weights, axis=-1))


def finish(numerator, denominator):
    safe_den = jnp.where(denominator > 0.0, denominator, 1.0)
    mixed = numerator / safe_den[..., None]
    return mixed.reshape(mixed.shape[0], -1).astype(jnp.bfloat16)


def shards(
    hidden_input,
    queries,
    prompt_cache,
    suffix_cache,
    owner_replica,
    group_slot,
    prompt_length,
    suffix_length,
    output_weight,
    post_gain,
):
    replicas = lax.axis_size("replica")
    requests = queries.shape[0]
    capacity = max(2, (2 * requests + replicas - 1) // replicas)
    slots = replicas * capacity
    group_count = prompt_cache.shape[0]
    window = suffix_cache.shape[2]
    target = owner_replica[:, 0]
    row_ids = lax.broadcasted_iota(jnp.int32, (requests, requests), 0)
    col_ids = lax.broadcasted_iota(jnp.int32, (requests, requests), 1)
    earlier = (target[:, None] == target[None, :]) & (col_ids < row_ids)
    rank_in = jnp.sum(earlier.astype(jnp.int32), axis=1)
    position = target * capacity + rank_in
    slot_ids = lax.broadcasted_iota(jnp.int32, (slots, requests), 0)
    request_ids = lax.broadcasted_iota(jnp.int32, (slots, requests), 1)
    matches = slot_ids == position[None, :]
    source = jnp.sum(jnp.where(matches, request_ids, 0), axis=1)
    filled = jnp.any(matches, axis=1)
    send_queries = jnp.where(filled[:, None], jnp.take(queries, source, axis=0), 0)
    group_ids = lax.broadcasted_iota(jnp.int32, (slots, group_count), 1)
    send_select = ((group_slot[source][:, None] == group_ids) & filled[:, None]).astype(
        jnp.bfloat16
    )
    query_blocks = send_queries.reshape(replicas, capacity, -1)
    select_blocks = send_select.reshape(replicas, capacity, group_count)
    send_cache = jnp.where(filled[:, None, None, None], jnp.take(suffix_cache, source, axis=0), 0)
    slot_window = lax.broadcasted_iota(jnp.int32, (slots, window), 1)
    send_alive = ((slot_window < suffix_length[source][:, None]) & filled[:, None]).astype(
        jnp.bfloat16
    )
    cache_blocks = send_cache.reshape((replicas, capacity) + suffix_cache.shape[1:])
    alive_blocks = send_alive.reshape(replicas, capacity, window)
    got_queries = lax.all_to_all(query_blocks, "replica", split_axis=0, concat_axis=0, tiled=True)
    got_cache = lax.all_to_all(cache_blocks, "replica", split_axis=0, concat_axis=0, tiled=True)
    got_alive = lax.all_to_all(alive_blocks, "replica", split_axis=0, concat_axis=0, tiled=True)
    got_select = lax.all_to_all(select_blocks, "replica", split_axis=0, concat_axis=0, tiled=True)
    outer = got_queries.shape[0]
    inner = got_queries.shape[1]
    flat_queries = got_queries.reshape(outer * inner, -1)
    prompt_num, prompt_den = prompt_part(
        flat_queries, got_select.reshape(outer * inner, -1), prompt_cache, prompt_length
    )
    own_num, own_den = suffix_part(
        flat_queries,
        got_cache.reshape((outer * inner,) + got_cache.shape[2:]),
        got_alive.reshape(outer * inner, -1) > 0,
    )
    mixed = finish(prompt_num + own_num, prompt_den + own_den)
    answered = mixed.reshape(outer, inner, -1)
    returned = lax.all_to_all(answered, "replica", split_axis=0, concat_axis=0, tiled=True)
    attention = jnp.take(returned.reshape(slots, -1), position, axis=0)
    width = hidden_input.shape[1]
    partial_proj = jnp.dot(attention, output_weight, preferred_element_type=jnp.float32)
    total = lax.psum(partial_proj, "tensor")
    mean_square = jnp.mean(total * total, axis=-1)
    mine = lax.dynamic_slice_in_dim(total, lax.axis_index("tensor") * width, width, 1)
    normed = mine * lax.rsqrt(mean_square + epsilon)[:, None] * post_gain[None, :]
    return (hidden_input.astype(jnp.float32) + normed).astype(jnp.bfloat16)


def solution(mesh):
    in_specs = (
        P("replica", "tensor"),
        P("replica", "tensor"),
        P("replica", None, None, "tensor"),
        P("replica", None, None, "tensor"),
        P("replica", None),
        P("replica"),
        P("replica"),
        P("replica"),
        P("tensor", None),
        P("tensor"),
    )
    out_specs = P("replica", "tensor")
    return jax.shard_map(shards, mesh=mesh, in_specs=in_specs, out_specs=out_specs, check_vma=False)
```

profile of v0, /device:TPU:0, one launch (start us, length us, event | category | flops | bytes accessed | tf_op | source)
XLA Modules:
  0.0 322.2 jit_solution(15772780921316354118)
XLA Ops:
  6.5 0.9 convert_reduce_fusion
  8.4 1.6 gather_fusion
  10.7 7.3 %all-to-all-start = ((bf16[8,16,4]{1,2,0:T(4,128)(2,1)}), bf16[8,16,4]{1,2,0:T(4,128)(2,1)S(1)}, u32[]{:S(2)}, u32[]{:S(2)}) async-start(bf16[8,16,4]{1,2,0:T(4,128)(2,1)} %fusion.80), calls=%async_computation | async-start | bytes 16384 | tf_op jit(solution)/shard_map/all_to_all | solution.py:119
  18.0 1.6 gather_fusion.2
  19.8 0.8 gather_fusion.1
  20.7 0.7 reshape.481
  21.4 3.1 all-to-all-done
  24.5 3.3 %all-to-all-start.2 = ((bf16[8,2,512]{2,1,0:T(2,128)(2,1)}), bf16[8,2,512]{2,1,0:T(2,128)(2,1)S(1)}, u32[]{:S(2)}, u32[]{:S(2)}) async-start(bf16[8,2,512]{2,1,0:T(2,128)(2,1)} %reshape.481), calls=%async_computation.2 | async-start | bytes 32768 | tf_op jit(solution)/shard_map/all_to_all | solution.py:118
  27.8 0.8 select_select_fusion.1
  28.6 8.7 %gather_fusion.3 = bf16[128,2,64,256]{3,2,1,0:T(8,128)(2,1)} fusion(bf16[64,2,64,256]{3,2,1,0:T(8,128)(2,1)} %param.13, s32[1024]{0:T(1024)S(1)} %pad_clamp_fusion.1), kind=kCustom, calls=%fused_computation.3 | custom fusion | bytes 16777728 | tf_op jit(solution)/shard_map/jit(_take)/gather | solution.py:109
  37.2 5.9 %all-to-all-start.1 = ((bf16[8,16,512]{2,1,0:T(8,128)(2,1)}), bf16[8,16,512]{2,1,0:T(8,128)(2,1)S(1)}, u32[]{:S(2)}, u32[]{:S(2)}) async-start(bf16[8,16,512]{2,1,0:T(8,128)(2,1)} %select_select_fusion.1), calls=%async_computation.1 | async-start | bytes 262144 | tf_op jit(solution)/shard_map/all_to_all | solution.py:116
  43.2 7.4 %select_select_fusion = bf16[8,16,2,64,256]{4,3,2,1,0:T(8,128)(2,1)} fusion(bf16[8,16,2,64,256]{4,3,2,1,0:T(8,128)(2,1)} %bitcast.208, pred[8,16]{1,0:T(8,128)(4,1)S(1)} %compare_and_fusion, pred[8,16]{1,0:T(8,128)(4,1)S(1)} %and.42), kind=kLoop, calls=%fused_computation.5 | loop fusion | flops 8388608 | bytes 16777472 | tf_op jit(solution)/shard_map/jit(_where)/select_n | solution.py:109
  50.6 8.3 %copy.54 = bf16[8,16,2,64,256]{4,3,1,2,0:T(8,128)(2,1)} copy(bf16[8,16,2,64,256]{4,3,2,1,0:T(8,128)(2,1)} %select_select_fusion) | data formatting | bytes 16777216 | tf_op jit(solution)/shard_map/jit(_where)/select_n | solution.py:109
  58.8 6.1 %all-to-all-start.3 = ((bf16[8,16,2,64,256]{4,3,1,2,0:T(8,128)(2,1)}), bf16[8,16,2,64,256]{4,3,1,2,0:T(8,128)(2,1)}, u32[]{:S(2)}, u32[]{:S(2)}) async-start(bf16[8,16,2,64,256]{4,3,1,2,0:T(8,128)(2,1)} %copy.54), calls=%async_computation.3 | async-start | bytes 16777216 | tf_op jit(solution)/shard_map/all_to_all | solution.py:117
  66.9 0.7 iota_compare_fusion.6
  68.5 2.3 fusion.85
  70.8 2.3 fusion.86
  73.1 2.1 fusion.87
  75.2 0.9 fusion.88
  77.4 168.6 %all-to-all-done.3 = bf16[8,16,2,64,256]{4,3,1,2,0:T(8,128)(2,1)} async-done(((bf16[8,16,2,64,256]{4,3,1,2,0:T(8,128)(2,1)}), bf16[8,16,2,64,256]{4,3,1,2,0:T(8,128)(2,1)}, u32[]{:S(2)}, u32[]{:S(2)}) %all-to-all-start.3) | async-done | bytes 8388640 | tf_op jit(solution)/shard_map/all_to_all | solution.py:117
  246.1 8.3 %copy.55 = bf16[8,16,2,64,256]{4,3,1,0,2:T(8,128)(2,1)} copy(bf16[8,16,2,64,256]{4,3,1,2,0:T(8,128)(2,1)} %all-to-all-done.3) | data formatting | bytes 16777216 | tf_op jit(solution)/shard_map/all_to_all | solution.py:117
  254.4 3.5 %fusion.84 = (f32[128,2]{1,0:T(8,128)S(1)}, bf16[128,2,64]{2,1,0:T(2,128)(2,1)S(1)}) fusion(bf16[128,2,256]{2,1,0:T(2,128)(2,1)S(1)} %reshape.408, bf16[128,2,64,256]{3,2,0,1:T(8,128)(2,1)} %bitcast.209, pred[128,64]{1,0:T(8,128)(4,1)S(1)} %bitcast.213), kind=kOutput, calls=%fused_computation.129 | convolution fusion | flops 8470272 | bytes 4367360 | tf_op jit(solution)/shard_map/mkqd,mskd->mkqs/dot_general | solution.py:54
  257.9 2.9 fusion
  260.8 1.7 fusion.36
  262.6 0.7 convert_element_type.118
  263.4 3.6 %all-to-all-start.4 = ((bf16[8,16,512]{2,1,0:T(8,128)(2,1)}), bf16[8,16,512]{2,1,0:T(8,128)(2,1)S(1)}, u32[]{:S(2)}, u32[]{:S(2)}) async-start(bf16[8,16,512]{2,1,0:T(8,128)(2,1)} %convert_element_type.118), calls=%async_computation.4 | async-start | bytes 262144 | tf_op jit(solution)/shard_map/all_to_all | solution.py:133
  267.1 7.3 %all-to-all-done.4 = bf16[8,16,512]{2,1,0:T(8,128)(2,1)S(1)} async-done(((bf16[8,16,512]{2,1,0:T(8,128)(2,1)}), bf16[8,16,512]{2,1,0:T(8,128)(2,1)S(1)}, u32[]{:S(2)}, u32[]{:S(2)}) %all-to-all-start.4) | async-done | bytes 131104 | tf_op jit(solution)/shard_map/all_to_all | solution.py:133
  274.4 0.7 gather_fusion.4
  275.1 3.8 %fusion.70 = f32[64,3584]{1,0:T(8,128)} fusion(bf16[512,3584]{1,0:T(8,128)(2,1)} %param.18, bf16[64,512]{1,0:T(8,128)(2,1)S(1)} %gather_fusion.4, pred[64]{0:T(512)(128)(4,1)S(1)} %get-tuple-element.5), kind=kOutput, calls=%fused_computation.89 | convolution fusion | flops 234913792 | bytes 4653120 | tf_op jit(solution)/shard_map/dot_general | solution.py:136
  278.9 33.4 %all-reduce.2.cloned.1.call-done = f32[64,3584]{1,0:T(8,128)} async-done(((f32[64,3584]{1,0:T(8,128)}), f32[64,3584]{1,0:T(8,128)}) %all-reduce.2.cloned.1.call-update) | async-done | bytes 917520 | tf_op jit(solution)/shard_map/psum | solution.py:137
  312.3 1.3 multiply_reduce_fusion
  313.6 1.7 add_convert_fusion
  (50 shorter events, 6.4 us)
Async XLA Ops:
  6.5 13.3 %copy-start = (bf16[64,512]{1,0:T(8,128)(2,1)S(1)}, bf16[64,512]{1,0:T(8,128)(2,1)}, u32[]{:S(2)}) copy-start(bf16[64,512]{1,0:T(8,128)(2,1)} %param.11) | copy-start | bytes 196612
  10.7 13.8 %all-to-all-start = ((bf16[8,16,4]{1,2,0:T(4,128)(2,1)}), bf16[8,16,4]{1,2,0:T(4,128)(2,1)S(1)}, u32[]{:S(2)}, u32[]{:S(2)}) async-start(bf16[8,16,4]{1,2,0:T(4,128)(2,1)} %fusion.80), calls=%async_computation | async-start | bytes 16384 | tf_op jit(solution)/shard_map/all_to_all | solution.py:119
  24.5 12.8 %all-to-all-start.2 = ((bf16[8,2,512]{2,1,0:T(2,128)(2,1)}), bf16[8,2,512]{2,1,0:T(2,128)(2,1)S(1)}, u32[]{:S(2)}, u32[]{:S(2)}) async-start(bf16[8,2,512]{2,1,0:T(2,128)(2,1)} %reshape.481), calls=%async_computation.2 | async-start | bytes 32768 | tf_op jit(solution)/shard_map/all_to_all | solution.py:118
  37.2 21.6 %all-to-all-start.1 = ((bf16[8,16,512]{2,1,0:T(8,128)(2,1)}), bf16[8,16,512]{2,1,0:T(8,128)(2,1)S(1)}, u32[]{:S(2)}, u32[]{:S(2)}) async-start(bf16[8,16,512]{2,1,0:T(8,128)(2,1)} %select_select_fusion.1), calls=%async_computation.1 | async-start | bytes 262144 | tf_op jit(solution)/shard_map/all_to_all | solution.py:116
  58.8 6.1 %copy-start.2 = (s32[4]{0:T(128)S(1)}, s32[4]{0:T(128)}, u32[]{:S(2)}) copy-start(s32[4]{0:T(128)} %param.16) | copy-start | bytes 52
  58.8 187.3 %all-to-all-start.3 = ((bf16[8,16,2,64,256]{4,3,1,2,0:T(8,128)(2,1)}), bf16[8,16,2,64,256]{4,3,1,2,0:T(8,128)(2,1)}, u32[]{:S(2)}, u32[]{:S(2)}) async-start(bf16[8,16,2,64,256]{4,3,1,2,0:T(8,128)(2,1)} %copy.54), calls=%async_computation.3 | async-start | bytes 16777216 | tf_op jit(solution)/shard_map/all_to_all | solution.py:117
  68.5 6.7 %slice-start = ((s8[8388608]{0:T(1024)(128)(4,1)}), s8[4194304]{0:T(1024)(128)(4,1)S(1)}, s32[]{:S(2)}) async-start(s8[8388608]{0:T(1024)(128)(4,1)} %bitcast.216), calls=%async_computation.6 | async-start | bytes 8388608
  70.8 4.4 %slice-start.1 = ((s8[8388608]{0:T(1024)(128)(4,1)}), s8[4194304]{0:T(1024)(128)(4,1)S(1)}, s32[]{:S(2)}) async-start(s8[8388608]{0:T(1024)(128)(4,1)} %bitcast.216), calls=%async_computation.7 | async-start | bytes 8388608
  257.9 9.2 %copy-start.4 = (s32[64,1]{0,1:T(1,128)S(1)}, s32[64,1]{0,1:T(1,128)}, u32[]{:S(2)}) copy-start(s32[64,1]{0,1:T(1,128)} %param.14) | copy-start | bytes 772
  262.5 51.2 %copy-start.1 = (bf16[64,896]{1,0:T(8,128)(2,1)S(1)}, bf16[64,896]{1,0:T(8,128)(2,1)}, u32[]{:S(2)}) copy-start(bf16[64,896]{1,0:T(8,128)(2,1)} %param.10) | copy-start | bytes 344068
  262.5 51.2 %copy-start.3 = (f32[896]{0:T(1024)S(1)}, f32[896]{0:T(1024)}, u32[]{:S(2)}) copy-start(f32[896]{0:T(1024)} %param.19) | copy-start | bytes 10756
  263.4 11.0 %all-to-all-start.4 = ((bf16[8,16,512]{2,1,0:T(8,128)(2,1)}), bf16[8,16,512]{2,1,0:T(8,128)(2,1)S(1)}, u32[]{:S(2)}, u32[]{:S(2)}) async-start(bf16[8,16,512]{2,1,0:T(8,128)(2,1)} %convert_element_type.118), calls=%async_computation.4 | async-start | bytes 262144 | tf_op jit(solution)/shard_map/all_to_all | solution.py:133
  267.0 45.3 %all-reduce.2.cloned.1.call-start = ((), (), s32[]{:S(2)}) async-start(), calls=%async_computation.5 | async-start | bytes 1835008 | tf_op jit(solution)/shard_map/psum | solution.py:137
Sparse Core Ops, SparseCore 0:
  279.0 33.2 all-reduce.1
where the time goes:
time: 323 us; the launch traced here: 322 us
  waiting for transfers between devices  212 us (66%)
  local copies, waits for them, and re-layouts  32.8 us (10%)
  starting transfers between devices  26.3 us (8%)
  matrix products  20.7 us (6%)
  other arithmetic  16.4 us (5%)
  between operations  13.7 us (4%)
    all_to_all x1, waiting for transfers between devices, shards(): lax.all_to_all(cache_blocks, 'replica', split_axis=0, concat_axis=0, tile...  169 us
    psum x1, waiting for transfers between devices, shards(): total = lax.psum(partial_proj, 'tensor')  33.4 us
    gather x1, local copies, waits for them, and re-layouts, shards(): jnp.take(suffix_cache, source, axis=0)  8.65 us
    all_to_all x1, local copies, waits for them, and re-layouts, shards(): lax.all_to_all(cache_blocks, 'replica', split_axis=0, concat_axis=0, tile...  8.26 us
    select_n x1, local copies, waits for them, and re-layouts, shards(): jnp.where(filled[:, None, None, None], jnp.take(suffix_cache, source, axi...  8.26 us
    dot_general x4, matrix products, prompt_part(): jnp.einsum('mkqd,pkd->mkqp', grouped, key_rows, preferred_element_type=jn...  7.52 us
    select_n x1, other arithmetic, shards(): jnp.where(filled[:, None, None, None], jnp.take(suffix_cache, source, axi...  7.41 us
    all_to_all x1, waiting for transfers between devices, shards(): lax.all_to_all(answered, 'replica', split_axis=0, concat_axis=0, tiled=True)  7.26 us
  transfers between devices with their start and end apart: 6, of which 4 were waited for; matrix products, arithmetic and copies ran while one was open for 13% of the time, Pallas kernels for 0%

commit v1 on v0

v1 whole, which is shorter than its diff:
```python
import functools
import math

import jax
import jax.numpy as jnp
from jax import lax
from jax.experimental import pallas as pl
from jax.experimental.pallas import tpu as pltpu
from jax.sharding import PartitionSpec as P

HD = 256
softcap = 50.0
epsilon = 1e-06
score_scale = 1.0 / (softcap * math.sqrt(HD))
weight_scale = softcap * math.log2(math.e)
EXTRA = 128
f32 = jnp.float32
bf16 = jnp.bfloat16
VMEM = pltpu.MemorySpace.VMEM
SMEM = pltpu.MemorySpace.SMEM


def iota(shape, axis):
    return lax.broadcasted_iota(jnp.int32, shape, axis)


def heads_below(block, heads):
    return jnp.concatenate([block[:, h * HD : (h + 1) * HD] for h in range(heads)], axis=0)


def weights_of(scores, alive):
    return jnp.where(alive, jnp.exp2(weight_scale * jnp.tanh(scores * score_scale)), 0.0)


def owners(owner_ref):
    requests = owner_ref.shape[0]
    rows, cols = iota((requests, requests), 0), iota((requests, requests), 1)
    by_row = jnp.broadcast_to(owner_ref[...], (requests, requests)).astype(f32)
    by_col = jnp.sum(jnp.where(rows == cols, by_row, 0.0), axis=0, keepdims=True)
    return by_row, by_col, rows, cols


def route_kernel(capacity, owner_ref, group_ref, queries_ref, out_ref):
    requests, width = queries_ref.shape
    slots = out_ref.shape[0]
    by_row, by_col, rows, cols = owners(owner_ref)
    earlier = jnp.where((by_row == by_col) & (rows < cols), 1.0, 0.0)
    position = (by_col * capacity + jnp.sum(earlier, axis=0, keepdims=True)).astype(jnp.int32)
    matches = iota((slots, requests), 0) == position
    out_ref[:, :width] = jnp.dot(
        jnp.where(matches, 1.0, 0.0).astype(bf16), queries_ref[...], preferred_element_type=f32
    ).astype(bf16)
    numbered = (group_ref[...] + 1).astype(f32)
    mark = jnp.sum(jnp.where(matches, numbered, 0.0), axis=1, keepdims=True)
    out_ref[:, width:] = jnp.broadcast_to(mark, (slots, EXTRA)).astype(bf16)


def suffix_kernel(
    capacity, owner_ref, length_ref, queries_ref, cache_ref, back_ref, num_ref, den_ref
):
    requests, slots = back_ref.shape
    block, _, window, _ = cache_ref.shape
    heads = queries_ref.shape[1] // HD

    @pl.when(pl.program_id(0) == 0)
    def _():
        by_row, by_col, rows, cols = owners(owner_ref)
        earlier = jnp.where((by_row == by_col) & (cols < rows), 1.0, 0.0)
        rank = jnp.sum(earlier, axis=1, keepdims=True).astype(jnp.int32)
        position = owner_ref[...] * capacity + rank
        back_ref[...] = jnp.where(iota((requests, slots), 1) == position, 1.0, 0.0).astype(bf16)

    stacked = heads_below(queries_ref[...], heads)
    keys = cache_ref[:, 0].reshape(block * window, HD)
    values = cache_ref[:, 1].reshape(block * window, HD)
    scores = lax.dot_general(
        stacked, keys, (((1,), (1,)), ((), ())), preferred_element_type=f32
    )
    cols = iota((block, block * window), 1)
    first = iota((block, block * window), 0) * window
    alive = (cols >= first) & (cols < first + length_ref[...])
    weights = weights_of(scores, jnp.concatenate([alive] * heads, axis=0))
    numerator = jnp.dot(weights.astype(bf16), values, preferred_element_type=f32)
    denominator = jnp.sum(weights, axis=1, keepdims=True)
    for h in range(heads):
        mine = slice(h * block, (h + 1) * block)
        num_ref[:, h * HD : (h + 1) * HD] = numerator[mine]
        den_ref[:, h * 128 : (h + 1) * 128] = jnp.broadcast_to(denominator[mine], (block, 128))


def prompt_kernel(chunk, length_ref, slots_ref, cache_ref, out_ref, held, num, den, sems):
    groups, _, size, _ = cache_ref.shape
    slots = slots_ref.shape[0]
    width = slots_ref.shape[1] - EXTRA
    heads = width // HD
    rows = heads * slots
    chunks = size // chunk

    def copy(g, c, part):
        span = pl.ds(c * chunk, chunk)
        return pltpu.make_async_copy(
            cache_ref.at[g, part, span, :], held.at[g, part, span, :], sems.at[g, c, part]
        )

    for g in range(groups):
        for c in range(chunks):

            @pl.when(c * chunk < length_ref[g])
            def _():
                copy(g, c, 0).start()
                copy(g, c, 1).start()

    stacked = heads_below(slots_ref[:, :width], heads)
    mark = slots_ref[:, width : width + 1].astype(f32)
    mark = jnp.concatenate([mark] * heads, axis=0)
    num[...] = jnp.zeros_like(num)
    den[...] = jnp.zeros_like(den)
    for g in range(groups):
        limit = jnp.where(mark == g + 1.0, length_ref[g], 0)

        def step(c, carry):
            copy(g, c, 0).wait()
            span = pl.ds(pl.multiple_of(c * chunk, chunk), chunk)
            scores = lax.dot_general(
                stacked, held[g, 0, span, :], (((1,), (1,)), ((), ())), preferred_element_type=f32
            )
            alive = iota((rows, chunk), 1) < limit - c * chunk
            weights = weights_of(scores, alive)
            copy(g, c, 1).wait()
            num[...] += jnp.dot(
                weights.astype(bf16), held[g, 1, span, :], preferred_element_type=f32
            )
            part = weights[:, :128]
            for k in range(1, chunk // 128):
                part = part + weights[:, k * 128 : (k + 1) * 128]
            den[...] += part
            return carry

        lax.fori_loop(0, (length_ref[g] + chunk - 1) // chunk, step, 0)

    total = jnp.sum(den[...], axis=1, keepdims=True)
    lanes = iota((slots, EXTRA), 1)
    extra = jnp.zeros((slots, EXTRA), f32)
    for h in range(heads):
        out_ref[:, h * HD : (h + 1) * HD] = num[h * slots : (h + 1) * slots].astype(bf16)
        rest = total[h * slots : (h + 1) * slots]
        for k in range(3):
            piece = rest.astype(bf16).astype(f32)
            rest = rest - piece
            extra = jnp.where(lanes == 3 * h + k, piece, extra)
    out_ref[:, width:] = extra.astype(bf16)


def quarters(weight_ref, attention, first, second):
    width = weight_ref.shape[1] // 4
    out = []
    for q in (first, second):
        cols = pl.ds(pl.multiple_of(q * width, 128), width)
        out.append(jnp.dot(attention, weight_ref[:, cols], preferred_element_type=f32))
    return out


def combine_kernel(core_ref, returned_ref, back_ref, num_ref, den_ref, weight_ref, att_ref, give_ref):
    width = num_ref.shape[1]
    heads = width // HD
    other = 1 - core_ref[0]
    mine = jnp.dot(back_ref[...], returned_ref[...], preferred_element_type=f32)
    for h in range(heads):
        cols = slice(h * HD, (h + 1) * HD)
        numerator = mine[:, cols] + num_ref[:, cols]
        at = width + 3 * h
        denominator = den_ref[:, h * 128 : h * 128 + 1] + (
            mine[:, at : at + 1] + mine[:, at + 1 : at + 2] + mine[:, at + 2 : at + 3]
        )
        att_ref[:, cols] = (numerator / denominator).astype(bf16)
    a, b = quarters(weight_ref, att_ref[...], other, other + 2)
    half = a.shape[1]
    give_ref[:, :half] = a.astype(bf16)
    give_ref[:, half:] = b.astype(bf16)


def own_kernel(core_ref, att_ref, weight_ref, own_ref):
    a, b = quarters(weight_ref, att_ref[...], core_ref[0], core_ref[0] + 2)
    half = a.shape[1]
    own_ref[:, :half] = a
    own_ref[:, half:] = b


def chip_kernel(own_ref, got_ref, sum_ref, send_ref):
    total = own_ref[...] + got_ref[...].astype(f32)
    sum_ref[...] = total
    send_ref[...] = total.astype(bf16)


def square_kernel(row_ref, sum_ref, got_ref, mine_ref, square_ref):
    width = mine_ref.shape[1]
    total = sum_ref[...] + got_ref[...].astype(f32)
    part = jnp.zeros(square_ref.shape, f32)
    for k in range(total.shape[1] // 128):
        piece = total[:, k * 128 : (k + 1) * 128]
        part = part + piece * piece
    square_ref[...] = part
    mine_ref[...] = jnp.where(row_ref[0] == 0, total[:, :width], total[:, width:])


def final_kernel(features, mine_ref, square_ref, got_ref, gain_ref, hidden_ref, out_ref):
    square = jnp.sum(square_ref[...] + got_ref[...], axis=1, keepdims=True)
    scale = lax.rsqrt(square * (1.0 / features) + epsilon)
    normed = mine_ref[...] * scale * gain_ref[...]
    out_ref[...] = (hidden_ref[...].astype(f32) + normed).astype(bf16)


def call(kernel, outs, ins, **kw):
    specs = [
        pl.BlockSpec(memory_space=SMEM if a.ndim == 1 else VMEM) for a in ins
    ]
    return pl.pallas_call(
        kernel,
        out_shape=outs,
        in_specs=specs,
        out_specs=jax.tree.map(lambda _: pl.BlockSpec(memory_space=VMEM), outs),
        compiler_params=pltpu.CompilerParams(vmem_limit_bytes=40 * 2**20),
        **kw,
    )(*ins)


def shape(dims, dtype):
    return jax.ShapeDtypeStruct(dims, dtype)


def shards(
    hidden_input,
    queries,
    prompt_cache,
    suffix_cache,
    owner_replica,
    group_slot,
    prompt_length,
    suffix_length,
    output_weight,
    post_gain,
):
    replicas = lax.axis_size("replica")
    ranks = lax.axis_size("tensor")
    requests, width = queries.shape
    capacity = max(2, (2 * requests + replicas - 1) // replicas)
    slots = replicas * capacity
    groups, _, size, _ = prompt_cache.shape
    window = suffix_cache.shape[2]
    features = output_weight.shape[1]
    quarter = features // ranks
    heads = width // HD
    index = lax.axis_index("tensor")
    core = (index % 2).reshape(1)
    row = (index // 2).reshape(1)

    def exchange(x):
        blocks = x.reshape(replicas, capacity, width + EXTRA)
        blocks = lax.all_to_all(blocks, "replica", split_axis=0, concat_axis=0, tiled=True)
        return blocks.reshape(slots, width + EXTRA)

    def permute(x, bit):
        return lax.ppermute(x, "tensor", [(i, i ^ bit) for i in range(ranks)])

    sent = call(
        functools.partial(route_kernel, capacity),
        shape((slots, width + EXTRA), bf16),
        [owner_replica, group_slot.reshape(1, requests), queries],
    )
    got = exchange(sent)

    block = 16
    back, own_num, own_den = pl.pallas_call(
        functools.partial(suffix_kernel, capacity),
        out_shape=[
            shape((requests, slots), bf16),
            shape((requests, width), f32),
            shape((requests, heads * 128), f32),
        ],
        grid=(requests // block,),
        in_specs=[
            pl.BlockSpec((requests, 1), lambda i: (0, 0)),
            pl.BlockSpec((block, 1), lambda i: (i, 0)),
            pl.BlockSpec((block, width), lambda i: (i, 0)),
            pl.BlockSpec((block, 2, window, HD), lambda i: (i, 0, 0, 0)),
        ],
        out_specs=[
            pl.BlockSpec((requests, slots), lambda i: (0, 0)),
            pl.BlockSpec((block, width), lambda i: (i, 0)),
            pl.BlockSpec((block, heads * 128), lambda i: (i, 0)),
        ],
        compiler_params=pltpu.CompilerParams(vmem_limit_bytes=40 * 2**20),
        cost_estimate=pl.CostEstimate(
            flops=8 * requests * window * HD * block,
            bytes_accessed=suffix_cache.size * 2,
            transcendentals=0,
        ),
    )(owner_replica, suffix_length.reshape(requests, 1), queries, suffix_cache)

    chunk = math.gcd(512, size)
    answered = pl.pallas_call(
        functools.partial(prompt_kernel, chunk),
        out_shape=shape((slots, width + EXTRA), bf16),
        in_specs=[
            pl.BlockSpec(memory_space=SMEM),
            pl.BlockSpec(memory_space=VMEM),
            pl.BlockSpec(memory_space=pl.ANY),
        ],
        out_specs=pl.BlockSpec(memory_space=VMEM),
        scratch_shapes=[
            pltpu.VMEM(prompt_cache.shape, bf16),
            pltpu.VMEM((heads * slots, HD), f32),
            pltpu.VMEM((heads * slots, 128), f32),
            pltpu.SemaphoreType.DMA((groups, size // chunk, 2)),
        ],
        compiler_params=pltpu.CompilerParams(vmem_limit_bytes=40 * 2**20),
    )(prompt_length, got, prompt_cache)
    returned = exchange(answered)

    attention, give = call(
        combine_kernel,
        [shape((requests, width), bf16), shape((requests, 2 * quarter), bf16)],
        [core, returned, back, own_num, own_den, output_weight],
    )
    received = permute(give, 1)
    own = call(own_kernel, shape((requests, 2 * quarter), f32), [core, attention, output_weight])
    chip, send = call(
        chip_kernel,
        [shape((requests, 2 * quarter), f32), shape((requests, 2 * quarter), bf16)],
        [own, received],
    )
    far = permute(send, 2)
    mine, square = call(
        square_kernel,
        [shape((requests, quarter), f32), shape((requests, 128), f32)],
        [row, chip, far],
    )
    beside = permute(square, 1)
    return call(
        functools.partial(final_kernel, features),
        shape((requests, quarter), bf16),
        [mine, square, beside, post_gain.reshape(1, quarter), hidden_input],
    )


def solution(mesh):
    in_specs = (
        P("replica", "tensor"),
        P("replica", "tensor"),
        P("replica", None, None, "tensor"),
        P("replica", None, None, "tensor"),
        P("replica", None),
        P("replica"),
        P("replica"),
        P("replica"),
        P("tensor", None),
        P("tensor"),
    )
    out_specs = P("replica", "tensor")
    return jax.shard_map(shards, mesh=mesh, in_specs=in_specs, out_specs=out_specs, check_vma=False)
```

time: 323 us -> 56.2 us (0.17)
  waiting for transfers between devices: 212 us -> 10.3 us
  local copies, waits for them, and re-layouts: 32.8 us -> 11.8 us
  matrix products: 20.7 us -> 0 us
  starting transfers between devices: 26.3 us -> 5.92 us
  other arithmetic: 16.4 us -> 0 us
  blocking collectives: 0 us -> 14.6 us
  Pallas kernels: 0 us -> 13.8 us
  between operations: 13.7 us -> 0.1 us
    all_to_all x5 -> x1, waiting for transfers between devices: 179 us -> 3.18 us  [exchange(): lax.all_to_all(blocks, 'replica', split_axis=0, concat_axis=0, tiled=True)]
    psum x1 -> x0, waiting for transfers between devices: 33.4 us -> none  [shards(): total = lax.psum(partial_proj, 'tensor')]
    all_to_all x5 -> x1, starting transfers between devices: 26.3 us -> 4.19 us  [exchange(): lax.all_to_all(blocks, 'replica', split_axis=0, concat_axis=0, tiled=True)]
    dot_general x11 -> x0, matrix products: 20.7 us -> none  [the longest x4 7.52 us: prompt_part(): jnp.einsum('mkqd,pkd->mkqp', grouped, key_rows, preferred_element_type=jn...]
    all_to_all x0 -> x1, blocking collectives: none -> 14.6 us  [exchange(): lax.all_to_all(blocks, 'replica', split_axis=0, concat_axis=0, tiled=True)]
    pallas_call x0 -> x8, Pallas kernels: none -> 13.8 us  [the longest x1 9.43 us: shards(): pl.pallas_call(functools.partial(prompt_kernel, chunk), out_shape=shape((...]
    gather x5 -> x0, local copies, waits for them, and re-layouts: 13.4 us -> none  [the longest x1 8.65 us: shards(): jnp.take(suffix_cache, source, axis=0)]
    unnamed x16 -> x23, local copies, waits for them, and re-layouts: 0.83 us -> 11.7 us
  transfers between devices with their start and end apart: 6 -> 4, of which waited for: 4 -> 3; matrix products, arithmetic and copies ran while one was open for 13% -> 0% of each run, Pallas kernels for 0% -> 4%
where the time goes in v1:
time: 56.2 us; the launch traced here: 56.6 us
  blocking collectives  14.6 us (26%)
  Pallas kernels  13.8 us (25%)
  local copies, waits for them, and re-layouts  11.8 us (21%)
  waiting for transfers between devices  10.3 us (18%)
  starting transfers between devices  5.92 us (11%)
    all_to_all x1, blocking collectives, exchange(): lax.all_to_all(blocks, 'replica', split_axis=0, concat_axis=0, tiled=True)  14.6 us
    unnamed x23, local copies, waits for them, and re-layouts  11.7 us
    pallas_call x1, Pallas kernels, shards(): pl.pallas_call(functools.partial(prompt_kernel, chunk), out_shape=shape((...  9.43 us
    ppermute x3, waiting for transfers between devices, permute(): return lax.ppermute(x, 'tensor', [(i, i ^ bit) for i in range(ranks)])  7.1 us
    all_to_all x1, starting transfers between devices, exchange(): lax.all_to_all(blocks, 'replica', split_axis=0, concat_axis=0, tiled=True)  4.19 us
    all_to_all x1, waiting for transfers between devices, exchange(): lax.all_to_all(blocks, 'replica', split_axis=0, concat_axis=0, tiled=True)  3.18 us
    pallas_call x6, Pallas kernels, call(): pl.pallas_call(kernel, out_shape=outs, in_specs=specs, out_specs=jax.tree...  2.33 us
    pallas_call x1, Pallas kernels, shards(): pl.pallas_call(functools.partial(suffix_kernel, capacity), out_shape=[sha...  2.09 us
  transfers between devices with their start and end apart: 4, of which 3 were waited for; matrix products, arithmetic and copies ran while one was open for 0% of the time, Pallas kernels for 4%

profile of v1, /device:TPU:0, one launch (start us, length us, event | category | flops | bytes accessed | tf_op | source)
XLA Modules:
  0.0 56.6 jit_solution(10975110445649556265)
XLA Ops:
  0.0 0.7 %copy.11.owner_ref = s32[64,1]{1,0:T(8,128)S(1)} copy(s32[64,1]{0,1:T(1,128)} %param.14) | data formatting | bytes 512 | tf_op args[4]
  0.7 0.0 copy-start.4
  0.7 0.8 %copy-done.4 = bf16[64,512]{1,0:T(8,128)(2,1)S(1)} copy-done((bf16[64,512]{1,0:T(8,128)(2,1)S(1)}, bf16[64,512]{1,0:T(8,128)(2,1)}, u32[]{:S(2)}) %copy-start.4) | copy-done | bytes 65560
  1.6 0.0 copy-start.7
  1.6 0.7 %copy-done.7 = s32[64]{0:T(128)S(1)} copy-done((s32[64]{0:T(128)S(1)}, s32[64]{0:T(128)}, u32[]{:S(2)}) %copy-start.7) | copy-done | bytes 280
  2.2 0.3 shard_map.100
  2.5 14.6 %all_to_all.10 = bf16[8,16,640]{2,1,0:T(8,128)(2,1)S(1)} all-to-all(bf16[8,16,640]{2,1,0:T(8,128)(2,1)S(1)} %bitcast.9), channel_id=1, replica_groups=mesh['replica'=8,'tensor'=4] {'replica'}, dimensions={0} | all-to-all | bytes 327680 | tf_op jit(solution)/shard_map/all_to_all | solution.py:259
  17.1 3.4 %copy-done.2 = bf16[4,2,2048,256]{3,2,1,0:T(8,128)(2,1)S(1)} copy-done((bf16[4,2,2048,256]{3,2,1,0:T(8,128)(2,1)S(1)}, bf16[4,2,2048,256]{3,2,1,0:T(8,128)(2,1)}, u32[]{:S(2)}) %copy-start.2) | copy-done | bytes 8388632
  20.5 0.7 %copy-done.8 = s32[4]{0:T(128)S(1)} copy-done((s32[4]{0:T(128)S(1)}, s32[4]{0:T(128)}, u32[]{:S(2)}) %copy-start.8) | copy-done | bytes 40
  21.2 9.4 %shard_map.101 = bf16[128,640]{1,0:T(8,128)(2,1)} custom-call(s32[4]{0:T(128)S(1)} %copy-done.8, bf16[128,640]{1,0:T(8,128)(2,1)S(1)} %bitcast.10, bf16[4,2,2048,256]{3,2,1,0:T(8,128)(2,1)S(1)} %copy-done.2), custom_call_target="tpu_custom_call" | custom-call | tf_op jit(solution)/shard_map/pallas_call | solution.py:301
  30.6 4.2 %all-to-all-start.1 = ((bf16[8,16,640]{2,1,0:T(8,128)(2,1)}), bf16[8,16,640]{2,1,0:T(8,128)(2,1)S(1)}, u32[]{:S(2)}, u32[]{:S(2)}) async-start(bf16[8,16,640]{2,1,0:T(8,128)(2,1)} %bitcast.5), calls=%async_computation.1 | async-start | bytes 327680 | tf_op jit(solution)/shard_map/all_to_all | solution.py:259
  34.8 0.0 copy-done.10
  34.8 0.1 copy.13.length_ref
  34.9 0.0 copy-done.5
  34.9 2.2 %copy-done.3 = bf16[64,2,64,256]{3,2,1,0:T(8,128)(2,1)S(1)} copy-done((bf16[64,2,64,256]{3,2,1,0:T(8,128)(2,1)S(1)}, bf16[64,2,64,256]{3,2,1,0:T(8,128)(2,1)}, u32[]{:S(2)}) %copy-start.3) | copy-done | bytes 4194328
  37.1 2.1 %shard_map.102 = (bf16[64,128]{1,0:T(8,128)(2,1)S(1)}, f32[64,512]{1,0:T(8,128)S(1)}, f32[64,256]{1,0:T(8,128)S(1)}) custom-call(s32[64,1]{1,0:T(8,128)S(1)} %copy.11.owner_ref, s32[64,1]{1,0:T(8,128)S(1)} %copy.13.length_ref, bf16[64,512]{1,0:T(8,128)(2,1)S(1)} %copy-done.5, bf16[64,2,64,256]{3,2,1,0:T(8,128)(2,1)S(1)} %copy-done.3), custom_call_target="tpu_custom_call" | custom-call | flops 134217728 | bytes 4194304 | tf_op jit(solution)/shard_map/pallas_call | solution.py:273
  39.2 3.2 %all-to-all-done.1 = bf16[8,16,640]{2,1,0:T(8,128)(2,1)S(1)} async-done(((bf16[8,16,640]{2,1,0:T(8,128)(2,1)}), bf16[8,16,640]{2,1,0:T(8,128)(2,1)S(1)}, u32[]{:S(2)}, u32[]{:S(2)}) %all-to-all-start.1) | async-done | bytes 163872 | tf_op jit(solution)/shard_map/all_to_all | solution.py:259
  42.4 2.0 %copy-done = bf16[512,3584]{1,0:T(8,128)(2,1)S(1)} copy-done((bf16[512,3584]{1,0:T(8,128)(2,1)S(1)}, bf16[512,3584]{1,0:T(8,128)(2,1)}, u32[]{:S(2)}) %copy-start) | copy-done | bytes 3670040
  44.4 0.7 %shard_map.103 = (bf16[64,512]{1,0:T(8,128)(2,1)S(1)}, bf16[64,1792]{1,0:T(8,128)(2,1)S(1)}) custom-call(s32[1]{0:T(128)} %bitcast.1.core_ref, bf16[128,640]{1,0:T(8,128)(2,1)S(1)} %bitcast.8, bf16[64,128]{1,0:T(8,128)(2,1)S(1)} %get-tuple-element.14.back_ref, f32[64,512]{1,0:T(8,128)S(1)} %get-tuple-element.15.num_ref, ...), custom_call_target="tpu_custom_call" | custom-call | tf_op jit(solution)/shard_map/pallas_call | solution.py:217
  45.1 0.1 collective-permute-start
  45.2 1.2 %copy-done.1 = bf16[512,3584]{1,0:T(8,128)(2,1)S(1)} copy-done((bf16[512,3584]{1,0:T(8,128)(2,1)S(1)}, bf16[512,3584]{1,0:T(8,128)(2,1)}, u32[]{:S(2)}) %copy-start.1) | copy-done | bytes 3670040
  46.4 0.4 shard_map.104.own_ref
  46.9 0.0 collective-permute-done.got_ref
  46.9 0.1 shard_map.105
  47.0 1.6 %collective-permute-start.1 = (bf16[64,1792]{1,0:T(8,128)(2,1)S(1)}, bf16[64,1792]{1,0:T(8,128)(2,1)S(1)}, u32[]{:S(2)}, u32[]{:S(2)}) collective-permute-start(bf16[64,1792]{1,0:T(8,128)(2,1)S(1)} %get-tuple-element.20), channel_id=1, source_target_pairs={{0,2},{1,3},{2,0},{3,1},{4,6},{5,7},{6,4},{7,5},{8,10},{9,11},{10,... | collective-permute-start | bytes 688136 | tf_op jit(solution)/shard_map/ppermute | solution.py:263
  48.5 5.9 %collective-permute-done.1.got_ref = bf16[64,1792]{1,0:T(8,128)(2,1)S(1)} collective-permute-done((bf16[64,1792]{1,0:T(8,128)(2,1)S(1)}, bf16[64,1792]{1,0:T(8,128)(2,1)S(1)}, u32[]{:S(2)}, u32[]{:S(2)}) %collective-permute-start.1) | collective-permute-done | bytes 229408 | tf_op jit(solution)/shard_map/ppermute | solution.py:263
  54.5 0.1 shard_map.106
  54.6 0.1 collective-permute-start.2
  54.6 0.0 copy-done.9
  54.7 1.2 %collective-permute-done.2.got_ref = f32[64,128]{1,0:T(8,128)S(1)} collective-permute-done((f32[64,128]{1,0:T(8,128)S(1)}, f32[64,128]{1,0:T(8,128)S(1)}, u32[]{:S(2)}, u32[]{:S(2)}) %collective-permute-start.2) | collective-permute-done | bytes 32800 | tf_op jit(solution)/shard_map/ppermute | solution.py:263
  55.8 0.0 copy-done.6
  55.8 0.8 %shard_map.107 = bf16[64,896]{1,0:T(8,128)(2,1)} custom-call(f32[64,896]{1,0:T(8,128)S(1)} %get-tuple-element.21.mine_ref, f32[64,128]{1,0:T(8,128)S(1)} %get-tuple-element.22.square_ref, f32[64,128]{1,0:T(8,128)S(1)} %collective-permute-done.2.got_ref, f32[1,896]{1,0:T(1,128)S(1)} %reshape.35.gain_ref, bf16[64,896]{1,0:T(8,128)(2,1)S(1)} %copy-done.6), custom_call_target="tpu_custom_call" | custom-call | tf_op jit(solution)/shard_map/pallas_call | solution.py:217
  (10 shorter events, 0.0 us)
Async XLA Ops:
  0.7 0.8 %copy-start.4 = (bf16[64,512]{1,0:T(8,128)(2,1)S(1)}, bf16[64,512]{1,0:T(8,128)(2,1)}, u32[]{:S(2)}) copy-start(bf16[64,512]{1,0:T(8,128)(2,1)} %queries_ref.3) | copy-start | bytes 196612
  1.6 0.7 %copy-start.7 = (s32[64]{0:T(128)S(1)}, s32[64]{0:T(128)}, u32[]{:S(2)}) copy-start(s32[64]{0:T(128)} %param.15) | copy-start | bytes 772
  17.1 3.4 %copy-start.2 = (bf16[4,2,2048,256]{3,2,1,0:T(8,128)(2,1)S(1)}, bf16[4,2,2048,256]{3,2,1,0:T(8,128)(2,1)}, u32[]{:S(2)}) copy-start(bf16[4,2,2048,256]{3,2,1,0:T(8,128)(2,1)} %cache_ref.2) | copy-start | bytes 25165828
  20.5 0.7 %copy-start.8 = (s32[4]{0:T(128)S(1)}, s32[4]{0:T(128)}, u32[]{:S(2)}) copy-start(s32[4]{0:T(128)} %length_ref.1) | copy-start | bytes 52
  21.2 13.6 %copy-start.10 = (s32[64]{0:T(128)S(1)}, s32[64]{0:T(128)}, u32[]{:S(2)}) copy-start(s32[64]{0:T(128)} %param.17) | copy-start | bytes 772
  21.2 13.7 %copy-start.5 = (bf16[64,512]{1,0:T(8,128)(2,1)S(1)}, bf16[64,512]{1,0:T(8,128)(2,1)}, u32[]{:S(2)}) copy-start(bf16[64,512]{1,0:T(8,128)(2,1)} %queries_ref.3) | copy-start | bytes 196612
  30.6 11.8 %all-to-all-start.1 = ((bf16[8,16,640]{2,1,0:T(8,128)(2,1)}), bf16[8,16,640]{2,1,0:T(8,128)(2,1)S(1)}, u32[]{:S(2)}, u32[]{:S(2)}) async-start(bf16[8,16,640]{2,1,0:T(8,128)(2,1)} %bitcast.5), calls=%async_computation.1 | async-start | bytes 327680 | tf_op jit(solution)/shard_map/all_to_all | solution.py:259
  34.9 2.2 %copy-start.3 = (bf16[64,2,64,256]{3,2,1,0:T(8,128)(2,1)S(1)}, bf16[64,2,64,256]{3,2,1,0:T(8,128)(2,1)}, u32[]{:S(2)}) copy-start(bf16[64,2,64,256]{3,2,1,0:T(8,128)(2,1)} %cache_ref.3) | copy-start | bytes 12582916
  42.4 2.0 %copy-start = (bf16[512,3584]{1,0:T(8,128)(2,1)S(1)}, bf16[512,3584]{1,0:T(8,128)(2,1)}, u32[]{:S(2)}) copy-start(bf16[512,3584]{1,0:T(8,128)(2,1)} %weight_ref.3) | copy-start | bytes 11010052
  44.4 2.0 %copy-start.1 = (bf16[512,3584]{1,0:T(8,128)(2,1)S(1)}, bf16[512,3584]{1,0:T(8,128)(2,1)}, u32[]{:S(2)}) copy-start(bf16[512,3584]{1,0:T(8,128)(2,1)} %weight_ref.3) | copy-start | bytes 11010052
  44.4 10.2 %copy-start.9 = (f32[896]{0:T(1024)S(1)}, f32[896]{0:T(1024)}, u32[]{:S(2)}) copy-start(f32[896]{0:T(1024)} %param.19) | copy-start | bytes 10756
  44.4 11.4 %copy-start.6 = (bf16[64,896]{1,0:T(8,128)(2,1)S(1)}, bf16[64,896]{1,0:T(8,128)(2,1)}, u32[]{:S(2)}) copy-start(bf16[64,896]{1,0:T(8,128)(2,1)} %hidden_ref.1) | copy-start | bytes 344068
  45.1 1.7 %collective-permute-start = (bf16[64,1792]{1,0:T(8,128)(2,1)S(1)}, bf16[64,1792]{1,0:T(8,128)(2,1)S(1)}, u32[]{:S(2)}, u32[]{:S(2)}) collective-permute-start(bf16[64,1792]{1,0:T(8,128)(2,1)S(1)} %get-tuple-element.18), channel_id=1, source_target_pairs={{0,1},{1,0},{2,3},{3,2},{4,5},{5,4},{6,7},{7,6},{8,9},{9,8},{10,11... | collective-permute-start | bytes 688136 | tf_op jit(solution)/shard_map/ppermute | solution.py:263
  47.0 7.5 %collective-permute-start.1 = (bf16[64,1792]{1,0:T(8,128)(2,1)S(1)}, bf16[64,1792]{1,0:T(8,128)(2,1)S(1)}, u32[]{:S(2)}, u32[]{:S(2)}) collective-permute-start(bf16[64,1792]{1,0:T(8,128)(2,1)S(1)} %get-tuple-element.20), channel_id=1, source_target_pairs={{0,2},{1,3},{2,0},{3,1},{4,6},{5,7},{6,4},{7,5},{8,10},{9,11},{10,... | collective-permute-start | bytes 688136 | tf_op jit(solution)/shard_map/ppermute | solution.py:263
  54.6 1.3 %collective-permute-start.2 = (f32[64,128]{1,0:T(8,128)S(1)}, f32[64,128]{1,0:T(8,128)S(1)}, u32[]{:S(2)}, u32[]{:S(2)}) collective-permute-start(f32[64,128]{1,0:T(8,128)S(1)} %get-tuple-element.22.square_ref), channel_id=1, source_target_pairs={{0,1},{1,0},{2,3},{3,2},{4,5},{5,4},{6,7},{7,6},{8,9},{9,8},{10,11... | collective-permute-start | bytes 98312 | tf_op jit(solution)/shard_map/ppermute | solution.py:263

commit v2 on v1

v2 whole, which is shorter than its diff:
```python
import functools
import math

import jax
import jax.numpy as jnp
from jax import lax
from jax.experimental import pallas as pl
from jax.experimental.pallas import tpu as pltpu
from jax.sharding import PartitionSpec as P

HD = 256
softcap = 50.0
epsilon = 1e-06
score_scale = 1.0 / (softcap * math.sqrt(HD))
weight_scale = softcap * math.log2(math.e)
EXTRA = 128
f32 = jnp.float32
bf16 = jnp.bfloat16
VMEM = pltpu.MemorySpace.VMEM
SMEM = pltpu.MemorySpace.SMEM
VMEM_SPEC = pl.BlockSpec(memory_space=VMEM)
SMEM_SPEC = pl.BlockSpec(memory_space=SMEM)
HBM_SPEC = pl.BlockSpec(memory_space=pltpu.MemorySpace.HBM)
PARAMS = pltpu.CompilerParams(vmem_limit_bytes=40 * 2**20)


def iota(shape, axis):
    return lax.broadcasted_iota(jnp.int32, shape, axis)


def heads_below(block, heads):
    return jnp.concatenate([block[:, h * HD : (h + 1) * HD] for h in range(heads)], axis=0)


def weights_of(scores, alive):
    return jnp.where(alive, jnp.exp2(weight_scale * jnp.tanh(scores * score_scale)), 0.0)


def owners(owner_ref):
    requests = owner_ref.shape[1]
    rows, cols = iota((requests, requests), 0), iota((requests, requests), 1)
    by_col = jnp.broadcast_to(owner_ref[...], (requests, requests)).astype(f32)
    by_row = jnp.sum(jnp.where(rows == cols, by_col, 0.0), axis=1, keepdims=True)
    return by_row, by_col, rows, cols


def route_kernel(
    capacity, owner_hbm, group_hbm, queries_hbm, out_ref, owner_ref, group_ref, queries_ref, sems
):
    pairs = ((owner_hbm, owner_ref), (group_hbm, group_ref), (queries_hbm, queries_ref))
    copies = [pltpu.make_async_copy(a, b, sems.at[i]) for i, (a, b) in enumerate(pairs)]
    for copy in copies:
        copy.start()
    for copy in copies:
        copy.wait()
    requests, width = queries_ref.shape
    slots = out_ref.shape[0]
    by_row, by_col, rows, cols = owners(owner_ref)
    earlier = jnp.where((by_row == by_col) & (rows < cols), 1.0, 0.0)
    position = (by_col[:1] * capacity + jnp.sum(earlier, axis=0, keepdims=True)).astype(jnp.int32)
    matches = iota((slots, requests), 0) == position
    out_ref[:, :width] = jnp.dot(
        jnp.where(matches, 1.0, 0.0).astype(bf16), queries_ref[...], preferred_element_type=f32
    ).astype(bf16)
    numbered = (group_ref[...] + 1).astype(f32)
    mark = jnp.sum(jnp.where(matches, numbered, 0.0), axis=1, keepdims=True)
    out_ref[:, width:] = jnp.broadcast_to(mark, (slots, EXTRA)).astype(bf16)


def suffix_kernel(
    capacity,
    block,
    owner_hbm,
    length_hbm,
    queries_hbm,
    cache_hbm,
    core_ref,
    weight_hbm,
    after_hbm,
    back_ref,
    num_ref,
    den_ref,
    weight_ref,
    owner_ref,
    length_ref,
    queries_ref,
    cache_ref,
    sems,
    cache_sems,
    weight_sems,
):
    requests, slots = back_ref.shape
    window = cache_ref.shape[2]
    heads = queries_ref.shape[1] // HD
    steps = requests // block
    pairs = ((owner_hbm, owner_ref), (length_hbm, length_ref), (queries_hbm, queries_ref))
    copies = [pltpu.make_async_copy(a, b, sems.at[i]) for i, (a, b) in enumerate(pairs)]
    parts = []
    for i in range(steps):
        span = pl.ds(i * block, block)
        parts.append(
            pltpu.make_async_copy(cache_hbm.at[span], cache_ref.at[span], cache_sems.at[i])
        )
    quarter = weight_ref.shape[2]
    weight_copies = []
    for i, q in enumerate((1 - core_ref[0], 3 - core_ref[0], core_ref[0])):
        cols = pl.ds(pl.multiple_of(q * quarter, 128), quarter)
        weight_copies.append(
            pltpu.make_async_copy(weight_hbm.at[:, cols], weight_ref.at[i], weight_sems.at[i])
        )
    for copy in copies + parts + weight_copies:
        copy.start()
    for copy in copies:
        copy.wait()

    by_row, by_col, rows, cols = owners(owner_ref)
    earlier = jnp.where((by_row == by_col) & (cols < rows), 1.0, 0.0)
    rank = jnp.sum(earlier, axis=1, keepdims=True)
    position = (by_row * capacity + rank).astype(jnp.int32)
    back_ref[...] = jnp.where(iota((requests, slots), 1) == position, 1.0, 0.0).astype(bf16)
    live = jnp.sum(
        jnp.where(rows == cols, length_ref[...].astype(f32), 0.0), axis=1, keepdims=True
    ).astype(jnp.int32)

    at = iota((block, block * window), 1)
    first = iota((block, block * window), 0) * window
    for i in range(steps):
        mine = slice(i * block, (i + 1) * block)
        parts[i].wait()
        stacked = heads_below(queries_ref[mine, :], heads)
        keys = cache_ref[mine, 0].reshape(block * window, HD)
        values = cache_ref[mine, 1].reshape(block * window, HD)
        scores = lax.dot_general(
            stacked, keys, (((1,), (1,)), ((), ())), preferred_element_type=f32
        )
        alive = (at >= first) & (at < first + live[mine])
        weights = weights_of(scores, jnp.concatenate([alive] * heads, axis=0))
        numerator = jnp.dot(weights.astype(bf16), values, preferred_element_type=f32)
        denominator = jnp.sum(weights, axis=1, keepdims=True)
        for h in range(heads):
            own = slice(h * block, (h + 1) * block)
            num_ref[mine, h * HD : (h + 1) * HD] = numerator[own]
            den_ref[mine, h * 128 : (h + 1) * 128] = jnp.broadcast_to(
                denominator[own], (block, 128)
            )
    for copy in weight_copies:
        copy.wait()


def prefetch_kernel(cache_hbm, early_ref, sems):
    parts = parts_of(cache_hbm.shape[0])
    copies = [
        pltpu.make_async_copy(cache_hbm.at[parts[i]], early_ref.at[i], sems.at[i])
        for i in range(early_ref.shape[0])
    ]
    for copy in copies:
        copy.start()
    for copy in copies:
        copy.wait()


def parts_of(groups):
    return [(g, part) for g in range(groups) for part in range(2)]


def prompt_kernel(
    chunk,
    window,
    length_hbm,
    slots_ref,
    early_ref,
    cache_hbm,
    out_ref,
    length_ref,
    held,
    sorted_ref,
    done_ref,
    num_ref,
    den_ref,
    sems,
    length_sem,
):
    groups, _, size, _ = cache_hbm.shape
    slots = slots_ref.shape[0]
    width = slots_ref.shape[1] - EXTRA
    heads = width // HD
    parts = parts_of(groups)
    early = early_ref.shape[0]
    length_copy = pltpu.make_async_copy(length_hbm, length_ref, length_sem)
    length_copy.start()
    copies = {
        parts[i]: pltpu.make_async_copy(
            cache_hbm.at[parts[i]], held.at[i - early], sems.at[i - early]
        )
        for i in range(early, len(parts))
    }
    for part in parts[early:]:
        copies[part].start()

    def wait(g, part):
        if (g, part) in copies:
            copies[g, part].wait()

    def read(g, part, span):
        i = parts.index((g, part))
        return early_ref[i, span, :] if i < early else held[i - early, span, :]

    def pieces(total, rows):
        lanes = iota((1, EXTRA), 1)
        extra = jnp.zeros((rows, EXTRA), f32)
        for h in range(heads):
            rest = total[h * rows : (h + 1) * rows]
            for k in range(3):
                piece = rest.astype(bf16).astype(f32)
                rest = rest - piece
                extra = jnp.where(lanes == 3 * h + k, piece, extra)
        return extra.astype(bf16)

    def fold(weights):
        part = weights[:, :128]
        for k in range(1, weights.shape[1] // 128):
            part = part + weights[:, k * 128 : (k + 1) * 128]
        return part

    rows, cols = iota((slots, slots), 0), iota((slots, slots), 1)
    by_row = jnp.broadcast_to(slots_ref[:, width : width + 1].astype(f32), (slots, slots))
    by_col = jnp.sum(jnp.where(rows == cols, by_row, 0.0), axis=0, keepdims=True)
    same = by_row == by_col
    rank_row = jnp.sum(jnp.where(same & (cols < rows), 1.0, 0.0), axis=1, keepdims=True)
    rank_col = jnp.sum(jnp.where(same & (rows < cols), 1.0, 0.0), axis=0, keepdims=True)
    length_copy.wait()
    crowded = jnp.max(jnp.where(by_col > 0.0, rank_col, 0.0)) >= window

    @pl.when(jnp.logical_not(crowded))
    def _():
        at_row = (by_row[:, :1] - 1.0) * window + rank_row
        at_col = jnp.where(by_col > 0.0, (by_col - 1.0) * window + rank_col, -1.0)
        at_row = jnp.where(by_row[:, :1] > 0.0, at_row, -1.0).astype(jnp.int32)
        room = groups * window
        there = jnp.where(iota((room, slots), 0) == at_col.astype(jnp.int32), 1.0, 0.0)
        back = jnp.where(iota((slots, room), 1) == at_row, 1.0, 0.0)
        sorted_ref[...] = jnp.dot(
            there.astype(bf16), slots_ref[:, :width], preferred_element_type=f32
        ).astype(bf16)
        nums, dens, scores = [None] * groups, [None] * groups, [None] * groups
        everything = slice(0, size)
        for u in range(groups + 1):
            if u < groups:
                wait(u, 0)
                stacked = heads_below(sorted_ref[u * window : (u + 1) * window, :], heads)
                scores[u] = lax.dot_general(
                    stacked,
                    read(u, 0, everything),
                    (((1,), (1,)), ((), ())),
                    preferred_element_type=f32,
                )
            if u > 0:
                g = u - 1
                weights = weights_of(scores[g], iota((1, size), 1) < length_ref[g])
                wait(g, 1)
                nums[g] = jnp.dot(
                    weights.astype(bf16), read(g, 1, everything), preferred_element_type=f32
                )
                dens[g] = fold(weights)
        for g in range(groups):
            mine = slice(g * window, (g + 1) * window)
            for h in range(heads):
                done_ref[mine, h * HD : (h + 1) * HD] = nums[g][
                    h * window : (h + 1) * window
                ].astype(bf16)
            done_ref[mine, width:] = pieces(jnp.sum(dens[g], axis=1, keepdims=True), window)
        out_ref[...] = jnp.dot(
            back.astype(bf16), done_ref[...], preferred_element_type=f32
        ).astype(bf16)

    @pl.when(crowded)
    def _():
        for part in parts:
            wait(*part)
        stacked = heads_below(slots_ref[:, :width], heads)
        mark = jnp.concatenate([by_row[:, :1]] * heads, axis=0)
        num_ref[...] = jnp.zeros_like(num_ref)
        den_ref[...] = jnp.zeros_like(den_ref)
        for g in range(groups):
            limit = jnp.where(mark == g + 1.0, length_ref[g], 0)

            @pl.loop(0, (length_ref[g] + chunk - 1) // chunk)
            def _(c):
                span = pl.ds(pl.multiple_of(c * chunk, chunk), chunk)
                scores = lax.dot_general(
                    stacked,
                    read(g, 0, span),
                    (((1,), (1,)), ((), ())),
                    preferred_element_type=f32,
                )
                alive = iota((heads * slots, chunk), 1) < limit - c * chunk
                weights = weights_of(scores, alive)
                num_ref[...] += jnp.dot(
                    weights.astype(bf16), read(g, 1, span), preferred_element_type=f32
                )
                den_ref[...] += fold(weights)

        for h in range(heads):
            out_ref[:, h * HD : (h + 1) * HD] = num_ref[h * slots : (h + 1) * slots].astype(bf16)
        out_ref[:, width:] = pieces(jnp.sum(den_ref[...], axis=1, keepdims=True), slots)


def combine_kernel(
    core_ref, returned_ref, back_ref, num_ref, den_ref, weight_ref, weight_hbm, att_ref, give_ref, last_ref, sem
):
    quarter = weight_ref.shape[2]
    cols = pl.ds(pl.multiple_of((core_ref[0] + 2) * quarter, 128), quarter)
    copy = pltpu.make_async_copy(weight_hbm.at[:, cols], last_ref, sem)
    copy.start()
    width = num_ref.shape[1]
    heads = width // HD
    mine = jnp.dot(back_ref[...], returned_ref[...], preferred_element_type=f32)
    for h in range(heads):
        cols = slice(h * HD, (h + 1) * HD)
        numerator = mine[:, cols] + num_ref[:, cols]
        at = width + 3 * h
        denominator = den_ref[:, h * 128 : h * 128 + 1] + (
            mine[:, at : at + 1] + mine[:, at + 1 : at + 2] + mine[:, at + 2 : at + 3]
        )
        att_ref[:, cols] = (numerator / denominator).astype(bf16)
    for i in range(2):
        give_ref[:, i * quarter : (i + 1) * quarter] = jnp.dot(
            att_ref[...], weight_ref[i], preferred_element_type=f32
        ).astype(bf16)
    copy.wait()


def own_kernel(att_ref, weight_ref, last_ref, own_ref):
    quarter = weight_ref.shape[2]
    own_ref[:, :quarter] = jnp.dot(att_ref[...], weight_ref[2], preferred_element_type=f32)
    own_ref[:, quarter:] = jnp.dot(att_ref[...], last_ref[...], preferred_element_type=f32)


def chip_kernel(own_ref, got_ref, sum_ref, send_ref):
    total = own_ref[...] + got_ref[...].astype(f32)
    sum_ref[...] = total
    send_ref[...] = total.astype(bf16)


def square_kernel(row_ref, sum_ref, got_ref, mine_ref, square_ref):
    width = mine_ref.shape[1]
    total = sum_ref[...] + got_ref[...].astype(f32)
    part = jnp.zeros(square_ref.shape, f32)
    for k in range(total.shape[1] // 128):
        piece = total[:, k * 128 : (k + 1) * 128]
        part = part + piece * piece
    square_ref[...] = part
    mine_ref[...] = jnp.where(row_ref[0] == 0, total[:, :width], total[:, width:])


def final_kernel(features, mine_ref, square_ref, got_ref, gain_ref, hidden_ref, out_ref):
    square = jnp.sum(square_ref[...] + got_ref[...], axis=1, keepdims=True)
    scale = lax.rsqrt(square * (1.0 / features) + epsilon)
    normed = mine_ref[...] * scale * gain_ref[...]
    out_ref[...] = (hidden_ref[...].astype(f32) + normed).astype(bf16)


def call(kernel, outs, ins, **kw):
    specs = [
        pl.BlockSpec(memory_space=SMEM if a.ndim == 1 else VMEM) for a in ins
    ]
    return pl.pallas_call(
        kernel,
        out_shape=outs,
        in_specs=specs,
        out_specs=jax.tree.map(lambda _: pl.BlockSpec(memory_space=VMEM), outs),
        compiler_params=PARAMS,
        **kw,
    )(*ins)


def in_hbm(*arrays):
    return [pltpu.with_memory_space_constraint(a, pltpu.MemorySpace.HBM) for a in arrays]


def shape(dims, dtype):
    return jax.ShapeDtypeStruct(dims, dtype)


def shards(
    hidden_input,
    queries,
    prompt_cache,
    suffix_cache,
    owner_replica,
    group_slot,
    prompt_length,
    suffix_length,
    output_weight,
    post_gain,
):
    replicas = lax.axis_size("replica")
    ranks = lax.axis_size("tensor")
    requests, width = queries.shape
    capacity = max(2, (2 * requests + replicas - 1) // replicas)
    slots = replicas * capacity
    groups, _, size, _ = prompt_cache.shape
    window = suffix_cache.shape[2]
    features = output_weight.shape[1]
    quarter = features // ranks
    heads = width // HD
    index = lax.axis_index("tensor")
    core = (index % 2).reshape(1)
    row = (index // 2).reshape(1)

    def exchange(x):
        blocks = x.reshape(replicas, capacity, width + EXTRA)
        blocks = lax.all_to_all(blocks, "replica", split_axis=0, concat_axis=0, tiled=True)
        return blocks.reshape(slots, width + EXTRA)

    def permute(x, bit):
        return lax.ppermute(x, "tensor", [(i, i ^ bit) for i in range(ranks)])

    owner_row = owner_replica.reshape(1, requests)
    sent = pl.pallas_call(
        functools.partial(route_kernel, capacity),
        out_shape=shape((slots, width + EXTRA), bf16),
        in_specs=[HBM_SPEC] * 3,
        out_specs=VMEM_SPEC,
        scratch_shapes=[
            pltpu.VMEM((1, requests), jnp.int32),
            pltpu.VMEM((1, requests), jnp.int32),
            pltpu.VMEM((requests, width), bf16),
            pltpu.SemaphoreType.DMA((3,)),
        ],
        compiler_params=PARAMS,
    )(*in_hbm(owner_row, group_slot.reshape(1, requests), queries))
    got = exchange(sent)

    early = 3
    prefetched = pl.pallas_call(
        prefetch_kernel,
        out_shape=pltpu.VMEM((early, size, HD), bf16),
        in_specs=[HBM_SPEC],
        out_specs=VMEM_SPEC,
        scratch_shapes=[pltpu.SemaphoreType.DMA((early,))],
        compiler_params=PARAMS,
        cost_estimate=pl.CostEstimate(
            flops=0, bytes_accessed=2 * early * size * HD * 2, transcendentals=0
        ),
    )(*in_hbm(prompt_cache))

    chunk = math.gcd(512, size)
    fit = min(48, slots)
    answered = pl.pallas_call(
        functools.partial(prompt_kernel, chunk, fit),
        out_shape=shape((slots, width + EXTRA), bf16),
        in_specs=[HBM_SPEC, VMEM_SPEC, VMEM_SPEC, HBM_SPEC],
        out_specs=VMEM_SPEC,
        scratch_shapes=[
            pltpu.SMEM((groups,), jnp.int32),
            pltpu.VMEM((2 * groups - early, size, HD), bf16),
            pltpu.VMEM((groups * fit, width), bf16),
            pltpu.VMEM((groups * fit, width + EXTRA), bf16),
            pltpu.VMEM((heads * slots, HD), f32),
            pltpu.VMEM((heads * slots, 128), f32),
            pltpu.SemaphoreType.DMA((2 * groups - early,)),
            pltpu.SemaphoreType.DMA,
        ],
        compiler_params=PARAMS,
    )(
        *in_hbm(prompt_length),
        got,
        pltpu.with_memory_space_constraint(prefetched, VMEM),
        *in_hbm(prompt_cache),
    )
    returned = exchange(answered)

    block = math.gcd(16, requests)
    back, own_num, own_den, weight = pl.pallas_call(
        functools.partial(suffix_kernel, capacity, block),
        out_shape=[
            shape((requests, slots), bf16),
            shape((requests, width), f32),
            shape((requests, heads * 128), f32),
            pltpu.VMEM((3, width, quarter), bf16),
        ],
        in_specs=[HBM_SPEC] * 4 + [SMEM_SPEC, HBM_SPEC, HBM_SPEC],
        out_specs=[VMEM_SPEC] * 4,
        scratch_shapes=[
            pltpu.VMEM((1, requests), jnp.int32),
            pltpu.VMEM((1, requests), jnp.int32),
            pltpu.VMEM((requests, width), bf16),
            pltpu.VMEM(suffix_cache.shape, bf16),
            pltpu.SemaphoreType.DMA((3,)),
            pltpu.SemaphoreType.DMA((requests // block,)),
            pltpu.SemaphoreType.DMA((3,)),
        ],
        compiler_params=PARAMS,
        cost_estimate=pl.CostEstimate(
            flops=8 * requests * window * HD * block,
            bytes_accessed=(suffix_cache.size + output_weight.size) * 2,
            transcendentals=0,
        ),
    )(
        *in_hbm(owner_row, suffix_length.reshape(1, requests), queries, suffix_cache),
        core,
        *in_hbm(output_weight, answered),
    )
    weight = pltpu.with_memory_space_constraint(weight, VMEM)

    attention, give, last = pl.pallas_call(
        combine_kernel,
        out_shape=[
            shape((requests, width), bf16),
            shape((requests, 2 * quarter), bf16),
            pltpu.VMEM((width, quarter), bf16),
        ],
        in_specs=[SMEM_SPEC] + [VMEM_SPEC] * 5 + [HBM_SPEC],
        out_specs=[VMEM_SPEC] * 3,
        scratch_shapes=[pltpu.SemaphoreType.DMA],
        compiler_params=PARAMS,
    )(core, returned, back, own_num, own_den, weight, *in_hbm(output_weight))
    received = permute(give, 1)
    own = call(
        own_kernel,
        shape((requests, 2 * quarter), f32),
        [attention, weight, pltpu.with_memory_space_constraint(last, VMEM)],
    )
    chip, send = call(
        chip_kernel,
        [shape((requests, 2 * quarter), f32), shape((requests, 2 * quarter), bf16)],
        [own, received],
    )
    far = permute(send, 2)
    mine, square = call(
        square_kernel,
        [shape((requests, quarter), f32), shape((requests, 128), f32)],
        [row, chip, far],
    )
    beside = permute(square, 1)
    return call(
        functools.partial(final_kernel, features),
        shape((requests, quarter), bf16),
        [mine, square, beside, post_gain.reshape(1, quarter), hidden_input],
    )


def solution(mesh):
    in_specs = (
        P("replica", "tensor"),
        P("replica", "tensor"),
        P("replica", None, None, "tensor"),
        P("replica", None, None, "tensor"),
        P("replica", None),
        P("replica"),
        P("replica"),
        P("replica"),
        P("tensor", None),
        P("tensor"),
    )
    out_specs = P("replica", "tensor")
    return jax.shard_map(shards, mesh=mesh, in_specs=in_specs, out_specs=out_specs, check_vma=False)
```

time: 56.2 us -> 46.4 us (0.83); the launches traced: 56.6 us -> 46 us
  blocking collectives: 14.6 us -> 0 us
  local copies, waits for them, and re-layouts: 11.8 us -> 0.02 us
  waiting for transfers between devices: 10.3 us -> 17 us
  starting transfers between devices: 5.92 us -> 12.4 us
  Pallas kernels: 13.8 us -> 16.5 us
    all_to_all x1 -> x0, blocking collectives: 14.6 us -> none  [exchange(): lax.all_to_all(blocks, 'replica', split_axis=0, concat_axis=0, tiled=True)]
    unnamed x23 -> x4, local copies, waits for them, and re-layouts: 11.7 us -> 0.01 us
    all_to_all x1 -> x2, starting transfers between devices: 4.19 us -> 10.7 us  [exchange(): lax.all_to_all(blocks, 'replica', split_axis=0, concat_axis=0, tiled=True)]
    all_to_all x1 -> x2, waiting for transfers between devices: 3.18 us -> 8.63 us  [exchange(): lax.all_to_all(blocks, 'replica', split_axis=0, concat_axis=0, tiled=True)]
    pallas_call x2 -> x5, Pallas kernels: 11.5 us -> 15.1 us  [the longest x1 5.47 us: shards(): pl.pallas_call(functools.partial(prompt_kernel, chunk, fit), out_shape=sh...]
    ppermute x3, waiting for transfers between devices: 7.1 us -> 8.34 us  [permute(): return lax.ppermute(x, 'tensor', [(i, i ^ bit) for i in range(ranks)])]
    pallas_call x6 -> x4, Pallas kernels: 2.33 us -> 1.35 us  [call(): pl.pallas_call(kernel, out_shape=outs, in_specs=specs, out_specs=jax.tree...]
  transfers between devices with their start and end apart: 4 -> 5, of which waited for: 3 -> 5; matrix products, arithmetic and copies ran while one was open for 0% -> 0% of each run, Pallas kernels for 4% -> 15%
where the time goes in v2:
time: 46.4 us; the launch traced here: 46 us
  waiting for transfers between devices  17 us (37%)
  Pallas kernels  16.5 us (36%)
  starting transfers between devices  12.4 us (27%)
    all_to_all x2, starting transfers between devices, exchange(): lax.all_to_all(blocks, 'replica', split_axis=0, concat_axis=0, tiled=True)  10.7 us
    all_to_all x2, waiting for transfers between devices, exchange(): lax.all_to_all(blocks, 'replica', split_axis=0, concat_axis=0, tiled=True)  8.63 us
    ppermute x3, waiting for transfers between devices, permute(): return lax.ppermute(x, 'tensor', [(i, i ^ bit) for i in range(ranks)])  8.34 us
    pallas_call x1, Pallas kernels, shards(): pl.pallas_call(functools.partial(prompt_kernel, chunk, fit), out_shape=sh...  5.47 us
    pallas_call x1, Pallas kernels, shards(): pl.pallas_call(functools.partial(suffix_kernel, capacity, block), out_sha...  4.52 us
    pallas_call x1, Pallas kernels, shards(): pl.pallas_call(prefetch_kernel, out_shape=pltpu.VMEM((early, size, HD), b...  1.88 us
    pallas_call x1, Pallas kernels, shards(): pl.pallas_call(functools.partial(route_kernel, capacity), out_shape=shape...  1.82 us
    ppermute x3, starting transfers between devices, permute(): return lax.ppermute(x, 'tensor', [(i, i ^ bit) for i in range(ranks)])  1.73 us
  transfers between devices with their start and end apart: 5, of which 5 were waited for; matrix products, arithmetic and copies ran while one was open for 0% of the time, Pallas kernels for 15%

profile of v2, /device:TPU:0, one launch (start us, length us, event | category | flops | bytes accessed | tf_op | source)
XLA Modules:
  0.0 46.0 jit_solution(3179877912844303376)
XLA Ops:
  0.0 1.8 %shard_map.100 = bf16[128,640]{1,0:T(8,128)(2,1)} custom-call(s32[1,64]{1,0:T(1,128)} %bitcast.11, s32[1,64]{1,0:T(1,128)} %bitcast.13, bf16[64,512]{1,0:T(8,128)(2,1)} %queries_hbm.3), custom_call_target="tpu_custom_call" | custom-call | tf_op jit(solution)/shard_map/pallas_call | solution.py:420
  1.8 7.3 %all-to-all-start = ((bf16[8,16,640]{2,1,0:T(8,128)(2,1)}), bf16[8,16,640]{2,1,0:T(8,128)(2,1)S(1)}, u32[]{:S(2)}, u32[]{:S(2)}) async-start(bf16[8,16,640]{2,1,0:T(8,128)(2,1)} %bitcast.4), calls=%async_computation | async-start | bytes 327680 | tf_op jit(solution)/shard_map/all_to_all | solution.py:413
  9.1 1.9 %shard_map.101.early_ref = bf16[3,2048,256]{2,1,0:T(8,128)(2,1)S(1)} custom-call(bf16[4,2,2048,256]{3,2,1,0:T(8,128)(2,1)} %cache_hbm.4), custom_call_target="tpu_custom_call" | custom-call | bytes 6291456 | tf_op jit(solution)/shard_map/pallas_call | solution.py:436
  11.0 5.7 %all-to-all-done = bf16[8,16,640]{2,1,0:T(8,128)(2,1)S(1)} async-done(((bf16[8,16,640]{2,1,0:T(8,128)(2,1)}), bf16[8,16,640]{2,1,0:T(8,128)(2,1)S(1)}, u32[]{:S(2)}, u32[]{:S(2)}) %all-to-all-start) | async-done | bytes 163872 | tf_op jit(solution)/shard_map/all_to_all | solution.py:413
  16.7 5.5 %shard_map.102.after_hbm = bf16[128,640]{1,0:T(8,128)(2,1)} custom-call(s32[4]{0:T(128)} %length_hbm.1, bf16[128,640]{1,0:T(8,128)(2,1)S(1)} %bitcast.10, bf16[3,2048,256]{2,1,0:T(8,128)(2,1)S(1)} %shard_map.101.early_ref, bf16[4,2,2048,256]{3,2,1,0:T(8,128)(2,1)} %cache_hbm.4), custom_call_target="tpu_custom_call" | custom-call | tf_op jit(solution)/shard_map/pallas_call | solution.py:450
  22.1 3.4 %all-to-all-start.1 = ((bf16[8,16,640]{2,1,0:T(8,128)(2,1)}), bf16[8,16,640]{2,1,0:T(8,128)(2,1)S(1)}, u32[]{:S(2)}, u32[]{:S(2)}) async-start(bf16[8,16,640]{2,1,0:T(8,128)(2,1)} %bitcast.6), calls=%async_computation.1 | async-start | bytes 327680 | tf_op jit(solution)/shard_map/all_to_all | solution.py:413
  25.6 4.5 %shard_map.103 = (bf16[64,128]{1,0:T(8,128)(2,1)S(1)}, f32[64,512]{1,0:T(8,128)S(1)}, f32[64,256]{1,0:T(8,128)S(1)}, bf16[3,512,896]{2,1,0:T(8,128)(2,1)S(1)}) custom-call(s32[1,64]{1,0:T(1,128)} %bitcast.12, s32[1,64]{1,0:T(1,128)} %bitcast.14, bf16[64,512]{1,0:T(8,128)(2,1)} %queries_hbm.3, bf16[64,2,64,256]{3,2,1,0:T(8,128)(2,1)} %cache_hbm.5, ...), custom_call_target="tpu_custom_call" | custom-call | flops 134217728 | bytes 7864320 | tf_op jit(solution)/shard_map/pallas_call | solution.py:475
  30.1 3.0 %all-to-all-done.1 = bf16[8,16,640]{2,1,0:T(8,128)(2,1)S(1)} async-done(((bf16[8,16,640]{2,1,0:T(8,128)(2,1)}), bf16[8,16,640]{2,1,0:T(8,128)(2,1)S(1)}, u32[]{:S(2)}, u32[]{:S(2)}) %all-to-all-start.1) | async-done | bytes 163872 | tf_op jit(solution)/shard_map/all_to_all | solution.py:413
  33.0 1.4 %shard_map.104 = (bf16[64,512]{1,0:T(8,128)(2,1)S(1)}, bf16[64,1792]{1,0:T(8,128)(2,1)S(1)}, bf16[512,896]{1,0:T(8,128)(2,1)S(1)}) custom-call(s32[1]{0:T(128)} %bitcast.1.core_ref, bf16[128,640]{1,0:T(8,128)(2,1)S(1)} %bitcast.9, bf16[64,128]{1,0:T(8,128)(2,1)S(1)} %get-tuple-element.16.back_ref, f32[64,512]{1,0:T(8,128)S(1)} %get-tuple-element.17.num_ref, ...), custom_call_target="tpu_custom_call" | custom-call | tf_op jit(solution)/shard_map/pallas_call | solution.py:507
  34.5 0.0 copy-start.1
  34.5 0.0 copy-start
  34.5 0.1 collective-permute-start
  34.6 0.4 shard_map.105.own_ref
  35.0 1.0 %collective-permute-done.got_ref = bf16[64,1792]{1,0:T(8,128)(2,1)S(1)} collective-permute-done((bf16[64,1792]{1,0:T(8,128)(2,1)S(1)}, bf16[64,1792]{1,0:T(8,128)(2,1)S(1)}, u32[]{:S(2)}, u32[]{:S(2)}) %collective-permute-start) | collective-permute-done | bytes 229408 | tf_op jit(solution)/shard_map/ppermute | solution.py:417
  36.1 0.1 shard_map.106
  36.1 1.6 %collective-permute-start.1 = (bf16[64,1792]{1,0:T(8,128)(2,1)S(1)}, bf16[64,1792]{1,0:T(8,128)(2,1)S(1)}, u32[]{:S(2)}, u32[]{:S(2)}) collective-permute-start(bf16[64,1792]{1,0:T(8,128)(2,1)S(1)} %get-tuple-element.24), channel_id=1, source_target_pairs={{0,2},{1,3},{2,0},{3,1},{4,6},{5,7},{6,4},{7,5},{8,10},{9,11},{10,... | collective-permute-start | bytes 688136 | tf_op jit(solution)/shard_map/ppermute | solution.py:417
  37.7 6.1 %collective-permute-done.1.got_ref = bf16[64,1792]{1,0:T(8,128)(2,1)S(1)} collective-permute-done((bf16[64,1792]{1,0:T(8,128)(2,1)S(1)}, bf16[64,1792]{1,0:T(8,128)(2,1)S(1)}, u32[]{:S(2)}, u32[]{:S(2)}) %collective-permute-start.1) | collective-permute-done | bytes 229408 | tf_op jit(solution)/shard_map/ppermute | solution.py:417
  43.8 0.1 shard_map.107
  43.9 0.1 collective-permute-start.2
  44.0 0.0 copy-done.1
  44.0 1.2 %collective-permute-done.2.got_ref = f32[64,128]{1,0:T(8,128)S(1)} collective-permute-done((f32[64,128]{1,0:T(8,128)S(1)}, f32[64,128]{1,0:T(8,128)S(1)}, u32[]{:S(2)}, u32[]{:S(2)}) %collective-permute-start.2) | collective-permute-done | bytes 32800 | tf_op jit(solution)/shard_map/ppermute | solution.py:417
  45.2 0.0 copy-done
  45.2 0.8 %shard_map.108 = bf16[64,896]{1,0:T(8,128)(2,1)} custom-call(f32[64,896]{1,0:T(8,128)S(1)} %get-tuple-element.25.mine_ref, f32[64,128]{1,0:T(8,128)S(1)} %get-tuple-element.26.square_ref, f32[64,128]{1,0:T(8,128)S(1)} %collective-permute-done.2.got_ref, f32[1,896]{1,0:T(1,128)S(1)} %reshape.39.gain_ref, bf16[64,896]{1,0:T(8,128)(2,1)S(1)} %copy-done), custom_call_target="tpu_custom_call" | custom-call | tf_op jit(solution)/shard_map/pallas_call | solution.py:367
  (1 shorter events, 0.0 us)
Async XLA Ops:
  1.8 14.8 %all-to-all-start = ((bf16[8,16,640]{2,1,0:T(8,128)(2,1)}), bf16[8,16,640]{2,1,0:T(8,128)(2,1)S(1)}, u32[]{:S(2)}, u32[]{:S(2)}) async-start(bf16[8,16,640]{2,1,0:T(8,128)(2,1)} %bitcast.4), calls=%async_computation | async-start | bytes 327680 | tf_op jit(solution)/shard_map/all_to_all | solution.py:413
  22.1 10.9 %all-to-all-start.1 = ((bf16[8,16,640]{2,1,0:T(8,128)(2,1)}), bf16[8,16,640]{2,1,0:T(8,128)(2,1)S(1)}, u32[]{:S(2)}, u32[]{:S(2)}) async-start(bf16[8,16,640]{2,1,0:T(8,128)(2,1)} %bitcast.6), calls=%async_computation.1 | async-start | bytes 327680 | tf_op jit(solution)/shard_map/all_to_all | solution.py:413
  34.5 9.5 %copy-start.1 = (f32[896]{0:T(1024)S(1)}, f32[896]{0:T(1024)}, u32[]{:S(2)}) copy-start(f32[896]{0:T(1024)} %param.19) | copy-start | bytes 10756
  34.5 10.7 %copy-start = (bf16[64,896]{1,0:T(8,128)(2,1)S(1)}, bf16[64,896]{1,0:T(8,128)(2,1)}, u32[]{:S(2)}) copy-start(bf16[64,896]{1,0:T(8,128)(2,1)} %hidden_ref.1) | copy-start | bytes 344068
  34.5 1.6 %collective-permute-start = (bf16[64,1792]{1,0:T(8,128)(2,1)S(1)}, bf16[64,1792]{1,0:T(8,128)(2,1)S(1)}, u32[]{:S(2)}, u32[]{:S(2)}) collective-permute-start(bf16[64,1792]{1,0:T(8,128)(2,1)S(1)} %get-tuple-element.22), channel_id=1, source_target_pairs={{0,1},{1,0},{2,3},{3,2},{4,5},{5,4},{6,7},{7,6},{8,9},{9,8},{10,11... | collective-permute-start | bytes 688136 | tf_op jit(solution)/shard_map/ppermute | solution.py:417
  36.1 7.7 %collective-permute-start.1 = (bf16[64,1792]{1,0:T(8,128)(2,1)S(1)}, bf16[64,1792]{1,0:T(8,128)(2,1)S(1)}, u32[]{:S(2)}, u32[]{:S(2)}) collective-permute-start(bf16[64,1792]{1,0:T(8,128)(2,1)S(1)} %get-tuple-element.24), channel_id=1, source_target_pairs={{0,2},{1,3},{2,0},{3,1},{4,6},{5,7},{6,4},{7,5},{8,10},{9,11},{10,... | collective-permute-start | bytes 688136 | tf_op jit(solution)/shard_map/ppermute | solution.py:417
  43.9 1.3 %collective-permute-start.2 = (f32[64,128]{1,0:T(8,128)S(1)}, f32[64,128]{1,0:T(8,128)S(1)}, u32[]{:S(2)}, u32[]{:S(2)}) collective-permute-start(f32[64,128]{1,0:T(8,128)S(1)} %get-tuple-element.26.square_ref), channel_id=1, source_target_pairs={{0,1},{1,0},{2,3},{3,2},{4,5},{5,4},{6,7},{7,6},{8,9},{9,8},{10,11... | collective-permute-start | bytes 98312 | tf_op jit(solution)/shard_map/ppermute | solution.py:417

commit v3 on v2

--- a/solution.py
+++ b/solution.py
@@ -147,15 +147,22 @@
         copy.wait()
 
 
-def prefetch_kernel(cache_hbm, early_ref, sems):
+def prefetch_kernel(core_ref, cache_hbm, weight_hbm, early_ref, last_hbm, staged, sems, last_sem):
     parts = parts_of(cache_hbm.shape[0])
+    quarter = last_hbm.shape[1]
+    cols = pl.ds(pl.multiple_of((core_ref[0] + 2) * quarter, 128), quarter)
+    stage = pltpu.make_async_copy(weight_hbm.at[:, cols], staged, last_sem)
+    unstage = pltpu.make_async_copy(staged, last_hbm, last_sem)
+    stage.start()
     copies = [
         pltpu.make_async_copy(cache_hbm.at[parts[i]], early_ref.at[i], sems.at[i])
         for i in range(early_ref.shape[0])
     ]
     for copy in copies:
         copy.start()
-    for copy in copies:
+    stage.wait()
+    unstage.start()
+    for copy in copies + [unstage]:
         copy.wait()
 
 
@@ -197,10 +204,6 @@
     for part in parts[early:]:
         copies[part].start()
 
-    def wait(g, part):
-        if (g, part) in copies:
-            copies[g, part].wait()
-
     def read(g, part, span):
         i = parts.index((g, part))
         return early_ref[i, span, :] if i < early else held[i - early, span, :]
@@ -231,52 +234,51 @@
     length_copy.wait()
     crowded = jnp.max(jnp.where(by_col > 0.0, rank_col, 0.0)) >= window
 
-    @pl.when(jnp.logical_not(crowded))
-    def _():
-        at_row = (by_row[:, :1] - 1.0) * window + rank_row
-        at_col = jnp.where(by_col > 0.0, (by_col - 1.0) * window + rank_col, -1.0)
-        at_row = jnp.where(by_row[:, :1] > 0.0, at_row, -1.0).astype(jnp.int32)
-        room = groups * window
-        there = jnp.where(iota((room, slots), 0) == at_col.astype(jnp.int32), 1.0, 0.0)
-        back = jnp.where(iota((slots, room), 1) == at_row, 1.0, 0.0)
-        sorted_ref[...] = jnp.dot(
-            there.astype(bf16), slots_ref[:, :width], preferred_element_type=f32
-        ).astype(bf16)
-        nums, dens, scores = [None] * groups, [None] * groups, [None] * groups
-        everything = slice(0, size)
-        for u in range(groups + 1):
-            if u < groups:
-                wait(u, 0)
-                stacked = heads_below(sorted_ref[u * window : (u + 1) * window, :], heads)
-                scores[u] = lax.dot_general(
-                    stacked,
-                    read(u, 0, everything),
-                    (((1,), (1,)), ((), ())),
-                    preferred_element_type=f32,
-                )
-            if u > 0:
-                g = u - 1
-                weights = weights_of(scores[g], iota((1, size), 1) < length_ref[g])
-                wait(g, 1)
-                nums[g] = jnp.dot(
-                    weights.astype(bf16), read(g, 1, everything), preferred_element_type=f32
-                )
-                dens[g] = fold(weights)
+    at_row = (by_row[:, :1] - 1.0) * window + rank_row
+    at_row = jnp.where(by_row[:, :1] > 0.0, at_row, -1.0).astype(jnp.int32)
+    at_col = jnp.where(by_col > 0.0, (by_col - 1.0) * window + rank_col, -1.0).astype(jnp.int32)
+    room = groups * window
+    there = jnp.where(iota((room, slots), 0) == at_col, 1.0, 0.0).astype(bf16)
+    back = jnp.where(iota((slots, room), 1) == at_row, 1.0, 0.0).astype(bf16)
+    for h in range(heads):
+        part = jnp.dot(there, slots_ref[:, h * HD : (h + 1) * HD], preferred_element_type=f32)
         for g in range(groups):
+            at = (g * heads + h) * window
+            sorted_ref[at : at + window, :] = part[g * window : (g + 1) * window].astype(bf16)
+    scores = [None] * groups
+    waited = early
+    everything = slice(0, size)
+    for u in range(groups + 1):
+        needed = min(2 * u + 1, len(parts))
+        if needed > waited:
+            needed = min(needed + 1, len(parts))
+            for part in parts[waited:needed]:
+                copies[part].wait()
+            waited = needed
+        if u < groups:
+            scores[u] = lax.dot_general(
+                sorted_ref[u * heads * window : (u + 1) * heads * window, :],
+                read(u, 0, everything),
+                (((1,), (1,)), ((), ())),
+                preferred_element_type=f32,
+            )
+        if u > 0:
+            g = u - 1
+            weights = weights_of(scores[g], iota((1, size), 1) < length_ref[g])
+            num = jnp.dot(
+                weights.astype(bf16), read(g, 1, everything), preferred_element_type=f32
+            )
             mine = slice(g * window, (g + 1) * window)
             for h in range(heads):
-                done_ref[mine, h * HD : (h + 1) * HD] = nums[g][
+                done_ref[mine, h * HD : (h + 1) * HD] = num[
                     h * window : (h + 1) * window
                 ].astype(bf16)
-            done_ref[mine, width:] = pieces(jnp.sum(dens[g], axis=1, keepdims=True), window)
-        out_ref[...] = jnp.dot(
-            back.astype(bf16), done_ref[...], preferred_element_type=f32
-        ).astype(bf16)
+            den = jnp.sum(fold(weights), axis=1, keepdims=True)
+            done_ref[mine, width:] = pieces(den, window)
+    out_ref[...] = jnp.dot(back, done_ref[...], preferred_element_type=f32).astype(bf16)
 
     @pl.when(crowded)
     def _():
-        for part in parts:
-            wait(*part)
         stacked = heads_below(slots_ref[:, :width], heads)
         mark = jnp.concatenate([by_row[:, :1]] * heads, axis=0)
         num_ref[...] = jnp.zeros_like(num_ref)
@@ -306,12 +308,9 @@
 
 
 def combine_kernel(
-    core_ref, returned_ref, back_ref, num_ref, den_ref, weight_ref, weight_hbm, att_ref, give_ref, last_ref, sem
+    returned_ref, back_ref, num_ref, den_ref, weight_ref, att_ref, give_ref
 ):
     quarter = weight_ref.shape[2]
-    cols = pl.ds(pl.multiple_of((core_ref[0] + 2) * quarter, 128), quarter)
-    copy = pltpu.make_async_copy(weight_hbm.at[:, cols], last_ref, sem)
-    copy.start()
     width = num_ref.shape[1]
     heads = width // HD
     mine = jnp.dot(back_ref[...], returned_ref[...], preferred_element_type=f32)
@@ -327,7 +326,6 @@
         give_ref[:, i * quarter : (i + 1) * quarter] = jnp.dot(
             att_ref[...], weight_ref[i], preferred_element_type=f32
         ).astype(bf16)
-    copy.wait()
 
 
 def own_kernel(att_ref, weight_ref, last_ref, own_ref):
@@ -419,7 +417,7 @@
     owner_row = owner_replica.reshape(1, requests)
     sent = pl.pallas_call(
         functools.partial(route_kernel, capacity),
-        out_shape=shape((slots, width + EXTRA), bf16),
+        out_shape=pltpu.VMEM((slots, width + EXTRA), bf16),
         in_specs=[HBM_SPEC] * 3,
         out_specs=VMEM_SPEC,
         scratch_shapes=[
@@ -433,29 +431,33 @@
     got = exchange(sent)
 
     early = 3
-    prefetched = pl.pallas_call(
+    prefetched, last = pl.pallas_call(
         prefetch_kernel,
-        out_shape=pltpu.VMEM((early, size, HD), bf16),
-        in_specs=[HBM_SPEC],
-        out_specs=VMEM_SPEC,
-        scratch_shapes=[pltpu.SemaphoreType.DMA((early,))],
+        out_shape=[pltpu.VMEM((early, size, HD), bf16), pltpu.HBM((width, quarter), bf16)],
+        in_specs=[SMEM_SPEC, HBM_SPEC, HBM_SPEC],
+        out_specs=[VMEM_SPEC, HBM_SPEC],
+        scratch_shapes=[
+            pltpu.VMEM((width, quarter), bf16),
+            pltpu.SemaphoreType.DMA((early,)),
+            pltpu.SemaphoreType.DMA,
+        ],
         compiler_params=PARAMS,
         cost_estimate=pl.CostEstimate(
             flops=0, bytes_accessed=2 * early * size * HD * 2, transcendentals=0
         ),
-    )(*in_hbm(prompt_cache))
+    )(core, *in_hbm(prompt_cache, output_weight))
 
     chunk = math.gcd(512, size)
     fit = min(48, slots)
     answered = pl.pallas_call(
         functools.partial(prompt_kernel, chunk, fit),
-        out_shape=shape((slots, width + EXTRA), bf16),
+        out_shape=pltpu.VMEM((slots, width + EXTRA), bf16),
         in_specs=[HBM_SPEC, VMEM_SPEC, VMEM_SPEC, HBM_SPEC],
         out_specs=VMEM_SPEC,
         scratch_shapes=[
             pltpu.SMEM((groups,), jnp.int32),
             pltpu.VMEM((2 * groups - early, size, HD), bf16),
-            pltpu.VMEM((groups * fit, width), bf16),
+            pltpu.VMEM((groups * heads * fit, HD), bf16),
             pltpu.VMEM((groups * fit, width + EXTRA), bf16),
             pltpu.VMEM((heads * slots, HD), f32),
             pltpu.VMEM((heads * slots, 128), f32),
@@ -504,23 +506,16 @@
     )
     weight = pltpu.with_memory_space_constraint(weight, VMEM)
 
-    attention, give, last = pl.pallas_call(
+    attention, give = call(
         combine_kernel,
-        out_shape=[
-            shape((requests, width), bf16),
-            shape((requests, 2 * quarter), bf16),
-            pltpu.VMEM((width, quarter), bf16),
-        ],
-        in_specs=[SMEM_SPEC] + [VMEM_SPEC] * 5 + [HBM_SPEC],
-        out_specs=[VMEM_SPEC] * 3,
-        scratch_shapes=[pltpu.SemaphoreType.DMA],
-        compiler_params=PARAMS,
-    )(core, returned, back, own_num, own_den, weight, *in_hbm(output_weight))
+        [shape((requests, width), bf16), shape((requests, 2 * quarter), bf16)],
+        [returned, back, own_num, own_den, weight],
+    )
     received = permute(give, 1)
     own = call(
         own_kernel,
         shape((requests, 2 * quarter), f32),
-        [attention, weight, pltpu.with_memory_space_constraint(last, VMEM)],
+        [attention, weight, last],
     )
     chip, send = call(
         chip_kernel,

time: 46.4 us -> 44.5 us (0.959)
  waiting for transfers between devices: 17 us -> 15.7 us
  Pallas kernels: 16.5 us -> 15.5 us
    pallas_call x4 -> x3, Pallas kernels: 10.6 us -> 8.95 us  [the longest x1 4.35 us: shards(): pl.pallas_call(functools.partial(prompt_kernel, chunk, fit), out_shape=pl...]
    all_to_all x2, waiting for transfers between devices: 8.63 us -> 7.75 us  [exchange(): lax.all_to_all(blocks, 'replica', split_axis=0, concat_axis=0, tiled=True)]
    pallas_call x4 -> x5, Pallas kernels: 1.35 us -> 2.07 us  [call(): pl.pallas_call(kernel, out_shape=outs, in_specs=specs, out_specs=jax.tree...]
  transfers between devices with their start and end apart: 5 -> 5, of which waited for: 5 -> 5; matrix products, arithmetic and copies ran while one was open for 0% -> 0% of each run, Pallas kernels for 15% -> 18%
where the time goes in v3:
time: 44.5 us; the launch traced here: 44.1 us
  waiting for transfers between devices  15.7 us (35%)
  Pallas kernels  15.5 us (35%)
  starting transfers between devices  12.4 us (28%)
    all_to_all x2, starting transfers between devices, exchange(): lax.all_to_all(blocks, 'replica', split_axis=0, concat_axis=0, tiled=True)  10.7 us
    ppermute x3, waiting for transfers between devices, permute(): return lax.ppermute(x, 'tensor', [(i, i ^ bit) for i in range(ranks)])  7.97 us
    all_to_all x2, waiting for transfers between devices, exchange(): lax.all_to_all(blocks, 'replica', split_axis=0, concat_axis=0, tiled=True)  7.75 us
    pallas_call x1, Pallas kernels, shards(): pl.pallas_call(functools.partial(suffix_kernel, capacity, block), out_sha...  4.52 us
    pallas_call x1, Pallas kernels, shards(): pl.pallas_call(functools.partial(prompt_kernel, chunk, fit), out_shape=pl...  4.35 us
    pallas_call x1, Pallas kernels, shards(): pl.pallas_call(prefetch_kernel, out_shape=[pltpu.VMEM((early, size, HD),...  2.77 us
    pallas_call x5, Pallas kernels, call(): pl.pallas_call(kernel, out_shape=outs, in_specs=specs, out_specs=jax.tree...  2.07 us
    pallas_call x1, Pallas kernels, shards(): pl.pallas_call(functools.partial(route_kernel, capacity), out_shape=pltpu...  1.82 us
  transfers between devices with their start and end apart: 5, of which 5 were waited for; matrix products, arithmetic and copies ran while one was open for 0% of the time, Pallas kernels for 18%

profile of v3, /device:TPU:0, one launch (start us, length us, event | category | flops | bytes accessed | tf_op | source)
XLA Modules:
  0.0 44.1 jit_solution(14258798439025637946)
XLA Ops:
  0.0 1.8 %shard_map.100 = bf16[128,640]{1,0:T(8,128)(2,1)} custom-call(s32[1,64]{1,0:T(1,128)} %bitcast.11, s32[1,64]{1,0:T(1,128)} %bitcast.13, bf16[64,512]{1,0:T(8,128)(2,1)} %queries_hbm.3), custom_call_target="tpu_custom_call" | custom-call | tf_op jit(solution)/shard_map/pallas_call | solution.py:418
  1.8 7.3 %all-to-all-start = ((bf16[8,16,640]{2,1,0:T(8,128)(2,1)}), bf16[8,16,640]{2,1,0:T(8,128)(2,1)S(1)}, u32[]{:S(2)}, u32[]{:S(2)}) async-start(bf16[8,16,640]{2,1,0:T(8,128)(2,1)} %bitcast.3), calls=%async_computation | async-start | bytes 327680 | tf_op jit(solution)/shard_map/all_to_all | solution.py:411
  9.1 2.8 %shard_map.101 = (bf16[3,2048,256]{2,1,0:T(8,128)(2,1)S(1)}, bf16[512,896]{1,0:T(8,128)(2,1)}) custom-call(s32[1]{0:T(128)} %bitcast.5.core_ref, bf16[4,2,2048,256]{3,2,1,0:T(8,128)(2,1)} %cache_hbm.4, bf16[512,3584]{1,0:T(8,128)(2,1)} %weight_hbm.3), custom_call_target="tpu_custom_call" | custom-call | bytes 6291456 | tf_op jit(solution)/shard_map/pallas_call | solution.py:434
  11.9 4.8 %all-to-all-done = bf16[8,16,640]{2,1,0:T(8,128)(2,1)S(1)} async-done(((bf16[8,16,640]{2,1,0:T(8,128)(2,1)}), bf16[8,16,640]{2,1,0:T(8,128)(2,1)S(1)}, u32[]{:S(2)}, u32[]{:S(2)}) %all-to-all-start) | async-done | bytes 163872 | tf_op jit(solution)/shard_map/all_to_all | solution.py:411
  16.7 4.4 %shard_map.102.after_hbm = bf16[128,640]{1,0:T(8,128)(2,1)} custom-call(s32[4]{0:T(128)} %length_hbm.1, bf16[128,640]{1,0:T(8,128)(2,1)S(1)} %bitcast.10, bf16[3,2048,256]{2,1,0:T(8,128)(2,1)S(1)} %get-tuple-element.17.early_ref, bf16[4,2,2048,256]{3,2,1,0:T(8,128)(2,1)} %cache_hbm.4), custom_call_target="tpu_custom_call" | custom-call | tf_op jit(solution)/shard_map/pallas_call | solution.py:452
  21.0 3.4 %all-to-all-start.1 = ((bf16[8,16,640]{2,1,0:T(8,128)(2,1)}), bf16[8,16,640]{2,1,0:T(8,128)(2,1)S(1)}, u32[]{:S(2)}, u32[]{:S(2)}) async-start(bf16[8,16,640]{2,1,0:T(8,128)(2,1)} %bitcast.6), calls=%async_computation.1 | async-start | bytes 327680 | tf_op jit(solution)/shard_map/all_to_all | solution.py:411
  24.4 4.5 %shard_map.103 = (bf16[64,128]{1,0:T(8,128)(2,1)S(1)}, f32[64,512]{1,0:T(8,128)S(1)}, f32[64,256]{1,0:T(8,128)S(1)}, bf16[3,512,896]{2,1,0:T(8,128)(2,1)S(1)}) custom-call(s32[1,64]{1,0:T(1,128)} %bitcast.12, s32[1,64]{1,0:T(1,128)} %bitcast.14, bf16[64,512]{1,0:T(8,128)(2,1)} %queries_hbm.3, bf16[64,2,64,256]{3,2,1,0:T(8,128)(2,1)} %cache_hbm.5, ...), custom_call_target="tpu_custom_call" | custom-call | flops 134217728 | bytes 7864320 | tf_op jit(solution)/shard_map/pallas_call | solution.py:477
  29.0 3.0 %all-to-all-done.1 = bf16[8,16,640]{2,1,0:T(8,128)(2,1)S(1)} async-done(((bf16[8,16,640]{2,1,0:T(8,128)(2,1)}), bf16[8,16,640]{2,1,0:T(8,128)(2,1)S(1)}, u32[]{:S(2)}, u32[]{:S(2)}) %all-to-all-start.1) | async-done | bytes 163872 | tf_op jit(solution)/shard_map/all_to_all | solution.py:411
  31.9 0.0 copy-start
  31.9 0.0 copy-start.2
  31.9 0.0 copy-start.1
  31.9 0.7 %shard_map.104 = (bf16[64,512]{1,0:T(8,128)(2,1)S(1)}, bf16[64,1792]{1,0:T(8,128)(2,1)S(1)}) custom-call(bf16[128,640]{1,0:T(8,128)(2,1)S(1)} %bitcast.9, bf16[64,128]{1,0:T(8,128)(2,1)S(1)} %get-tuple-element.18.back_ref, f32[64,512]{1,0:T(8,128)S(1)} %get-tuple-element.19.num_ref, f32[64,256]{1,0:T(8,128)S(1)} %get-tuple-element.20.den_ref, ...), custom_call_target="tpu_custom_call" | custom-call | tf_op jit(solution)/shard_map/pallas_call | solution.py:365
  32.7 0.1 collective-permute-start
  32.7 0.4 copy-done
  33.1 0.4 shard_map.105.own_ref
  33.5 0.7 %collective-permute-done.got_ref = bf16[64,1792]{1,0:T(8,128)(2,1)S(1)} collective-permute-done((bf16[64,1792]{1,0:T(8,128)(2,1)S(1)}, bf16[64,1792]{1,0:T(8,128)(2,1)S(1)}, u32[]{:S(2)}, u32[]{:S(2)}) %collective-permute-start) | collective-permute-done | bytes 229408 | tf_op jit(solution)/shard_map/ppermute | solution.py:415
  34.2 0.1 shard_map.106
  34.3 1.6 %collective-permute-start.1 = (bf16[64,1792]{1,0:T(8,128)(2,1)S(1)}, bf16[64,1792]{1,0:T(8,128)(2,1)S(1)}, u32[]{:S(2)}, u32[]{:S(2)}) collective-permute-start(bf16[64,1792]{1,0:T(8,128)(2,1)S(1)} %get-tuple-element.26), channel_id=1, source_target_pairs={{0,2},{1,3},{2,0},{3,1},{4,6},{5,7},{6,4},{7,5},{8,10},{9,11},{10,... | collective-permute-start | bytes 688136 | tf_op jit(solution)/shard_map/ppermute | solution.py:415
  35.9 6.1 %collective-permute-done.1.got_ref = bf16[64,1792]{1,0:T(8,128)(2,1)S(1)} collective-permute-done((bf16[64,1792]{1,0:T(8,128)(2,1)S(1)}, bf16[64,1792]{1,0:T(8,128)(2,1)S(1)}, u32[]{:S(2)}, u32[]{:S(2)}) %collective-permute-start.1) | collective-permute-done | bytes 229408 | tf_op jit(solution)/shard_map/ppermute | solution.py:415
  42.0 0.1 shard_map.107
  42.1 0.1 collective-permute-start.2
  42.2 0.0 copy-done.2
  42.2 1.2 %collective-permute-done.2.got_ref = f32[64,128]{1,0:T(8,128)S(1)} collective-permute-done((f32[64,128]{1,0:T(8,128)S(1)}, f32[64,128]{1,0:T(8,128)S(1)}, u32[]{:S(2)}, u32[]{:S(2)}) %collective-permute-start.2) | collective-permute-done | bytes 32800 | tf_op jit(solution)/shard_map/ppermute | solution.py:415
  43.4 0.0 copy-done.1
  43.4 0.8 %shard_map.108 = bf16[64,896]{1,0:T(8,128)(2,1)} custom-call(f32[64,896]{1,0:T(8,128)S(1)} %get-tuple-element.27.mine_ref, f32[64,128]{1,0:T(8,128)S(1)} %get-tuple-element.28.square_ref, f32[64,128]{1,0:T(8,128)S(1)} %collective-permute-done.2.got_ref, f32[1,896]{1,0:T(1,128)S(1)} %reshape.39.gain_ref, bf16[64,896]{1,0:T(8,128)(2,1)S(1)} %copy-done.1), custom_call_target="tpu_custom_call" | custom-call | tf_op jit(solution)/shard_map/pallas_call | solution.py:365
  (1 shorter events, 0.0 us)
Async XLA Ops:
  1.8 14.8 %all-to-all-start = ((bf16[8,16,640]{2,1,0:T(8,128)(2,1)}), bf16[8,16,640]{2,1,0:T(8,128)(2,1)S(1)}, u32[]{:S(2)}, u32[]{:S(2)}) async-start(bf16[8,16,640]{2,1,0:T(8,128)(2,1)} %bitcast.3), calls=%async_computation | async-start | bytes 327680 | tf_op jit(solution)/shard_map/all_to_all | solution.py:411
  21.0 10.9 %all-to-all-start.1 = ((bf16[8,16,640]{2,1,0:T(8,128)(2,1)}), bf16[8,16,640]{2,1,0:T(8,128)(2,1)S(1)}, u32[]{:S(2)}, u32[]{:S(2)}) async-start(bf16[8,16,640]{2,1,0:T(8,128)(2,1)} %bitcast.6), calls=%async_computation.1 | async-start | bytes 327680 | tf_op jit(solution)/shard_map/all_to_all | solution.py:411
  31.9 1.2 %copy-start = (bf16[512,896]{1,0:T(8,128)(2,1)S(1)}, bf16[512,896]{1,0:T(8,128)(2,1)}, u32[]{:S(2)}) copy-start(bf16[512,896]{1,0:T(8,128)(2,1)} %get-tuple-element.23.last_ref) | copy-start | bytes 2752516
  31.9 10.2 %copy-start.2 = (f32[896]{0:T(1024)S(1)}, f32[896]{0:T(1024)}, u32[]{:S(2)}) copy-start(f32[896]{0:T(1024)} %param.19) | copy-start | bytes 10756
  31.9 11.4 %copy-start.1 = (bf16[64,896]{1,0:T(8,128)(2,1)S(1)}, bf16[64,896]{1,0:T(8,128)(2,1)}, u32[]{:S(2)}) copy-start(bf16[64,896]{1,0:T(8,128)(2,1)} %hidden_ref.1) | copy-start | bytes 344068
  32.7 1.6 %collective-permute-start = (bf16[64,1792]{1,0:T(8,128)(2,1)S(1)}, bf16[64,1792]{1,0:T(8,128)(2,1)S(1)}, u32[]{:S(2)}, u32[]{:S(2)}) collective-permute-start(bf16[64,1792]{1,0:T(8,128)(2,1)S(1)} %get-tuple-element.24), channel_id=1, source_target_pairs={{0,1},{1,0},{2,3},{3,2},{4,5},{5,4},{6,7},{7,6},{8,9},{9,8},{10,11... | collective-permute-start | bytes 688136 | tf_op jit(solution)/shard_map/ppermute | solution.py:415
  34.3 7.7 %collective-permute-start.1 = (bf16[64,1792]{1,0:T(8,128)(2,1)S(1)}, bf16[64,1792]{1,0:T(8,128)(2,1)S(1)}, u32[]{:S(2)}, u32[]{:S(2)}) collective-permute-start(bf16[64,1792]{1,0:T(8,128)(2,1)S(1)} %get-tuple-element.26), channel_id=1, source_target_pairs={{0,2},{1,3},{2,0},{3,1},{4,6},{5,7},{6,4},{7,5},{8,10},{9,11},{10,... | collective-permute-start | bytes 688136 | tf_op jit(solution)/shard_map/ppermute | solution.py:415
  42.1 1.3 %collective-permute-start.2 = (f32[64,128]{1,0:T(8,128)S(1)}, f32[64,128]{1,0:T(8,128)S(1)}, u32[]{:S(2)}, u32[]{:S(2)}) collective-permute-start(f32[64,128]{1,0:T(8,128)S(1)} %get-tuple-element.28.square_ref), channel_id=1, source_target_pairs={{0,1},{1,0},{2,3},{3,2},{4,5},{5,4},{6,7},{7,6},{8,9},{9,8},{10,11... | collective-permute-start | bytes 98312 | tf_op jit(solution)/shard_map/ppermute | solution.py:415

commit v4 on v3

--- a/solution.py
+++ b/solution.py
@@ -36,16 +36,25 @@
     return jnp.where(alive, jnp.exp2(weight_scale * jnp.tanh(scores * score_scale)), 0.0)
 
 
-def owners(owner_ref):
+def order_of(replicas):
+    return {8: (4, 5, 6, 1, 0, 7, 2, 3)}.get(replicas, tuple(range(replicas)))
+
+
+def owners(owner_ref, order):
     requests = owner_ref.shape[1]
     rows, cols = iota((requests, requests), 0), iota((requests, requests), 1)
-    by_col = jnp.broadcast_to(owner_ref[...], (requests, requests)).astype(f32)
+    owner = owner_ref[...]
+    place = owner
+    for i, replica in enumerate(order):
+        if i != replica:
+            place = jnp.where(owner == replica, i, place)
+    by_col = jnp.broadcast_to(place, (requests, requests)).astype(f32)
     by_row = jnp.sum(jnp.where(rows == cols, by_col, 0.0), axis=1, keepdims=True)
     return by_row, by_col, rows, cols
 
 
 def route_kernel(
-    capacity, owner_hbm, group_hbm, queries_hbm, out_ref, owner_ref, group_ref, queries_ref, sems
+    capacity, order, owner_hbm, group_hbm, queries_hbm, out_ref, owner_ref, group_ref, queries_ref, sems
 ):
     pairs = ((owner_hbm, owner_ref), (group_hbm, group_ref), (queries_hbm, queries_ref))
     copies = [pltpu.make_async_copy(a, b, sems.at[i]) for i, (a, b) in enumerate(pairs)]
@@ -55,7 +64,7 @@
         copy.wait()
     requests, width = queries_ref.shape
     slots = out_ref.shape[0]
-    by_row, by_col, rows, cols = owners(owner_ref)
+    by_row, by_col, rows, cols = owners(owner_ref, order)
     earlier = jnp.where((by_row == by_col) & (rows < cols), 1.0, 0.0)
     position = (by_col[:1] * capacity + jnp.sum(earlier, axis=0, keepdims=True)).astype(jnp.int32)
     matches = iota((slots, requests), 0) == position
@@ -69,6 +78,7 @@
 
 def suffix_kernel(
     capacity,
+    order,
     block,
     owner_hbm,
     length_hbm,
@@ -113,7 +123,7 @@
     for copy in copies:
         copy.wait()
 
-    by_row, by_col, rows, cols = owners(owner_ref)
+    by_row, by_col, rows, cols = owners(owner_ref, order)
     earlier = jnp.where((by_row == by_col) & (cols < rows), 1.0, 0.0)
     rank = jnp.sum(earlier, axis=1, keepdims=True)
     position = (by_row * capacity + rank).astype(jnp.int32)
@@ -402,13 +412,16 @@
     features = output_weight.shape[1]
     quarter = features // ranks
     heads = width // HD
+    order = order_of(replicas)
     index = lax.axis_index("tensor")
     core = (index % 2).reshape(1)
     row = (index // 2).reshape(1)
 
     def exchange(x):
         blocks = x.reshape(replicas, capacity, width + EXTRA)
-        blocks = lax.all_to_all(blocks, "replica", split_axis=0, concat_axis=0, tiled=True)
+        blocks = lax.all_to_all(
+            blocks, "replica", split_axis=0, concat_axis=0, axis_index_groups=[order], tiled=True
+        )
         return blocks.reshape(slots, width + EXTRA)
 
     def permute(x, bit):
@@ -416,7 +429,7 @@
 
     owner_row = owner_replica.reshape(1, requests)
     sent = pl.pallas_call(
-        functools.partial(route_kernel, capacity),
+        functools.partial(route_kernel, capacity, order),
         out_shape=pltpu.VMEM((slots, width + EXTRA), bf16),
         in_specs=[HBM_SPEC] * 3,
         out_specs=VMEM_SPEC,
@@ -475,7 +488,7 @@
 
     block = math.gcd(16, requests)
     back, own_num, own_den, weight = pl.pallas_call(
-        functools.partial(suffix_kernel, capacity, block),
+        functools.partial(suffix_kernel, capacity, order, block),
         out_shape=[
             shape((requests, slots), bf16),
             shape((requests, width), f32),

time: 44.5 us -> 41.5 us (0.933)
  waiting for transfers between devices: 15.7 us -> 9.58 us
  starting transfers between devices: 12.4 us -> 15.5 us
    all_to_all x2, waiting for transfers between devices: 7.75 us -> 1.57 us  [exchange(): lax.all_to_all(blocks, 'replica', split_axis=0, concat_axis=0, axis_index...]
    all_to_all x2, starting transfers between devices: 10.7 us -> 13.8 us  [exchange(): lax.all_to_all(blocks, 'replica', split_axis=0, concat_axis=0, axis_index...]
  transfers between devices with their start and end apart: 5 -> 5, of which waited for: 5 -> 4; matrix products, arithmetic and copies ran while one was open for 0% -> 0% of each run, Pallas kernels for 18% -> 19%
where the time goes in v4:
time: 41.5 us; the launch traced here: 41.1 us
  Pallas kernels  15.6 us (38%)
  starting transfers between devices  15.5 us (37%)
  waiting for transfers between devices  9.58 us (23%)
    all_to_all x2, starting transfers between devices, exchange(): lax.all_to_all(blocks, 'replica', split_axis=0, concat_axis=0, axis_index...  13.8 us
    ppermute x3, waiting for transfers between devices, permute(): return lax.ppermute(x, 'tensor', [(i, i ^ bit) for i in range(ranks)])  8 us
    pallas_call x1, Pallas kernels, shards(): pl.pallas_call(functools.partial(suffix_kernel, capacity, order, block),...  4.52 us
    pallas_call x1, Pallas kernels, shards(): pl.pallas_call(functools.partial(prompt_kernel, chunk, fit), out_shape=pl...  4.36 us
    pallas_call x1, Pallas kernels, shards(): pl.pallas_call(prefetch_kernel, out_shape=[pltpu.VMEM((early, size, HD),...  2.77 us
    pallas_call x5, Pallas kernels, call(): pl.pallas_call(kernel, out_shape=outs, in_specs=specs, out_specs=jax.tree...  2.08 us
    pallas_call x1, Pallas kernels, shards(): pl.pallas_call(functools.partial(route_kernel, capacity, order), out_shap...  1.83 us
    ppermute x3, starting transfers between devices, permute(): return lax.ppermute(x, 'tensor', [(i, i ^ bit) for i in range(ranks)])  1.73 us
  transfers between devices with their start and end apart: 5, of which 4 were waited for; matrix products, arithmetic and copies ran while one was open for 0% of the time, Pallas kernels for 19%

profile of v4, /device:TPU:0, one launch (start us, length us, event | category | flops | bytes accessed | tf_op | source)
XLA Modules:
  0.0 41.1 jit_solution(4898001174791751579)
XLA Ops:
  0.0 1.8 %shard_map.100 = bf16[128,640]{1,0:T(8,128)(2,1)} custom-call(s32[1,64]{1,0:T(1,128)} %bitcast.11, s32[1,64]{1,0:T(1,128)} %bitcast.13, bf16[64,512]{1,0:T(8,128)(2,1)} %queries_hbm.3), custom_call_target="tpu_custom_call" | custom-call | tf_op jit(solution)/shard_map/pallas_call | solution.py:431
  1.8 7.8 %all-to-all-start = ((bf16[8,16,640]{2,1,0:T(8,128)(2,1)}), bf16[8,16,640]{2,1,0:T(8,128)(2,1)S(1)}, u32[]{:S(2)}, u32[]{:S(2)}) async-start(bf16[8,16,640]{2,1,0:T(8,128)(2,1)} %bitcast.3), calls=%async_computation | async-start | bytes 327680 | tf_op jit(solution)/shard_map/all_to_all | solution.py:422
  9.7 2.8 %shard_map.101 = (bf16[3,2048,256]{2,1,0:T(8,128)(2,1)S(1)}, bf16[512,896]{1,0:T(8,128)(2,1)}) custom-call(s32[1]{0:T(128)} %bitcast.5.core_ref, bf16[4,2,2048,256]{3,2,1,0:T(8,128)(2,1)} %cache_hbm.4, bf16[512,3584]{1,0:T(8,128)(2,1)} %weight_hbm.3), custom_call_target="tpu_custom_call" | custom-call | bytes 6291456 | tf_op jit(solution)/shard_map/pallas_call | solution.py:447
  12.4 1.6 %all-to-all-done = bf16[8,16,640]{2,1,0:T(8,128)(2,1)S(1)} async-done(((bf16[8,16,640]{2,1,0:T(8,128)(2,1)}), bf16[8,16,640]{2,1,0:T(8,128)(2,1)S(1)}, u32[]{:S(2)}, u32[]{:S(2)}) %all-to-all-start) | async-done | bytes 163872 | tf_op jit(solution)/shard_map/all_to_all | solution.py:422
  14.0 4.4 %shard_map.102.after_hbm = bf16[128,640]{1,0:T(8,128)(2,1)} custom-call(s32[4]{0:T(128)} %length_hbm.1, bf16[128,640]{1,0:T(8,128)(2,1)S(1)} %bitcast.10, bf16[3,2048,256]{2,1,0:T(8,128)(2,1)S(1)} %get-tuple-element.17.early_ref, bf16[4,2,2048,256]{3,2,1,0:T(8,128)(2,1)} %cache_hbm.4), custom_call_target="tpu_custom_call" | custom-call | tf_op jit(solution)/shard_map/pallas_call | solution.py:465
  18.4 6.0 %all-to-all-start.1 = ((bf16[8,16,640]{2,1,0:T(8,128)(2,1)}), bf16[8,16,640]{2,1,0:T(8,128)(2,1)S(1)}, u32[]{:S(2)}, u32[]{:S(2)}) async-start(bf16[8,16,640]{2,1,0:T(8,128)(2,1)} %bitcast.6), calls=%async_computation.1 | async-start | bytes 327680 | tf_op jit(solution)/shard_map/all_to_all | solution.py:422
  24.4 4.5 %shard_map.103 = (bf16[64,128]{1,0:T(8,128)(2,1)S(1)}, f32[64,512]{1,0:T(8,128)S(1)}, f32[64,256]{1,0:T(8,128)S(1)}, bf16[3,512,896]{2,1,0:T(8,128)(2,1)S(1)}) custom-call(s32[1,64]{1,0:T(1,128)} %bitcast.12, s32[1,64]{1,0:T(1,128)} %bitcast.14, bf16[64,512]{1,0:T(8,128)(2,1)} %queries_hbm.3, bf16[64,2,64,256]{3,2,1,0:T(8,128)(2,1)} %cache_hbm.5, ...), custom_call_target="tpu_custom_call" | custom-call | flops 134217728 | bytes 7864320 | tf_op jit(solution)/shard_map/pallas_call | solution.py:490
  28.9 0.0 all-to-all-done.1
  28.9 0.0 copy-start
  28.9 0.0 copy-start.2
  28.9 0.0 copy-start.1
  28.9 0.7 %shard_map.104 = (bf16[64,512]{1,0:T(8,128)(2,1)S(1)}, bf16[64,1792]{1,0:T(8,128)(2,1)S(1)}) custom-call(bf16[128,640]{1,0:T(8,128)(2,1)S(1)} %bitcast.9, bf16[64,128]{1,0:T(8,128)(2,1)S(1)} %get-tuple-element.18.back_ref, f32[64,512]{1,0:T(8,128)S(1)} %get-tuple-element.19.num_ref, f32[64,256]{1,0:T(8,128)S(1)} %get-tuple-element.20.den_ref, ...), custom_call_target="tpu_custom_call" | custom-call | tf_op jit(solution)/shard_map/pallas_call | solution.py:375
  29.7 0.1 collective-permute-start
  29.7 0.3 copy-done
  30.1 0.4 %shard_map.105.own_ref = f32[64,1792]{1,0:T(8,128)S(1)} custom-call(bf16[64,512]{1,0:T(8,128)(2,1)S(1)} %get-tuple-element.22.att_ref, bf16[3,512,896]{2,1,0:T(8,128)(2,1)S(1)} %get-tuple-element.21.weight_ref, bf16[512,896]{1,0:T(8,128)(2,1)S(1)} %copy-done), custom_call_target="tpu_custom_call" | custom-call | tf_op jit(solution)/shard_map/pallas_call | solution.py:375
  30.5 0.7 %collective-permute-done.got_ref = bf16[64,1792]{1,0:T(8,128)(2,1)S(1)} collective-permute-done((bf16[64,1792]{1,0:T(8,128)(2,1)S(1)}, bf16[64,1792]{1,0:T(8,128)(2,1)S(1)}, u32[]{:S(2)}, u32[]{:S(2)}) %collective-permute-start) | collective-permute-done | bytes 229408 | tf_op jit(solution)/shard_map/ppermute | solution.py:428
  31.2 0.1 shard_map.106
  31.3 1.6 %collective-permute-start.1 = (bf16[64,1792]{1,0:T(8,128)(2,1)S(1)}, bf16[64,1792]{1,0:T(8,128)(2,1)S(1)}, u32[]{:S(2)}, u32[]{:S(2)}) collective-permute-start(bf16[64,1792]{1,0:T(8,128)(2,1)S(1)} %get-tuple-element.26), channel_id=1, source_target_pairs={{0,2},{1,3},{2,0},{3,1},{4,6},{5,7},{6,4},{7,5},{8,10},{9,11},{10,... | collective-permute-start | bytes 688136 | tf_op jit(solution)/shard_map/ppermute | solution.py:428
  32.9 6.1 %collective-permute-done.1.got_ref = bf16[64,1792]{1,0:T(8,128)(2,1)S(1)} collective-permute-done((bf16[64,1792]{1,0:T(8,128)(2,1)S(1)}, bf16[64,1792]{1,0:T(8,128)(2,1)S(1)}, u32[]{:S(2)}, u32[]{:S(2)}) %collective-permute-start.1) | collective-permute-done | bytes 229408 | tf_op jit(solution)/shard_map/ppermute | solution.py:428
  39.0 0.1 shard_map.107
  39.1 0.1 collective-permute-start.2
  39.2 0.0 copy-done.2
  39.2 1.2 %collective-permute-done.2.got_ref = f32[64,128]{1,0:T(8,128)S(1)} collective-permute-done((f32[64,128]{1,0:T(8,128)S(1)}, f32[64,128]{1,0:T(8,128)S(1)}, u32[]{:S(2)}, u32[]{:S(2)}) %collective-permute-start.2) | collective-permute-done | bytes 32800 | tf_op jit(solution)/shard_map/ppermute | solution.py:428
  40.4 0.0 copy-done.1
  40.4 0.8 %shard_map.108 = bf16[64,896]{1,0:T(8,128)(2,1)} custom-call(f32[64,896]{1,0:T(8,128)S(1)} %get-tuple-element.27.mine_ref, f32[64,128]{1,0:T(8,128)S(1)} %get-tuple-element.28.square_ref, f32[64,128]{1,0:T(8,128)S(1)} %collective-permute-done.2.got_ref, f32[1,896]{1,0:T(1,128)S(1)} %reshape.39.gain_ref, bf16[64,896]{1,0:T(8,128)(2,1)S(1)} %copy-done.1), custom_call_target="tpu_custom_call" | custom-call | tf_op jit(solution)/shard_map/pallas_call | solution.py:375
  (1 shorter events, 0.0 us)
Async XLA Ops:
  1.8 12.2 %all-to-all-start = ((bf16[8,16,640]{2,1,0:T(8,128)(2,1)}), bf16[8,16,640]{2,1,0:T(8,128)(2,1)S(1)}, u32[]{:S(2)}, u32[]{:S(2)}) async-start(bf16[8,16,640]{2,1,0:T(8,128)(2,1)} %bitcast.3), calls=%async_computation | async-start | bytes 327680 | tf_op jit(solution)/shard_map/all_to_all | solution.py:422
  18.4 10.5 %all-to-all-start.1 = ((bf16[8,16,640]{2,1,0:T(8,128)(2,1)}), bf16[8,16,640]{2,1,0:T(8,128)(2,1)S(1)}, u32[]{:S(2)}, u32[]{:S(2)}) async-start(bf16[8,16,640]{2,1,0:T(8,128)(2,1)} %bitcast.6), calls=%async_computation.1 | async-start | bytes 327680 | tf_op jit(solution)/shard_map/all_to_all | solution.py:422
  28.9 1.2 %copy-start = (bf16[512,896]{1,0:T(8,128)(2,1)S(1)}, bf16[512,896]{1,0:T(8,128)(2,1)}, u32[]{:S(2)}) copy-start(bf16[512,896]{1,0:T(8,128)(2,1)} %get-tuple-element.23.last_ref) | copy-start | bytes 2752516
  28.9 10.3 %copy-start.2 = (f32[896]{0:T(1024)S(1)}, f32[896]{0:T(1024)}, u32[]{:S(2)}) copy-start(f32[896]{0:T(1024)} %param.19) | copy-start | bytes 10756
  28.9 11.4 %copy-start.1 = (bf16[64,896]{1,0:T(8,128)(2,1)S(1)}, bf16[64,896]{1,0:T(8,128)(2,1)}, u32[]{:S(2)}) copy-start(bf16[64,896]{1,0:T(8,128)(2,1)} %hidden_ref.1) | copy-start | bytes 344068
  29.7 1.6 %collective-permute-start = (bf16[64,1792]{1,0:T(8,128)(2,1)S(1)}, bf16[64,1792]{1,0:T(8,128)(2,1)S(1)}, u32[]{:S(2)}, u32[]{:S(2)}) collective-permute-start(bf16[64,1792]{1,0:T(8,128)(2,1)S(1)} %get-tuple-element.24), channel_id=1, source_target_pairs={{0,1},{1,0},{2,3},{3,2},{4,5},{5,4},{6,7},{7,6},{8,9},{9,8},{10,11... | collective-permute-start | bytes 688136 | tf_op jit(solution)/shard_map/ppermute | solution.py:428
  31.3 7.7 %collective-permute-start.1 = (bf16[64,1792]{1,0:T(8,128)(2,1)S(1)}, bf16[64,1792]{1,0:T(8,128)(2,1)S(1)}, u32[]{:S(2)}, u32[]{:S(2)}) collective-permute-start(bf16[64,1792]{1,0:T(8,128)(2,1)S(1)} %get-tuple-element.26), channel_id=1, source_target_pairs={{0,2},{1,3},{2,0},{3,1},{4,6},{5,7},{6,4},{7,5},{8,10},{9,11},{10,... | collective-permute-start | bytes 688136 | tf_op jit(solution)/shard_map/ppermute | solution.py:428
  39.1 1.3 %collective-permute-start.2 = (f32[64,128]{1,0:T(8,128)S(1)}, f32[64,128]{1,0:T(8,128)S(1)}, u32[]{:S(2)}, u32[]{:S(2)}) collective-permute-start(f32[64,128]{1,0:T(8,128)S(1)} %get-tuple-element.28.square_ref), channel_id=1, source_target_pairs={{0,1},{1,0},{2,3},{3,2},{4,5},{5,4},{6,7},{7,6},{8,9},{9,8},{10,11... | collective-permute-start | bytes 98312 | tf_op jit(solution)/shard_map/ppermute | solution.py:428

commit v5 on v4

--- a/solution.py
+++ b/solution.py
@@ -76,74 +76,21 @@
     out_ref[:, width:] = jnp.broadcast_to(mark, (slots, EXTRA)).astype(bf16)
 
 
-def suffix_kernel(
-    capacity,
-    order,
-    block,
-    owner_hbm,
-    length_hbm,
-    queries_hbm,
-    cache_hbm,
-    core_ref,
-    weight_hbm,
-    after_hbm,
-    back_ref,
-    num_ref,
-    den_ref,
-    weight_ref,
-    owner_ref,
-    length_ref,
-    queries_ref,
-    cache_ref,
-    sems,
-    cache_sems,
-    weight_sems,
-):
-    requests, slots = back_ref.shape
-    window = cache_ref.shape[2]
+def attend_own(block, first, live, queries_ref, cache_ref, num_ref, den_ref):
+    requests, _, window, _ = cache_ref.shape
     heads = queries_ref.shape[1] // HD
-    steps = requests // block
-    pairs = ((owner_hbm, owner_ref), (length_hbm, length_ref), (queries_hbm, queries_ref))
-    copies = [pltpu.make_async_copy(a, b, sems.at[i]) for i, (a, b) in enumerate(pairs)]
-    parts = []
-    for i in range(steps):
-        span = pl.ds(i * block, block)
-        parts.append(
-            pltpu.make_async_copy(cache_hbm.at[span], cache_ref.at[span], cache_sems.at[i])
-        )
-    quarter = weight_ref.shape[2]
-    weight_copies = []
-    for i, q in enumerate((1 - core_ref[0], 3 - core_ref[0], core_ref[0])):
-        cols = pl.ds(pl.multiple_of(q * quarter, 128), quarter)
-        weight_copies.append(
-            pltpu.make_async_copy(weight_hbm.at[:, cols], weight_ref.at[i], weight_sems.at[i])
-        )
-    for copy in copies + parts + weight_copies:
-        copy.start()
-    for copy in copies:
-        copy.wait()
-
-    by_row, by_col, rows, cols = owners(owner_ref, order)
-    earlier = jnp.where((by_row == by_col) & (cols < rows), 1.0, 0.0)
-    rank = jnp.sum(earlier, axis=1, keepdims=True)
-    position = (by_row * capacity + rank).astype(jnp.int32)
-    back_ref[...] = jnp.where(iota((requests, slots), 1) == position, 1.0, 0.0).astype(bf16)
-    live = jnp.sum(
-        jnp.where(rows == cols, length_ref[...].astype(f32), 0.0), axis=1, keepdims=True
-    ).astype(jnp.int32)
-
     at = iota((block, block * window), 1)
-    first = iota((block, block * window), 0) * window
-    for i in range(steps):
+    start = iota((block, block * window), 0) * window
+    for i in range(requests // block):
         mine = slice(i * block, (i + 1) * block)
-        parts[i].wait()
-        stacked = heads_below(queries_ref[mine, :], heads)
+        there = slice(first + i * block, first + (i + 1) * block)
+        stacked = heads_below(queries_ref[there, :], heads)
         keys = cache_ref[mine, 0].reshape(block * window, HD)
         values = cache_ref[mine, 1].reshape(block * window, HD)
         scores = lax.dot_general(
             stacked, keys, (((1,), (1,)), ((), ())), preferred_element_type=f32
         )
-        alive = (at >= first) & (at < first + live[mine])
+        alive = (at >= start) & (at < start + live[there])
         weights = weights_of(scores, jnp.concatenate([alive] * heads, axis=0))
         numerator = jnp.dot(weights.astype(bf16), values, preferred_element_type=f32)
         denominator = jnp.sum(weights, axis=1, keepdims=True)
@@ -153,26 +100,112 @@
             den_ref[mine, h * 128 : (h + 1) * 128] = jnp.broadcast_to(
                 denominator[own], (block, 128)
             )
-    for copy in weight_copies:
-        copy.wait()
-
-
-def prefetch_kernel(core_ref, cache_hbm, weight_hbm, early_ref, last_hbm, staged, sems, last_sem):
-    parts = parts_of(cache_hbm.shape[0])
+
+
+def down(row, rows, cols):
+    return jnp.sum(jnp.where(rows == cols, row.astype(f32), 0.0), axis=1, keepdims=True)
+
+
+def early_kernel(
+    capacity,
+    order,
+    block,
+    core_ref,
+    owner_hbm,
+    length_hbm,
+    queries_hbm,
+    cache_hbm,
+    prompt_hbm,
+    weight_hbm,
+    back_ref,
+    num_ref,
+    den_ref,
+    early_ref,
+    last_hbm,
+    owner_ref,
+    length_ref,
+    queries_ref,
+    cache_ref,
+    staged,
+    sems,
+    early_sems,
+    last_sem,
+):
+    requests, slots = back_ref.shape
+    parts = parts_of(prompt_hbm.shape[0])
+    pairs = (
+        (owner_hbm, owner_ref),
+        (length_hbm, length_ref),
+        (queries_hbm, queries_ref),
+        (cache_hbm.at[pl.ds(0, cache_ref.shape[0])], cache_ref),
+    )
+    copies = [pltpu.make_async_copy(a, b, sems.at[i]) for i, (a, b) in enumerate(pairs)]
     quarter = last_hbm.shape[1]
     cols = pl.ds(pl.multiple_of((core_ref[0] + 2) * quarter, 128), quarter)
     stage = pltpu.make_async_copy(weight_hbm.at[:, cols], staged, last_sem)
     unstage = pltpu.make_async_copy(staged, last_hbm, last_sem)
-    stage.start()
-    copies = [
-        pltpu.make_async_copy(cache_hbm.at[parts[i]], early_ref.at[i], sems.at[i])
+    prompts = [
+        pltpu.make_async_copy(prompt_hbm.at[parts[i]], early_ref.at[i], early_sems.at[i])
         for i in range(early_ref.shape[0])
     ]
+    for copy in copies + [stage] + prompts:
+        copy.start()
     for copy in copies:
-        copy.start()
+        copy.wait()
     stage.wait()
     unstage.start()
-    for copy in copies + [unstage]:
+    by_row, by_col, rows, cols = owners(owner_ref, order)
+    earlier = jnp.where((by_row == by_col) & (cols < rows), 1.0, 0.0)
+    rank = jnp.sum(earlier, axis=1, keepdims=True)
+    position = (by_row * capacity + rank).astype(jnp.int32)
+    back_ref[...] = jnp.where(iota((requests, slots), 1) == position, 1.0, 0.0).astype(bf16)
+    live = down(length_ref[...], rows, cols).astype(jnp.int32)
+    attend_own(block, 0, live, queries_ref, cache_ref, num_ref, den_ref)
+    for copy in prompts + [unstage]:
+        copy.wait()
+
+
+def late_kernel(
+    block,
+    core_ref,
+    length_hbm,
+    queries_hbm,
+    cache_hbm,
+    weight_hbm,
+    after_hbm,
+    num_ref,
+    den_ref,
+    weight_ref,
+    length_ref,
+    queries_ref,
+    cache_ref,
+    sems,
+    weight_sems,
+):
+    requests = queries_ref.shape[0]
+    half = cache_ref.shape[0]
+    first = requests - half
+    pairs = (
+        (length_hbm, length_ref),
+        (queries_hbm, queries_ref),
+        (cache_hbm.at[pl.ds(first, half)], cache_ref),
+    )
+    copies = [pltpu.make_async_copy(a, b, sems.at[i]) for i, (a, b) in enumerate(pairs)]
+    quarter = weight_ref.shape[2]
+    weight_copies = []
+    for i, q in enumerate((1 - core_ref[0], 3 - core_ref[0], core_ref[0])):
+        cols = pl.ds(pl.multiple_of(q * quarter, 128), quarter)
+        weight_copies.append(
+            pltpu.make_async_copy(weight_hbm.at[:, cols], weight_ref.at[i], weight_sems.at[i])
+        )
+    for copy in copies + weight_copies:
+        copy.start()
+    for copy in copies:
+        copy.wait()
+    rows, cols = iota((requests, requests), 0), iota((requests, requests), 1)
+    live = down(length_ref[...], rows, cols).astype(jnp.int32)
+    attend_own(block, first, live, queries_ref, cache_ref, num_ref, den_ref)
+    for copy in weight_copies:
         copy.wait()
 
 
@@ -318,17 +351,18 @@
 
 
 def combine_kernel(
-    returned_ref, back_ref, num_ref, den_ref, weight_ref, att_ref, give_ref
+    returned_ref, back_ref, num_a, den_a, num_b, den_b, weight_ref, att_ref, give_ref
 ):
     quarter = weight_ref.shape[2]
-    width = num_ref.shape[1]
+    width = num_a.shape[1]
     heads = width // HD
     mine = jnp.dot(back_ref[...], returned_ref[...], preferred_element_type=f32)
     for h in range(heads):
         cols = slice(h * HD, (h + 1) * HD)
-        numerator = mine[:, cols] + num_ref[:, cols]
+        numerator = mine[:, cols] + jnp.concatenate([num_a[:, cols], num_b[:, cols]], axis=0)
         at = width + 3 * h
-        denominator = den_ref[:, h * 128 : h * 128 + 1] + (
+        lane = slice(h * 128, h * 128 + 1)
+        denominator = jnp.concatenate([den_a[:, lane], den_b[:, lane]], axis=0) + (
             mine[:, at : at + 1] + mine[:, at + 1 : at + 2] + mine[:, at + 2 : at + 3]
         )
         att_ref[:, cols] = (numerator / denominator).astype(bf16)
@@ -415,7 +449,7 @@
     order = order_of(replicas)
     index = lax.axis_index("tensor")
     core = (index % 2).reshape(1)
-    row = (index // 2).reshape(1)
+    far_row = (index // 2).reshape(1)
 
     def exchange(x):
         blocks = x.reshape(replicas, capacity, width + EXTRA)
@@ -444,21 +478,41 @@
     got = exchange(sent)
 
     early = 3
-    prefetched, last = pl.pallas_call(
-        prefetch_kernel,
-        out_shape=[pltpu.VMEM((early, size, HD), bf16), pltpu.HBM((width, quarter), bf16)],
-        in_specs=[SMEM_SPEC, HBM_SPEC, HBM_SPEC],
-        out_specs=[VMEM_SPEC, HBM_SPEC],
-        scratch_shapes=[
+    half = requests // 2
+    block = math.gcd(16, half)
+    length_row = suffix_length.reshape(1, requests)
+    halves = [shape((half, width), f32), shape((half, heads * 128), f32)]
+    row = pltpu.VMEM((1, requests), jnp.int32)
+    own_scratch = [
+        row,
+        pltpu.VMEM((requests, width), bf16),
+        pltpu.VMEM((half,) + suffix_cache.shape[1:], bf16),
+    ]
+    back, num_a, den_a, prefetched, last = pl.pallas_call(
+        functools.partial(early_kernel, capacity, order, block),
+        out_shape=[shape((requests, slots), bf16)]
+        + halves
+        + [pltpu.VMEM((early, size, HD), bf16), pltpu.HBM((width, quarter), bf16)],
+        in_specs=[SMEM_SPEC] + [HBM_SPEC] * 6,
+        out_specs=[VMEM_SPEC] * 4 + [HBM_SPEC],
+        scratch_shapes=[row]
+        + own_scratch
+        + [
             pltpu.VMEM((width, quarter), bf16),
+            pltpu.SemaphoreType.DMA((4,)),
             pltpu.SemaphoreType.DMA((early,)),
             pltpu.SemaphoreType.DMA,
         ],
         compiler_params=PARAMS,
         cost_estimate=pl.CostEstimate(
-            flops=0, bytes_accessed=2 * early * size * HD * 2, transcendentals=0
+            flops=4 * requests * window * HD * block,
+            bytes_accessed=2 * early * size * HD * 2 + suffix_cache.size,
+            transcendentals=0,
         ),
-    )(core, *in_hbm(prompt_cache, output_weight))
+    )(
+        core,
+        *in_hbm(owner_row, length_row, queries, suffix_cache, prompt_cache, output_weight),
+    )
 
     chunk = math.gcd(512, size)
     fit = min(48, slots)
@@ -486,43 +540,26 @@
     )
     returned = exchange(answered)
 
-    block = math.gcd(16, requests)
-    back, own_num, own_den, weight = pl.pallas_call(
-        functools.partial(suffix_kernel, capacity, order, block),
-        out_shape=[
-            shape((requests, slots), bf16),
-            shape((requests, width), f32),
-            shape((requests, heads * 128), f32),
-            pltpu.VMEM((3, width, quarter), bf16),
-        ],
-        in_specs=[HBM_SPEC] * 4 + [SMEM_SPEC, HBM_SPEC, HBM_SPEC],
-        out_specs=[VMEM_SPEC] * 4,
-        scratch_shapes=[
-            pltpu.VMEM((1, requests), jnp.int32),
-            pltpu.VMEM((1, requests), jnp.int32),
-            pltpu.VMEM((requests, width), bf16),
-            pltpu.VMEM(suffix_cache.shape, bf16),
-            pltpu.SemaphoreType.DMA((3,)),
-            pltpu.SemaphoreType.DMA((requests // block,)),
-            pltpu.SemaphoreType.DMA((3,)),
-        ],
+    num_b, den_b, weight = pl.pallas_call(
+        functools.partial(late_kernel, block),
+        out_shape=halves + [pltpu.VMEM((3, width, quarter), bf16)],
+        in_specs=[SMEM_SPEC] + [HBM_SPEC] * 5,
+        out_specs=[VMEM_SPEC] * 3,
+        scratch_shapes=own_scratch
+        + [pltpu.SemaphoreType.DMA((3,)), pltpu.SemaphoreType.DMA((3,))],
         compiler_params=PARAMS,
         cost_estimate=pl.CostEstimate(
-            flops=8 * requests * window * HD * block,
-            bytes_accessed=(suffix_cache.size + output_weight.size) * 2,
+            flops=4 * requests * window * HD * block,
+            bytes_accessed=suffix_cache.size + output_weight.size * 2,
             transcendentals=0,
         ),
-    )(
-        *in_hbm(owner_row, suffix_length.reshape(1, requests), queries, suffix_cache),
-        core,
-        *in_hbm(output_weight, answered),
-    )
+    )(core, *in_hbm(length_row, queries, suffix_cache, output_weight, answered))
     weight = pltpu.with_memory_space_constraint(weight, VMEM)
 
     attention, give = call(
         combine_kernel,
         [shape((requests, width), bf16), shape((requests, 2 * quarter), bf16)],
-        [returned, back, own_num, own_den, weight],
+        [returned, back, num_a, den_a, num_b, den_b, weight],
     )
     received = permute(give, 1)
     own = call(
@@ -539,7 +576,7 @@
     mine, square = call(
         square_kernel,
         [shape((requests, quarter), f32), shape((requests, 128), f32)],
-        [row, chip, far],
+        [far_row, chip, far],
     )
     beside = permute(square, 1)
     return call(

time: 41.5 us -> 41.3 us (level)
  Pallas kernels: 15.6 us -> 14.7 us
  waiting for transfers between devices: 9.58 us -> 10.2 us
    pallas_call x2, Pallas kernels: 7.29 us -> 6.45 us  [the longest x1 3.49 us: shards(): pl.pallas_call(functools.partial(early_kernel, capacity, order, block), o...]
    all_to_all x2, waiting for transfers between devices: 1.57 us -> 2.21 us  [exchange(): lax.all_to_all(blocks, 'replica', split_axis=0, concat_axis=0, axis_index...]
  transfers between devices with their start and end apart: 5 -> 5, of which waited for: 4 -> 5; matrix products, arithmetic and copies ran while one was open for 0% -> 0% of each run, Pallas kernels for 19% -> 17%
where the time goes in v5:
time: 41.3 us; the launch traced here: 40.9 us
  starting transfers between devices  15.5 us (38%)
  Pallas kernels  14.7 us (36%)
  waiting for transfers between devices  10.2 us (25%)
    all_to_all x2, starting transfers between devices, exchange(): lax.all_to_all(blocks, 'replica', split_axis=0, concat_axis=0, axis_index...  13.8 us
    ppermute x3, waiting for transfers between devices, permute(): return lax.ppermute(x, 'tensor', [(i, i ^ bit) for i in range(ranks)])  7.97 us
    pallas_call x1, Pallas kernels, shards(): pl.pallas_call(functools.partial(prompt_kernel, chunk, fit), out_shape=pl...  4.36 us
    pallas_call x1, Pallas kernels, shards(): pl.pallas_call(functools.partial(early_kernel, capacity, order, block), o...  3.49 us
    pallas_call x1, Pallas kernels, shards(): pl.pallas_call(functools.partial(late_kernel, block), out_shape=halves +...  2.96 us
    all_to_all x2, waiting for transfers between devices, exchange(): lax.all_to_all(blocks, 'replica', split_axis=0, concat_axis=0, axis_index...  2.21 us
    pallas_call x5, Pallas kernels, call(): pl.pallas_call(kernel, out_shape=outs, in_specs=specs, out_specs=jax.tree...  2.07 us
    pallas_call x1, Pallas kernels, shards(): pl.pallas_call(functools.partial(route_kernel, capacity, order), out_shap...  1.83 us
  transfers between devices with their start and end apart: 5, of which 5 were waited for; matrix products, arithmetic and copies ran while one was open for 0% of the time, Pallas kernels for 17%

profile of v5, /device:TPU:0, one launch (start us, length us, event | category | flops | bytes accessed | tf_op | source)
XLA Modules:
  0.0 40.9 jit_solution(15052214045350513799)
XLA Ops:
  0.0 1.8 %shard_map.100 = bf16[128,640]{1,0:T(8,128)(2,1)} custom-call(s32[1,64]{1,0:T(1,128)} %bitcast.11, s32[1,64]{1,0:T(1,128)} %bitcast.15, bf16[64,512]{1,0:T(8,128)(2,1)} %queries_hbm.5), custom_call_target="tpu_custom_call" | custom-call | tf_op jit(solution)/shard_map/pallas_call | solution.py:465
  1.8 7.8 %all-to-all-start = ((bf16[8,16,640]{2,1,0:T(8,128)(2,1)}), bf16[8,16,640]{2,1,0:T(8,128)(2,1)S(1)}, u32[]{:S(2)}, u32[]{:S(2)}) async-start(bf16[8,16,640]{2,1,0:T(8,128)(2,1)} %bitcast.3), calls=%async_computation | async-start | bytes 327680 | tf_op jit(solution)/shard_map/all_to_all | solution.py:456
  9.7 3.5 %shard_map.101 = (bf16[64,128]{1,0:T(8,128)(2,1)S(1)}, f32[32,512]{1,0:T(8,128)S(1)}, f32[32,256]{1,0:T(8,128)S(1)}, bf16[3,2048,256]{2,1,0:T(8,128)(2,1)S(1)}, bf16[512,896]{1,0:T(8,128)(2,1)}) custom-call(s32[1]{0:T(128)} %bitcast.5.core_ref, s32[1,64]{1,0:T(1,128)} %bitcast.12, s32[1,64]{1,0:T(1,128)} %bitcast.13, bf16[64,512]{1,0:T(8,128)(2,1)} %queries_hbm.5, ...), custom_call_target="tpu_custom_call" | custom-call | flops 67108864 | bytes 8388608 | tf_op jit(solution)/shard_map/pallas_call | solution.py:491
  13.2 0.9 %all-to-all-done = bf16[8,16,640]{2,1,0:T(8,128)(2,1)S(1)} async-done(((bf16[8,16,640]{2,1,0:T(8,128)(2,1)}), bf16[8,16,640]{2,1,0:T(8,128)(2,1)S(1)}, u32[]{:S(2)}, u32[]{:S(2)}) %all-to-all-start) | async-done | bytes 163872 | tf_op jit(solution)/shard_map/all_to_all | solution.py:456
  14.0 4.4 %shard_map.102.after_hbm = bf16[128,640]{1,0:T(8,128)(2,1)} custom-call(s32[4]{0:T(128)} %length_hbm.1, bf16[128,640]{1,0:T(8,128)(2,1)S(1)} %bitcast.10, bf16[3,2048,256]{2,1,0:T(8,128)(2,1)S(1)} %get-tuple-element.19.early_ref, bf16[4,2,2048,256]{3,2,1,0:T(8,128)(2,1)} %cache_hbm.4), custom_call_target="tpu_custom_call" | custom-call | tf_op jit(solution)/shard_map/pallas_call | solution.py:519
  18.4 6.0 %all-to-all-start.1 = ((bf16[8,16,640]{2,1,0:T(8,128)(2,1)}), bf16[8,16,640]{2,1,0:T(8,128)(2,1)S(1)}, u32[]{:S(2)}, u32[]{:S(2)}) async-start(bf16[8,16,640]{2,1,0:T(8,128)(2,1)} %bitcast.7), calls=%async_computation.1 | async-start | bytes 327680 | tf_op jit(solution)/shard_map/all_to_all | solution.py:456
  24.4 3.0 %shard_map.103 = (f32[32,512]{1,0:T(8,128)S(1)}, f32[32,256]{1,0:T(8,128)S(1)}, bf16[3,512,896]{2,1,0:T(8,128)(2,1)S(1)}) custom-call(s32[1]{0:T(128)} %bitcast.5.core_ref, s32[1,64]{1,0:T(1,128)} %bitcast.14, bf16[64,512]{1,0:T(8,128)(2,1)} %queries_hbm.5, bf16[64,2,64,256]{3,2,1,0:T(8,128)(2,1)} %cache_hbm.5, bf16[512,3584]{1,0:T(8,128)(2,1)} %weight_hbm.3, ...), custom_call_target="tpu_custom_call" | custom-call | flops 67108864 | bytes 5767168 | tf_op jit(solution)/shard_map/pallas_call | solution.py:543
  27.3 1.4 %all-to-all-done.1 = bf16[8,16,640]{2,1,0:T(8,128)(2,1)S(1)} async-done(((bf16[8,16,640]{2,1,0:T(8,128)(2,1)}), bf16[8,16,640]{2,1,0:T(8,128)(2,1)S(1)}, u32[]{:S(2)}, u32[]{:S(2)}) %all-to-all-start.1) | async-done | bytes 163872 | tf_op jit(solution)/shard_map/all_to_all | solution.py:456
  28.7 0.0 copy-start
  28.7 0.0 copy-start.2
  28.7 0.0 copy-start.1
  28.7 0.7 %shard_map.104 = (bf16[64,512]{1,0:T(8,128)(2,1)S(1)}, bf16[64,1792]{1,0:T(8,128)(2,1)S(1)}) custom-call(bf16[128,640]{1,0:T(8,128)(2,1)S(1)} %bitcast.9, bf16[64,128]{1,0:T(8,128)(2,1)S(1)} %get-tuple-element.20.back_ref, f32[32,512]{1,0:T(8,128)S(1)} %get-tuple-element.21.num_a, f32[32,256]{1,0:T(8,128)S(1)} %get-tuple-element.22.den_a, ...), custom_call_target="tpu_custom_call" | custom-call | tf_op jit(solution)/shard_map/pallas_call | solution.py:409
  29.4 0.1 collective-permute-start
  29.5 0.4 copy-done
  29.9 0.4 %shard_map.105.own_ref = f32[64,1792]{1,0:T(8,128)S(1)} custom-call(bf16[64,512]{1,0:T(8,128)(2,1)S(1)} %get-tuple-element.26.att_ref, bf16[3,512,896]{2,1,0:T(8,128)(2,1)S(1)} %get-tuple-element.25.weight_ref, bf16[512,896]{1,0:T(8,128)(2,1)S(1)} %copy-done), custom_call_target="tpu_custom_call" | custom-call | tf_op jit(solution)/shard_map/pallas_call | solution.py:409
  30.3 0.7 %collective-permute-done.got_ref = bf16[64,1792]{1,0:T(8,128)(2,1)S(1)} collective-permute-done((bf16[64,1792]{1,0:T(8,128)(2,1)S(1)}, bf16[64,1792]{1,0:T(8,128)(2,1)S(1)}, u32[]{:S(2)}, u32[]{:S(2)}) %collective-permute-start) | collective-permute-done | bytes 229408 | tf_op jit(solution)/shard_map/ppermute | solution.py:462
  31.0 0.1 shard_map.106
  31.0 1.6 %collective-permute-start.1 = (bf16[64,1792]{1,0:T(8,128)(2,1)S(1)}, bf16[64,1792]{1,0:T(8,128)(2,1)S(1)}, u32[]{:S(2)}, u32[]{:S(2)}) collective-permute-start(bf16[64,1792]{1,0:T(8,128)(2,1)S(1)} %get-tuple-element.30), channel_id=1, source_target_pairs={{0,2},{1,3},{2,0},{3,1},{4,6},{5,7},{6,4},{7,5},{8,10},{9,11},{10,... | collective-permute-start | bytes 688136 | tf_op jit(solution)/shard_map/ppermute | solution.py:462
  32.6 6.1 %collective-permute-done.1.got_ref = bf16[64,1792]{1,0:T(8,128)(2,1)S(1)} collective-permute-done((bf16[64,1792]{1,0:T(8,128)(2,1)S(1)}, bf16[64,1792]{1,0:T(8,128)(2,1)S(1)}, u32[]{:S(2)}, u32[]{:S(2)}) %collective-permute-start.1) | collective-permute-done | bytes 229408 | tf_op jit(solution)/shard_map/ppermute | solution.py:462
  38.8 0.1 shard_map.107
  38.8 0.1 collective-permute-start.2
  38.9 0.0 copy-done.2
  38.9 1.2 %collective-permute-done.2.got_ref = f32[64,128]{1,0:T(8,128)S(1)} collective-permute-done((f32[64,128]{1,0:T(8,128)S(1)}, f32[64,128]{1,0:T(8,128)S(1)}, u32[]{:S(2)}, u32[]{:S(2)}) %collective-permute-start.2) | collective-permute-done | bytes 32800 | tf_op jit(solution)/shard_map/ppermute | solution.py:462
  40.1 0.0 copy-done.1
  40.1 0.8 %shard_map.108 = bf16[64,896]{1,0:T(8,128)(2,1)} custom-call(f32[64,896]{1,0:T(8,128)S(1)} %get-tuple-element.31.mine_ref, f32[64,128]{1,0:T(8,128)S(1)} %get-tuple-element.32.square_ref, f32[64,128]{1,0:T(8,128)S(1)} %collective-permute-done.2.got_ref, f32[1,896]{1,0:T(1,128)S(1)} %reshape.39.gain_ref, bf16[64,896]{1,0:T(8,128)(2,1)S(1)} %copy-done.1), custom_call_target="tpu_custom_call" | custom-call | tf_op jit(solution)/shard_map/pallas_call | solution.py:409
  (1 shorter events, 0.0 us)
Async XLA Ops:
  1.8 12.2 %all-to-all-start = ((bf16[8,16,640]{2,1,0:T(8,128)(2,1)}), bf16[8,16,640]{2,1,0:T(8,128)(2,1)S(1)}, u32[]{:S(2)}, u32[]{:S(2)}) async-start(bf16[8,16,640]{2,1,0:T(8,128)(2,1)} %bitcast.3), calls=%async_computation | async-start | bytes 327680 | tf_op jit(solution)/shard_map/all_to_all | solution.py:456
  18.4 10.3 %all-to-all-start.1 = ((bf16[8,16,640]{2,1,0:T(8,128)(2,1)}), bf16[8,16,640]{2,1,0:T(8,128)(2,1)S(1)}, u32[]{:S(2)}, u32[]{:S(2)}) async-start(bf16[8,16,640]{2,1,0:T(8,128)(2,1)} %bitcast.7), calls=%async_computation.1 | async-start | bytes 327680 | tf_op jit(solution)/shard_map/all_to_all | solution.py:456
  28.7 1.2 %copy-start = (bf16[512,896]{1,0:T(8,128)(2,1)S(1)}, bf16[512,896]{1,0:T(8,128)(2,1)}, u32[]{:S(2)}) copy-start(bf16[512,896]{1,0:T(8,128)(2,1)} %get-tuple-element.27.last_ref) | copy-start | bytes 2752516
  28.7 10.2 %copy-start.2 = (f32[896]{0:T(1024)S(1)}, f32[896]{0:T(1024)}, u32[]{:S(2)}) copy-start(f32[896]{0:T(1024)} %param.19) | copy-start | bytes 10756
  28.7 11.4 %copy-start.1 = (bf16[64,896]{1,0:T(8,128)(2,1)S(1)}, bf16[64,896]{1,0:T(8,128)(2,1)}, u32[]{:S(2)}) copy-start(bf16[64,896]{1,0:T(8,128)(2,1)} %hidden_ref.1) | copy-start | bytes 344068
  29.4 1.6 %collective-permute-start = (bf16[64,1792]{1,0:T(8,128)(2,1)S(1)}, bf16[64,1792]{1,0:T(8,128)(2,1)S(1)}, u32[]{:S(2)}, u32[]{:S(2)}) collective-permute-start(bf16[64,1792]{1,0:T(8,128)(2,1)S(1)} %get-tuple-element.28), channel_id=1, source_target_pairs={{0,1},{1,0},{2,3},{3,2},{4,5},{5,4},{6,7},{7,6},{8,9},{9,8},{10,11... | collective-permute-start | bytes 688136 | tf_op jit(solution)/shard_map/ppermute | solution.py:462
  31.0 7.7 %collective-permute-start.1 = (bf16[64,1792]{1,0:T(8,128)(2,1)S(1)}, bf16[64,1792]{1,0:T(8,128)(2,1)S(1)}, u32[]{:S(2)}, u32[]{:S(2)}) collective-permute-start(bf16[64,1792]{1,0:T(8,128)(2,1)S(1)} %get-tuple-element.30), channel_id=1, source_target_pairs={{0,2},{1,3},{2,0},{3,1},{4,6},{5,7},{6,4},{7,5},{8,10},{9,11},{10,... | collective-permute-start | bytes 688136 | tf_op jit(solution)/shard_map/ppermute | solution.py:462
  38.8 1.3 %collective-permute-start.2 = (f32[64,128]{1,0:T(8,128)S(1)}, f32[64,128]{1,0:T(8,128)S(1)}, u32[]{:S(2)}, u32[]{:S(2)}) collective-permute-start(f32[64,128]{1,0:T(8,128)S(1)} %get-tuple-element.32.square_ref), channel_id=1, source_target_pairs={{0,1},{1,0},{2,3},{3,2},{4,5},{5,4},{6,7},{7,6},{8,9},{9,8},{10,11... | collective-permute-start | bytes 98312 | tf_op jit(solution)/shard_map/ppermute | solution.py:462

commit v6 on v5

--- a/solution.py
+++ b/solution.py
@@ -36,8 +36,9 @@
     return jnp.where(alive, jnp.exp2(weight_scale * jnp.tanh(scores * score_scale)), 0.0)
 
 
-def order_of(replicas):
-    return {8: (4, 5, 6, 1, 0, 7, 2, 3)}.get(replicas, tuple(range(replicas)))
+def orders_of(replicas):
+    tuned = {8: ((4, 5, 6, 1, 0, 7, 2, 3), (5, 7, 2, 4, 6, 1, 3, 0))}
+    return tuned.get(replicas, (tuple(range(replicas)),) * 2)
 
 
 def owners(owner_ref, order):
@@ -216,6 +217,7 @@
 def prompt_kernel(
     chunk,
     window,
+    moves,
     length_hbm,
     slots_ref,
     early_ref,
@@ -251,6 +253,12 @@
         i = parts.index((g, part))
         return early_ref[i, span, :] if i < early else held[i - early, span, :]
 
+    def moved(block):
+        if moves == sorted(moves):
+            return block
+        step = slots // len(moves)
+        return jnp.concatenate([block[m * step : (m + 1) * step] for m in moves], axis=0)
+
     def pieces(total, rows):
         lanes = iota((1, EXTRA), 1)
         extra = jnp.zeros((rows, EXTRA), f32)
@@ -282,7 +290,7 @@
     at_col = jnp.where(by_col > 0.0, (by_col - 1.0) * window + rank_col, -1.0).astype(jnp.int32)
     room = groups * window
     there = jnp.where(iota((room, slots), 0) == at_col, 1.0, 0.0).astype(bf16)
-    back = jnp.where(iota((slots, room), 1) == at_row, 1.0, 0.0).astype(bf16)
+    back = jnp.where(iota((slots, room), 1) == moved(at_row), 1.0, 0.0).astype(bf16)
     for h in range(heads):
         part = jnp.dot(there, slots_ref[:, h * HD : (h + 1) * HD], preferred_element_type=f32)
         for g in range(groups):
@@ -346,8 +354,10 @@
                 den_ref[...] += fold(weights)
 
         for h in range(heads):
-            out_ref[:, h * HD : (h + 1) * HD] = num_ref[h * slots : (h + 1) * slots].astype(bf16)
-        out_ref[:, width:] = pieces(jnp.sum(den_ref[...], axis=1, keepdims=True), slots)
+            num = num_ref[h * slots : (h + 1) * slots]
+            out_ref[:, h * HD : (h + 1) * HD] = moved(num).astype(bf16)
+        extra = pieces(jnp.sum(den_ref[...], axis=1, keepdims=True), slots)
+        out_ref[:, width:] = moved(extra.astype(f32)).astype(bf16)
 
 
 def combine_kernel(
@@ -446,12 +456,12 @@
     features = output_weight.shape[1]
     quarter = features // ranks
     heads = width // HD
-    order = order_of(replicas)
+    there, back_again = orders_of(replicas)
     index = lax.axis_index("tensor")
     core = (index % 2).reshape(1)
     far_row = (index // 2).reshape(1)
 
-    def exchange(x):
+    def exchange(x, order):
         blocks = x.reshape(replicas, capacity, width + EXTRA)
         blocks = lax.all_to_all(
             blocks, "replica", split_axis=0, concat_axis=0, axis_index_groups=[order], tiled=True
@@ -463,7 +473,7 @@
 
     owner_row = owner_replica.reshape(1, requests)
     sent = pl.pallas_call(
-        functools.partial(route_kernel, capacity, order),
+        functools.partial(route_kernel, capacity, there),
         out_shape=pltpu.VMEM((slots, width + EXTRA), bf16),
         in_specs=[HBM_SPEC] * 3,
         out_specs=VMEM_SPEC,
@@ -475,7 +485,7 @@
         ],
         compiler_params=PARAMS,
     )(*in_hbm(owner_row, group_slot.reshape(1, requests), queries))
-    got = exchange(sent)
+    got = exchange(sent, there)
 
     early = 3
     half = requests // 2
@@ -489,7 +499,7 @@
         pltpu.VMEM((half,) + suffix_cache.shape[1:], bf16),
     ]
     back, num_a, den_a, prefetched, last = pl.pallas_call(
-        functools.partial(early_kernel, capacity, order, block),
+        functools.partial(early_kernel, capacity, back_again, block),
         out_shape=[shape((requests, slots), bf16)]
         + halves
         + [pltpu.VMEM((early, size, HD), bf16), pltpu.HBM((width, quarter), bf16)],
@@ -515,9 +525,10 @@
     )
 
     chunk = math.gcd(512, size)
+    moves = [there.index(replica) for replica in back_again]
     fit = min(48, slots)
     answered = pl.pallas_call(
-        functools.partial(prompt_kernel, chunk, fit),
+        functools.partial(prompt_kernel, chunk, fit, moves),
         out_shape=pltpu.VMEM((slots, width + EXTRA), bf16),
         in_specs=[HBM_SPEC, VMEM_SPEC, VMEM_SPEC, HBM_SPEC],
         out_specs=VMEM_SPEC,
@@ -538,7 +549,7 @@
         pltpu.with_memory_space_constraint(prefetched, VMEM),
         *in_hbm(prompt_cache),
     )
-    returned = exchange(answered)
+    returned = exchange(answered, back_again)
 
     num_b, den_b, weight = pl.pallas_call(
         functools.partial(late_kernel, block),

time: 41.3 us -> 40.4 us (0.978)
  waiting for transfers between devices: 10.2 us -> 9.49 us
    all_to_all x2, waiting for transfers between devices: 2.21 us -> 1.51 us  [exchange(): lax.all_to_all(blocks, 'replica', split_axis=0, concat_axis=0, axis_index...]
where the time goes in v6:
time: 40.4 us; the launch traced here: 40 us
  starting transfers between devices  15.3 us (38%)
  Pallas kernels  14.7 us (36%)
  waiting for transfers between devices  9.49 us (23%)
    all_to_all x2, starting transfers between devices, exchange(): lax.all_to_all(blocks, 'replica', split_axis=0, concat_axis=0, axis_index...  13.6 us
    ppermute x3, waiting for transfers between devices, permute(): return lax.ppermute(x, 'tensor', [(i, i ^ bit) for i in range(ranks)])  7.98 us
    pallas_call x1, Pallas kernels, shards(): pl.pallas_call(functools.partial(prompt_kernel, chunk, fit, moves), out_s...  4.36 us
    pallas_call x1, Pallas kernels, shards(): pl.pallas_call(functools.partial(early_kernel, capacity, back_again, bloc...  3.49 us
    pallas_call x1, Pallas kernels, shards(): pl.pallas_call(functools.partial(late_kernel, block), out_shape=halves +...  2.96 us
    pallas_call x5, Pallas kernels, call(): pl.pallas_call(kernel, out_shape=outs, in_specs=specs, out_specs=jax.tree...  2.07 us
    pallas_call x1, Pallas kernels, shards(): pl.pallas_call(functools.partial(route_kernel, capacity, there), out_shap...  1.83 us
    ppermute x3, starting transfers between devices, permute(): return lax.ppermute(x, 'tensor', [(i, i ^ bit) for i in range(ranks)])  1.73 us
  transfers between devices with their start and end apart: 5, of which 5 were waited for; matrix products, arithmetic and copies ran while one was open for 0% of the time, Pallas kernels for 17%

profile of v6, /device:TPU:0, one launch (start us, length us, event | category | flops | bytes accessed | tf_op | source)
XLA Modules:
  0.0 40.0 jit_solution(6171144884878806285)
XLA Ops:
  0.0 1.8 %shard_map.100 = bf16[128,640]{1,0:T(8,128)(2,1)} custom-call(s32[1,64]{1,0:T(1,128)} %bitcast.11, s32[1,64]{1,0:T(1,128)} %bitcast.15, bf16[64,512]{1,0:T(8,128)(2,1)} %queries_hbm.5), custom_call_target="tpu_custom_call" | custom-call | tf_op jit(solution)/shard_map/pallas_call | solution.py:475
  1.8 7.8 %all-to-all-start = ((bf16[8,16,640]{2,1,0:T(8,128)(2,1)}), bf16[8,16,640]{2,1,0:T(8,128)(2,1)S(1)}, u32[]{:S(2)}, u32[]{:S(2)}) async-start(bf16[8,16,640]{2,1,0:T(8,128)(2,1)} %bitcast.3), calls=%async_computation | async-start | bytes 327680 | tf_op jit(solution)/shard_map/all_to_all | solution.py:466
  9.7 3.5 %shard_map.101 = (bf16[64,128]{1,0:T(8,128)(2,1)S(1)}, f32[32,512]{1,0:T(8,128)S(1)}, f32[32,256]{1,0:T(8,128)S(1)}, bf16[3,2048,256]{2,1,0:T(8,128)(2,1)S(1)}, bf16[512,896]{1,0:T(8,128)(2,1)}) custom-call(s32[1]{0:T(128)} %bitcast.5.core_ref, s32[1,64]{1,0:T(1,128)} %bitcast.12, s32[1,64]{1,0:T(1,128)} %bitcast.13, bf16[64,512]{1,0:T(8,128)(2,1)} %queries_hbm.5, ...), custom_call_target="tpu_custom_call" | custom-call | flops 67108864 | bytes 8388608 | tf_op jit(solution)/shard_map/pallas_call | solution.py:501
  13.2 0.9 %all-to-all-done = bf16[8,16,640]{2,1,0:T(8,128)(2,1)S(1)} async-done(((bf16[8,16,640]{2,1,0:T(8,128)(2,1)}), bf16[8,16,640]{2,1,0:T(8,128)(2,1)S(1)}, u32[]{:S(2)}, u32[]{:S(2)}) %all-to-all-start) | async-done | bytes 163872 | tf_op jit(solution)/shard_map/all_to_all | solution.py:466
  14.0 4.4 %shard_map.102.after_hbm = bf16[128,640]{1,0:T(8,128)(2,1)} custom-call(s32[4]{0:T(128)} %length_hbm.1, bf16[128,640]{1,0:T(8,128)(2,1)S(1)} %bitcast.10, bf16[3,2048,256]{2,1,0:T(8,128)(2,1)S(1)} %get-tuple-element.19.early_ref, bf16[4,2,2048,256]{3,2,1,0:T(8,128)(2,1)} %cache_hbm.4), custom_call_target="tpu_custom_call" | custom-call | tf_op jit(solution)/shard_map/pallas_call | solution.py:530
  18.4 5.8 %all-to-all-start.1 = ((bf16[8,16,640]{2,1,0:T(8,128)(2,1)}), bf16[8,16,640]{2,1,0:T(8,128)(2,1)S(1)}, u32[]{:S(2)}, u32[]{:S(2)}) async-start(bf16[8,16,640]{2,1,0:T(8,128)(2,1)} %bitcast.7), calls=%async_computation.1 | async-start | bytes 327680 | tf_op jit(solution)/shard_map/all_to_all | solution.py:466
  24.2 3.0 %shard_map.103 = (f32[32,512]{1,0:T(8,128)S(1)}, f32[32,256]{1,0:T(8,128)S(1)}, bf16[3,512,896]{2,1,0:T(8,128)(2,1)S(1)}) custom-call(s32[1]{0:T(128)} %bitcast.5.core_ref, s32[1,64]{1,0:T(1,128)} %bitcast.14, bf16[64,512]{1,0:T(8,128)(2,1)} %queries_hbm.5, bf16[64,2,64,256]{3,2,1,0:T(8,128)(2,1)} %cache_hbm.5, bf16[512,3584]{1,0:T(8,128)(2,1)} %weight_hbm.3, ...), custom_call_target="tpu_custom_call" | custom-call | flops 67108864 | bytes 5767168 | tf_op jit(solution)/shard_map/pallas_call | solution.py:554
  27.1 0.7 %all-to-all-done.1 = bf16[8,16,640]{2,1,0:T(8,128)(2,1)S(1)} async-done(((bf16[8,16,640]{2,1,0:T(8,128)(2,1)}), bf16[8,16,640]{2,1,0:T(8,128)(2,1)S(1)}, u32[]{:S(2)}, u32[]{:S(2)}) %all-to-all-start.1) | async-done | bytes 163872 | tf_op jit(solution)/shard_map/all_to_all | solution.py:466
  27.8 0.0 copy-start
  27.8 0.0 copy-start.2
  27.8 0.0 copy-start.1
  27.8 0.7 %shard_map.104 = (bf16[64,512]{1,0:T(8,128)(2,1)S(1)}, bf16[64,1792]{1,0:T(8,128)(2,1)S(1)}) custom-call(bf16[128,640]{1,0:T(8,128)(2,1)S(1)} %bitcast.9, bf16[64,128]{1,0:T(8,128)(2,1)S(1)} %get-tuple-element.20.back_ref, f32[32,512]{1,0:T(8,128)S(1)} %get-tuple-element.21.num_a, f32[32,256]{1,0:T(8,128)S(1)} %get-tuple-element.22.den_a, ...), custom_call_target="tpu_custom_call" | custom-call | tf_op jit(solution)/shard_map/pallas_call | solution.py:419
  28.5 0.1 collective-permute-start
  28.6 0.4 copy-done
  29.0 0.4 %shard_map.105.own_ref = f32[64,1792]{1,0:T(8,128)S(1)} custom-call(bf16[64,512]{1,0:T(8,128)(2,1)S(1)} %get-tuple-element.26.att_ref, bf16[3,512,896]{2,1,0:T(8,128)(2,1)S(1)} %get-tuple-element.25.weight_ref, bf16[512,896]{1,0:T(8,128)(2,1)S(1)} %copy-done), custom_call_target="tpu_custom_call" | custom-call | tf_op jit(solution)/shard_map/pallas_call | solution.py:419
  29.4 0.7 %collective-permute-done.got_ref = bf16[64,1792]{1,0:T(8,128)(2,1)S(1)} collective-permute-done((bf16[64,1792]{1,0:T(8,128)(2,1)S(1)}, bf16[64,1792]{1,0:T(8,128)(2,1)S(1)}, u32[]{:S(2)}, u32[]{:S(2)}) %collective-permute-start) | collective-permute-done | bytes 229408 | tf_op jit(solution)/shard_map/ppermute | solution.py:472
  30.1 0.1 shard_map.106
  30.1 1.6 %collective-permute-start.1 = (bf16[64,1792]{1,0:T(8,128)(2,1)S(1)}, bf16[64,1792]{1,0:T(8,128)(2,1)S(1)}, u32[]{:S(2)}, u32[]{:S(2)}) collective-permute-start(bf16[64,1792]{1,0:T(8,128)(2,1)S(1)} %get-tuple-element.30), channel_id=1, source_target_pairs={{0,2},{1,3},{2,0},{3,1},{4,6},{5,7},{6,4},{7,5},{8,10},{9,11},{10,... | collective-permute-start | bytes 688136 | tf_op jit(solution)/shard_map/ppermute | solution.py:472
  31.7 6.1 %collective-permute-done.1.got_ref = bf16[64,1792]{1,0:T(8,128)(2,1)S(1)} collective-permute-done((bf16[64,1792]{1,0:T(8,128)(2,1)S(1)}, bf16[64,1792]{1,0:T(8,128)(2,1)S(1)}, u32[]{:S(2)}, u32[]{:S(2)}) %collective-permute-start.1) | collective-permute-done | bytes 229408 | tf_op jit(solution)/shard_map/ppermute | solution.py:472
  37.9 0.1 shard_map.107
  37.9 0.1 collective-permute-start.2
  38.0 0.0 copy-done.2
  38.0 1.2 %collective-permute-done.2.got_ref = f32[64,128]{1,0:T(8,128)S(1)} collective-permute-done((f32[64,128]{1,0:T(8,128)S(1)}, f32[64,128]{1,0:T(8,128)S(1)}, u32[]{:S(2)}, u32[]{:S(2)}) %collective-permute-start.2) | collective-permute-done | bytes 32800 | tf_op jit(solution)/shard_map/ppermute | solution.py:472
  39.2 0.0 copy-done.1
  39.2 0.8 %shard_map.108 = bf16[64,896]{1,0:T(8,128)(2,1)} custom-call(f32[64,896]{1,0:T(8,128)S(1)} %get-tuple-element.31.mine_ref, f32[64,128]{1,0:T(8,128)S(1)} %get-tuple-element.32.square_ref, f32[64,128]{1,0:T(8,128)S(1)} %collective-permute-done.2.got_ref, f32[1,896]{1,0:T(1,128)S(1)} %reshape.39.gain_ref, bf16[64,896]{1,0:T(8,128)(2,1)S(1)} %copy-done.1), custom_call_target="tpu_custom_call" | custom-call | tf_op jit(solution)/shard_map/pallas_call | solution.py:419
  (1 shorter events, 0.0 us)
Async XLA Ops:
  1.8 12.2 %all-to-all-start = ((bf16[8,16,640]{2,1,0:T(8,128)(2,1)}), bf16[8,16,640]{2,1,0:T(8,128)(2,1)S(1)}, u32[]{:S(2)}, u32[]{:S(2)}) async-start(bf16[8,16,640]{2,1,0:T(8,128)(2,1)} %bitcast.3), calls=%async_computation | async-start | bytes 327680 | tf_op jit(solution)/shard_map/all_to_all | solution.py:466
  18.4 9.4 %all-to-all-start.1 = ((bf16[8,16,640]{2,1,0:T(8,128)(2,1)}), bf16[8,16,640]{2,1,0:T(8,128)(2,1)S(1)}, u32[]{:S(2)}, u32[]{:S(2)}) async-start(bf16[8,16,640]{2,1,0:T(8,128)(2,1)} %bitcast.7), calls=%async_computation.1 | async-start | bytes 327680 | tf_op jit(solution)/shard_map/all_to_all | solution.py:466
  27.8 1.2 %copy-start = (bf16[512,896]{1,0:T(8,128)(2,1)S(1)}, bf16[512,896]{1,0:T(8,128)(2,1)}, u32[]{:S(2)}) copy-start(bf16[512,896]{1,0:T(8,128)(2,1)} %get-tuple-element.27.last_ref) | copy-start | bytes 2752516
  27.8 10.2 %copy-start.2 = (f32[896]{0:T(1024)S(1)}, f32[896]{0:T(1024)}, u32[]{:S(2)}) copy-start(f32[896]{0:T(1024)} %param.19) | copy-start | bytes 10756
  27.8 11.4 %copy-start.1 = (bf16[64,896]{1,0:T(8,128)(2,1)S(1)}, bf16[64,896]{1,0:T(8,128)(2,1)}, u32[]{:S(2)}) copy-start(bf16[64,896]{1,0:T(8,128)(2,1)} %hidden_ref.1) | copy-start | bytes 344068
  28.5 1.6 %collective-permute-start = (bf16[64,1792]{1,0:T(8,128)(2,1)S(1)}, bf16[64,1792]{1,0:T(8,128)(2,1)S(1)}, u32[]{:S(2)}, u32[]{:S(2)}) collective-permute-start(bf16[64,1792]{1,0:T(8,128)(2,1)S(1)} %get-tuple-element.28), channel_id=1, source_target_pairs={{0,1},{1,0},{2,3},{3,2},{4,5},{5,4},{6,7},{7,6},{8,9},{9,8},{10,11... | collective-permute-start | bytes 688136 | tf_op jit(solution)/shard_map/ppermute | solution.py:472
  30.1 7.7 %collective-permute-start.1 = (bf16[64,1792]{1,0:T(8,128)(2,1)S(1)}, bf16[64,1792]{1,0:T(8,128)(2,1)S(1)}, u32[]{:S(2)}, u32[]{:S(2)}) collective-permute-start(bf16[64,1792]{1,0:T(8,128)(2,1)S(1)} %get-tuple-element.30), channel_id=1, source_target_pairs={{0,2},{1,3},{2,0},{3,1},{4,6},{5,7},{6,4},{7,5},{8,10},{9,11},{10,... | collective-permute-start | bytes 688136 | tf_op jit(solution)/shard_map/ppermute | solution.py:472
  37.9 1.3 %collective-permute-start.2 = (f32[64,128]{1,0:T(8,128)S(1)}, f32[64,128]{1,0:T(8,128)S(1)}, u32[]{:S(2)}, u32[]{:S(2)}) collective-permute-start(f32[64,128]{1,0:T(8,128)S(1)} %get-tuple-element.32.square_ref), channel_id=1, source_target_pairs={{0,1},{1,0},{2,3},{3,2},{4,5},{5,4},{6,7},{7,6},{8,9},{9,8},{10,11... | collective-permute-start | bytes 98312 | tf_op jit(solution)/shard_map/ppermute | solution.py:472

commit v7 on v6

--- a/solution.py
+++ b/solution.py
@@ -363,7 +363,6 @@
 def combine_kernel(
     returned_ref, back_ref, num_a, den_a, num_b, den_b, weight_ref, att_ref, give_ref
 ):
-    quarter = weight_ref.shape[2]
     width = num_a.shape[1]
     heads = width // HD
     mine = jnp.dot(back_ref[...], returned_ref[...], preferred_element_type=f32)
@@ -376,16 +375,15 @@
             mine[:, at : at + 1] + mine[:, at + 1 : at + 2] + mine[:, at + 2 : at + 3]
         )
         att_ref[:, cols] = (numerator / denominator).astype(bf16)
-    for i in range(2):
-        give_ref[:, i * quarter : (i + 1) * quarter] = jnp.dot(
-            att_ref[...], weight_ref[i], preferred_element_type=f32
-        ).astype(bf16)
-
-
-def own_kernel(att_ref, weight_ref, last_ref, own_ref):
-    quarter = weight_ref.shape[2]
-    own_ref[:, :quarter] = jnp.dot(att_ref[...], weight_ref[2], preferred_element_type=f32)
-    own_ref[:, quarter:] = jnp.dot(att_ref[...], last_ref[...], preferred_element_type=f32)
+    give_ref[...] = jnp.dot(att_ref[...], weight_ref[0], preferred_element_type=f32).astype(bf16)
+
+
+def give_kernel(att_ref, weight_ref, give_ref):
+    give_ref[...] = jnp.dot(att_ref[...], weight_ref[1], preferred_element_type=f32).astype(bf16)
+
+
+def own_kernel(att_ref, weight_ref, own_ref):
+    own_ref[...] = jnp.dot(att_ref[...], weight_ref[2], preferred_element_type=f32)
 
 
 def chip_kernel(own_ref, got_ref, sum_ref, send_ref):
@@ -394,15 +392,24 @@
     send_ref[...] = total.astype(bf16)
 
 
-def square_kernel(row_ref, sum_ref, got_ref, mine_ref, square_ref):
-    width = mine_ref.shape[1]
-    total = sum_ref[...] + got_ref[...].astype(f32)
+def last_kernel(att_ref, weight_ref, got_ref, after_ref, sum_ref, send_ref):
+    total = jnp.dot(att_ref[...], weight_ref[...], preferred_element_type=f32)
+    total = total + got_ref[...].astype(f32)
+    sum_ref[...] = total
+    send_ref[...] = total.astype(bf16)
+
+
+def square_kernel(row_ref, sum_a, got_a, sum_b, got_b, mine_ref, square_ref):
     part = jnp.zeros(square_ref.shape, f32)
-    for k in range(total.shape[1] // 128):
-        piece = total[:, k * 128 : (k + 1) * 128]
-        part = part + piece * piece
+    totals = []
+    for sum_ref, got_ref in ((sum_a, got_a), (sum_b, got_b)):
+        total = sum_ref[...] + got_ref[...].astype(f32)
+        for k in range(total.shape[1] // 128):
+            piece = total[:, k * 128 : (k + 1) * 128]
+            part = part + piece * piece
+        totals.append(total)
     square_ref[...] = part
-    mine_ref[...] = jnp.where(row_ref[0] == 0, total[:, :width], total[:, width:])
+    mine_ref[...] = jnp.where(row_ref[0] == 0, totals[0], totals[1])
 
 
 def final_kernel(features, mine_ref, square_ref, got_ref, gain_ref, hidden_ref, out_ref):
@@ -567,27 +574,24 @@
     )(core, *in_hbm(length_row, queries, suffix_cache, output_weight, answered))
     weight = pltpu.with_memory_space_constraint(weight, VMEM)
 
-    attention, give = call(
+    block_f32 = shape((requests, quarter), f32)
+    block_bf16 = shape((requests, quarter), bf16)
+    attention, give_a = call(
         combine_kernel,
-        [shape((requests, width), bf16), shape((requests, 2 * quarter), bf16)],
+        [shape((requests, width), bf16), block_bf16],
         [returned, back, num_a, den_a, num_b, den_b, weight],
     )
-    received = permute(give, 1)
-    own = call(
-        own_kernel,
-        shape((requests, 2 * quarter), f32),
-        [attention, weight, last],
-    )
-    chip, send = call(
-        chip_kernel,
-        [shape((requests, 2 * quarter), f32), shape((requests, 2 * quarter), bf16)],
-        [own, received],
-    )
-    far = permute(send, 2)
+    got_a = permute(give_a, 1)
+    got_b = permute(call(give_kernel, block_bf16, [attention, weight]), 1)
+    own_a = call(own_kernel, block_f32, [attention, weight])
+    sum_a, send_a = call(chip_kernel, [block_f32, block_bf16], [own_a, got_a])
+    far_a = permute(send_a, 2)
+    sum_b, send_b = call(last_kernel, [block_f32, block_bf16], [attention, last, got_b, send_a])
+    far_b = permute(send_b, 2)
     mine, square = call(
         square_kernel,
-        [shape((requests, quarter), f32), shape((requests, 128), f32)],
-        [far_row, chip, far],
+        [block_f32, shape((requests, 128), f32)],
+        [far_row, sum_a, far_a, sum_b, far_b],
     )
     beside = permute(square, 1)
     return call(

time: 40.4 us -> 40 us (0.990)
  waiting for transfers between devices: 9.49 us -> 8.11 us
  starting transfers between devices: 15.3 us -> 16.4 us
    ppermute x3 -> x5, waiting for transfers between devices: 7.98 us -> 6.59 us  [permute(): return lax.ppermute(x, 'tensor', [(i, i ^ bit) for i in range(ranks)])]
    ppermute x3 -> x5, starting transfers between devices: 1.73 us -> 2.84 us  [permute(): return lax.ppermute(x, 'tensor', [(i, i ^ bit) for i in range(ranks)])]
    pallas_call x5 -> x7, Pallas kernels: 2.07 us -> 2.32 us  [call(): pl.pallas_call(kernel, out_shape=outs, in_specs=specs, out_specs=jax.tree...]
  transfers between devices with their start and end apart: 5 -> 7, of which waited for: 5 -> 6; matrix products, arithmetic and copies ran while one was open for 0% -> 0% of each run, Pallas kernels for 17% -> 19%
where the time goes in v7:
time: 40 us; the launch traced here: 39.6 us
  starting transfers between devices  16.4 us (41%)
  Pallas kernels  14.9 us (37%)
  waiting for transfers between devices  8.11 us (20%)
    all_to_all x2, starting transfers between devices, exchange(): lax.all_to_all(blocks, 'replica', split_axis=0, concat_axis=0, axis_index...  13.6 us
    ppermute x5, waiting for transfers between devices, permute(): return lax.ppermute(x, 'tensor', [(i, i ^ bit) for i in range(ranks)])  6.59 us
    pallas_call x1, Pallas kernels, shards(): pl.pallas_call(functools.partial(prompt_kernel, chunk, fit, moves), out_s...  4.34 us
    pallas_call x1, Pallas kernels, shards(): pl.pallas_call(functools.partial(early_kernel, capacity, back_again, bloc...  3.48 us
    pallas_call x1, Pallas kernels, shards(): pl.pallas_call(functools.partial(late_kernel, block), out_shape=halves +...  2.96 us
    ppermute x5, starting transfers between devices, permute(): return lax.ppermute(x, 'tensor', [(i, i ^ bit) for i in range(ranks)])  2.84 us
    pallas_call x7, Pallas kernels, call(): pl.pallas_call(kernel, out_shape=outs, in_specs=specs, out_specs=jax.tree...  2.32 us
    pallas_call x1, Pallas kernels, shards(): pl.pallas_call(functools.partial(route_kernel, capacity, there), out_shap...  1.82 us
  transfers between devices with their start and end apart: 7, of which 6 were waited for; matrix products, arithmetic and copies ran while one was open for 0% of the time, Pallas kernels for 19%

profile of v7, /device:TPU:0, one launch (start us, length us, event | category | flops | bytes accessed | tf_op | source)
XLA Modules:
  0.0 39.6 jit_solution(11726997217624368467)
XLA Ops:
  0.0 1.8 %shard_map.100 = bf16[128,640]{1,0:T(8,128)(2,1)} custom-call(s32[1,64]{1,0:T(1,128)} %bitcast.11, s32[1,64]{1,0:T(1,128)} %bitcast.15, bf16[64,512]{1,0:T(8,128)(2,1)} %queries_hbm.5), custom_call_target="tpu_custom_call" | custom-call | tf_op jit(solution)/shard_map/pallas_call | solution.py:482
  1.8 7.8 %all-to-all-start = ((bf16[8,16,640]{2,1,0:T(8,128)(2,1)}), bf16[8,16,640]{2,1,0:T(8,128)(2,1)S(1)}, u32[]{:S(2)}, u32[]{:S(2)}) async-start(bf16[8,16,640]{2,1,0:T(8,128)(2,1)} %bitcast.3), calls=%async_computation | async-start | bytes 327680 | tf_op jit(solution)/shard_map/all_to_all | solution.py:473
  9.6 3.5 %shard_map.101 = (bf16[64,128]{1,0:T(8,128)(2,1)S(1)}, f32[32,512]{1,0:T(8,128)S(1)}, f32[32,256]{1,0:T(8,128)S(1)}, bf16[3,2048,256]{2,1,0:T(8,128)(2,1)S(1)}, bf16[512,896]{1,0:T(8,128)(2,1)}) custom-call(s32[1]{0:T(128)} %bitcast.5.core_ref, s32[1,64]{1,0:T(1,128)} %bitcast.12, s32[1,64]{1,0:T(1,128)} %bitcast.13, bf16[64,512]{1,0:T(8,128)(2,1)} %queries_hbm.5, ...), custom_call_target="tpu_custom_call" | custom-call | flops 67108864 | bytes 8388608 | tf_op jit(solution)/shard_map/pallas_call | solution.py:508
  13.1 0.9 %all-to-all-done = bf16[8,16,640]{2,1,0:T(8,128)(2,1)S(1)} async-done(((bf16[8,16,640]{2,1,0:T(8,128)(2,1)}), bf16[8,16,640]{2,1,0:T(8,128)(2,1)S(1)}, u32[]{:S(2)}, u32[]{:S(2)}) %all-to-all-start) | async-done | bytes 163872 | tf_op jit(solution)/shard_map/all_to_all | solution.py:473
  14.0 4.3 %shard_map.102.after_hbm = bf16[128,640]{1,0:T(8,128)(2,1)} custom-call(s32[4]{0:T(128)} %length_hbm.1, bf16[128,640]{1,0:T(8,128)(2,1)S(1)} %bitcast.10, bf16[3,2048,256]{2,1,0:T(8,128)(2,1)S(1)} %get-tuple-element.21.early_ref, bf16[4,2,2048,256]{3,2,1,0:T(8,128)(2,1)} %cache_hbm.4), custom_call_target="tpu_custom_call" | custom-call | tf_op jit(solution)/shard_map/pallas_call | solution.py:537
  18.3 5.8 %all-to-all-start.1 = ((bf16[8,16,640]{2,1,0:T(8,128)(2,1)}), bf16[8,16,640]{2,1,0:T(8,128)(2,1)S(1)}, u32[]{:S(2)}, u32[]{:S(2)}) async-start(bf16[8,16,640]{2,1,0:T(8,128)(2,1)} %bitcast.7), calls=%async_computation.1 | async-start | bytes 327680 | tf_op jit(solution)/shard_map/all_to_all | solution.py:473
  24.1 3.0 %shard_map.103 = (f32[32,512]{1,0:T(8,128)S(1)}, f32[32,256]{1,0:T(8,128)S(1)}, bf16[3,512,896]{2,1,0:T(8,128)(2,1)S(1)}) custom-call(s32[1]{0:T(128)} %bitcast.5.core_ref, s32[1,64]{1,0:T(1,128)} %bitcast.14, bf16[64,512]{1,0:T(8,128)(2,1)} %queries_hbm.5, bf16[64,2,64,256]{3,2,1,0:T(8,128)(2,1)} %cache_hbm.5, bf16[512,3584]{1,0:T(8,128)(2,1)} %weight_hbm.3, ...), custom_call_target="tpu_custom_call" | custom-call | flops 67108864 | bytes 5767168 | tf_op jit(solution)/shard_map/pallas_call | solution.py:561
  27.1 0.7 %all-to-all-done.1 = bf16[8,16,640]{2,1,0:T(8,128)(2,1)S(1)} async-done(((bf16[8,16,640]{2,1,0:T(8,128)(2,1)}), bf16[8,16,640]{2,1,0:T(8,128)(2,1)S(1)}, u32[]{:S(2)}, u32[]{:S(2)}) %all-to-all-start.1) | async-done | bytes 163872 | tf_op jit(solution)/shard_map/all_to_all | solution.py:473
  27.7 0.6 %shard_map.104 = (bf16[64,512]{1,0:T(8,128)(2,1)S(1)}, bf16[64,896]{1,0:T(8,128)(2,1)S(1)}) custom-call(bf16[128,640]{1,0:T(8,128)(2,1)S(1)} %bitcast.9, bf16[64,128]{1,0:T(8,128)(2,1)S(1)} %get-tuple-element.22.back_ref, f32[32,512]{1,0:T(8,128)S(1)} %get-tuple-element.23.num_a, f32[32,256]{1,0:T(8,128)S(1)} %get-tuple-element.24.den_a, ...), custom_call_target="tpu_custom_call" | custom-call | tf_op jit(solution)/shard_map/pallas_call | solution.py:426
  28.3 0.0 copy-start
  28.3 0.1 collective-permute-start
  28.4 0.0 copy-start.2
  28.4 0.0 copy-start.1
  28.4 0.3 shard_map.107
  28.7 0.5 %collective-permute-start.2 = (bf16[64,896]{1,0:T(8,128)(2,1)S(1)}, bf16[64,896]{1,0:T(8,128)(2,1)S(1)}, u32[]{:S(2)}, u32[]{:S(2)}) collective-permute-start(bf16[64,896]{1,0:T(8,128)(2,1)S(1)} %shard_map.107), channel_id=1, source_target_pairs={{0,1},{1,0},{2,3},{3,2},{4,5},{5,4},{6,7},{7,6},{8,9},{9,8},{10,11... | collective-permute-start | bytes 344072 | tf_op jit(solution)/shard_map/ppermute | solution.py:479
  29.3 0.3 shard_map.105.own_ref
  29.6 0.2 collective-permute-done.got_ref
  29.8 1.6 %collective-permute-start.1 = (bf16[64,896]{1,0:T(8,128)(2,1)S(1)}, bf16[64,896]{1,0:T(8,128)(2,1)S(1)}, u32[]{:S(2)}, u32[]{:S(2)}) collective-permute-start(bf16[64,896]{1,0:T(8,128)(2,1)S(1)} %get-tuple-element.31.after_ref), channel_id=1, source_target_pairs={{0,2},{1,3},{2,0},{3,1},{4,6},{5,7},{6,4},{7,5},{8,10},{9,11},{10,... | collective-permute-start | bytes 344072 | tf_op jit(solution)/shard_map/ppermute | solution.py:479
  31.3 0.0 collective-permute-done.2.got_ref
  31.4 0.0 copy-done
  31.4 0.3 shard_map.108
  31.7 0.6 %collective-permute-start.3 = (bf16[64,896]{1,0:T(8,128)(2,1)S(1)}, bf16[64,896]{1,0:T(8,128)(2,1)S(1)}, u32[]{:S(2)}, u32[]{:S(2)}) collective-permute-start(bf16[64,896]{1,0:T(8,128)(2,1)S(1)} %get-tuple-element.34), channel_id=1, source_target_pairs={{0,2},{1,3},{2,0},{3,1},{4,6},{5,7},{6,4},{7,5},{8,10},{9,11},{10,... | collective-permute-start | bytes 344072 | tf_op jit(solution)/shard_map/ppermute | solution.py:479
  32.2 3.6 %collective-permute-done.1.got_a = bf16[64,896]{1,0:T(8,128)(2,1)S(1)} collective-permute-done((bf16[64,896]{1,0:T(8,128)(2,1)S(1)}, bf16[64,896]{1,0:T(8,128)(2,1)S(1)}, u32[]{:S(2)}, u32[]{:S(2)}) %collective-permute-start.1) | collective-permute-done | bytes 114720 | tf_op jit(solution)/shard_map/ppermute | solution.py:479
  35.8 1.7 %collective-permute-done.3.got_b = bf16[64,896]{1,0:T(8,128)(2,1)S(1)} collective-permute-done((bf16[64,896]{1,0:T(8,128)(2,1)S(1)}, bf16[64,896]{1,0:T(8,128)(2,1)S(1)}, u32[]{:S(2)}, u32[]{:S(2)}) %collective-permute-start.3) | collective-permute-done | bytes 114720 | tf_op jit(solution)/shard_map/ppermute | solution.py:479
  37.5 0.1 shard_map.109
  37.6 0.1 collective-permute-start.4
  37.6 0.0 copy-done.2
  37.7 1.2 %collective-permute-done.4.got_ref = f32[64,128]{1,0:T(8,128)S(1)} collective-permute-done((f32[64,128]{1,0:T(8,128)S(1)}, f32[64,128]{1,0:T(8,128)S(1)}, u32[]{:S(2)}, u32[]{:S(2)}) %collective-permute-start.4) | collective-permute-done | bytes 32800 | tf_op jit(solution)/shard_map/ppermute | solution.py:479
  38.8 0.0 copy-done.1
  38.8 0.8 %shard_map.110 = bf16[64,896]{1,0:T(8,128)(2,1)} custom-call(f32[64,896]{1,0:T(8,128)S(1)} %get-tuple-element.35.mine_ref, f32[64,128]{1,0:T(8,128)S(1)} %get-tuple-element.36.square_ref, f32[64,128]{1,0:T(8,128)S(1)} %collective-permute-done.4.got_ref, f32[1,896]{1,0:T(1,128)S(1)} %reshape.39.gain_ref, bf16[64,896]{1,0:T(8,128)(2,1)S(1)} %copy-done.1), custom_call_target="tpu_custom_call" | custom-call | tf_op jit(solution)/shard_map/pallas_call | solution.py:426
  (2 shorter events, 0.0 us)
Async XLA Ops:
  1.8 12.2 %all-to-all-start = ((bf16[8,16,640]{2,1,0:T(8,128)(2,1)}), bf16[8,16,640]{2,1,0:T(8,128)(2,1)S(1)}, u32[]{:S(2)}, u32[]{:S(2)}) async-start(bf16[8,16,640]{2,1,0:T(8,128)(2,1)} %bitcast.3), calls=%async_computation | async-start | bytes 327680 | tf_op jit(solution)/shard_map/all_to_all | solution.py:473
  18.3 9.4 %all-to-all-start.1 = ((bf16[8,16,640]{2,1,0:T(8,128)(2,1)}), bf16[8,16,640]{2,1,0:T(8,128)(2,1)S(1)}, u32[]{:S(2)}, u32[]{:S(2)}) async-start(bf16[8,16,640]{2,1,0:T(8,128)(2,1)} %bitcast.7), calls=%async_computation.1 | async-start | bytes 327680 | tf_op jit(solution)/shard_map/all_to_all | solution.py:473
  28.3 3.0 %copy-start = (bf16[512,896]{1,0:T(8,128)(2,1)S(1)}, bf16[512,896]{1,0:T(8,128)(2,1)}, u32[]{:S(2)}) copy-start(bf16[512,896]{1,0:T(8,128)(2,1)} %get-tuple-element.32.weight_ref) | copy-start | bytes 2752516
  28.3 1.4 %collective-permute-start = (bf16[64,896]{1,0:T(8,128)(2,1)S(1)}, bf16[64,896]{1,0:T(8,128)(2,1)S(1)}, u32[]{:S(2)}, u32[]{:S(2)}) collective-permute-start(bf16[64,896]{1,0:T(8,128)(2,1)S(1)} %get-tuple-element.29), channel_id=1, source_target_pairs={{0,1},{1,0},{2,3},{3,2},{4,5},{5,4},{6,7},{7,6},{8,9},{9,8},{10,11... | collective-permute-start | bytes 344072 | tf_op jit(solution)/shard_map/ppermute | solution.py:479
  28.4 9.2 %copy-start.2 = (f32[896]{0:T(1024)S(1)}, f32[896]{0:T(1024)}, u32[]{:S(2)}) copy-start(f32[896]{0:T(1024)} %param.19) | copy-start | bytes 10756
  28.4 10.4 %copy-start.1 = (bf16[64,896]{1,0:T(8,128)(2,1)S(1)}, bf16[64,896]{1,0:T(8,128)(2,1)}, u32[]{:S(2)}) copy-start(bf16[64,896]{1,0:T(8,128)(2,1)} %hidden_ref.1) | copy-start | bytes 344068
  28.7 2.6 %collective-permute-start.2 = (bf16[64,896]{1,0:T(8,128)(2,1)S(1)}, bf16[64,896]{1,0:T(8,128)(2,1)S(1)}, u32[]{:S(2)}, u32[]{:S(2)}) collective-permute-start(bf16[64,896]{1,0:T(8,128)(2,1)S(1)} %shard_map.107), channel_id=1, source_target_pairs={{0,1},{1,0},{2,3},{3,2},{4,5},{5,4},{6,7},{7,6},{8,9},{9,8},{10,11... | collective-permute-start | bytes 344072 | tf_op jit(solution)/shard_map/ppermute | solution.py:479
  29.8 6.1 %collective-permute-start.1 = (bf16[64,896]{1,0:T(8,128)(2,1)S(1)}, bf16[64,896]{1,0:T(8,128)(2,1)S(1)}, u32[]{:S(2)}, u32[]{:S(2)}) collective-permute-start(bf16[64,896]{1,0:T(8,128)(2,1)S(1)} %get-tuple-element.31.after_ref), channel_id=1, source_target_pairs={{0,2},{1,3},{2,0},{3,1},{4,6},{5,7},{6,4},{7,5},{8,10},{9,11},{10,... | collective-permute-start | bytes 344072 | tf_op jit(solution)/shard_map/ppermute | solution.py:479
  31.7 5.8 %collective-permute-start.3 = (bf16[64,896]{1,0:T(8,128)(2,1)S(1)}, bf16[64,896]{1,0:T(8,128)(2,1)S(1)}, u32[]{:S(2)}, u32[]{:S(2)}) collective-permute-start(bf16[64,896]{1,0:T(8,128)(2,1)S(1)} %get-tuple-element.34), channel_id=1, source_target_pairs={{0,2},{1,3},{2,0},{3,1},{4,6},{5,7},{6,4},{7,5},{8,10},{9,11},{10,... | collective-permute-start | bytes 344072 | tf_op jit(solution)/shard_map/ppermute | solution.py:479
  37.6 1.3 %collective-permute-start.4 = (f32[64,128]{1,0:T(8,128)S(1)}, f32[64,128]{1,0:T(8,128)S(1)}, u32[]{:S(2)}, u32[]{:S(2)}) collective-permute-start(f32[64,128]{1,0:T(8,128)S(1)} %get-tuple-element.36.square_ref), channel_id=1, source_target_pairs={{0,1},{1,0},{2,3},{3,2},{4,5},{5,4},{6,7},{7,6},{8,9},{9,8},{10,11... | collective-permute-start | bytes 98312 | tf_op jit(solution)/shard_map/ppermute | solution.py:479

commit v8 on v7

--- a/solution.py
+++ b/solution.py
@@ -37,7 +37,7 @@
 
 
 def orders_of(replicas):
-    tuned = {8: ((4, 5, 6, 1, 0, 7, 2, 3), (5, 7, 2, 4, 6, 1, 3, 0))}
+    tuned = {8: ((4, 3, 5, 1, 0, 7, 6, 2), (5, 7, 2, 4, 6, 1, 3, 0))}
     return tuned.get(replicas, (tuple(range(replicas)),) * 2)
 
 

time: 40 us -> 39.6 us (0.990)
    all_to_all x2, starting transfers between devices: 13.6 us -> 13.1 us  [exchange(): lax.all_to_all(blocks, 'replica', split_axis=0, concat_axis=0, axis_index...]
where the time goes in v8:
time: 39.6 us; the launch traced here: 39.3 us
  starting transfers between devices  16 us (40%)
  Pallas kernels  14.9 us (38%)
  waiting for transfers between devices  8.23 us (21%)
    all_to_all x2, starting transfers between devices, exchange(): lax.all_to_all(blocks, 'replica', split_axis=0, concat_axis=0, axis_index...  13.1 us
    ppermute x5, waiting for transfers between devices, permute(): return lax.ppermute(x, 'tensor', [(i, i ^ bit) for i in range(ranks)])  6.59 us
    pallas_call x1, Pallas kernels, shards(): pl.pallas_call(functools.partial(prompt_kernel, chunk, fit, moves), out_s...  4.35 us
    pallas_call x1, Pallas kernels, shards(): pl.pallas_call(functools.partial(early_kernel, capacity, back_again, bloc...  3.48 us
    pallas_call x1, Pallas kernels, shards(): pl.pallas_call(functools.partial(late_kernel, block), out_shape=halves +...  2.96 us
    ppermute x5, starting transfers between devices, permute(): return lax.ppermute(x, 'tensor', [(i, i ^ bit) for i in range(ranks)])  2.84 us
    pallas_call x7, Pallas kernels, call(): pl.pallas_call(kernel, out_shape=outs, in_specs=specs, out_specs=jax.tree...  2.32 us
    pallas_call x1, Pallas kernels, shards(): pl.pallas_call(functools.partial(route_kernel, capacity, there), out_shap...  1.81 us
  transfers between devices with their start and end apart: 7, of which 6 were waited for; matrix products, arithmetic and copies ran while one was open for 0% of the time, Pallas kernels for 19%

profile of v8, /device:TPU:0, one launch (start us, length us, event | category | flops | bytes accessed | tf_op | source)
XLA Modules:
  0.0 39.3 jit_solution(13968233077551763439)
XLA Ops:
  0.0 1.8 %shard_map.100 = bf16[128,640]{1,0:T(8,128)(2,1)} custom-call(s32[1,64]{1,0:T(1,128)} %bitcast.11, s32[1,64]{1,0:T(1,128)} %bitcast.15, bf16[64,512]{1,0:T(8,128)(2,1)} %queries_hbm.5), custom_call_target="tpu_custom_call" | custom-call | tf_op jit(solution)/shard_map/pallas_call | solution.py:482
  1.8 7.8 %all-to-all-start = ((bf16[8,16,640]{2,1,0:T(8,128)(2,1)}), bf16[8,16,640]{2,1,0:T(8,128)(2,1)S(1)}, u32[]{:S(2)}, u32[]{:S(2)}) async-start(bf16[8,16,640]{2,1,0:T(8,128)(2,1)} %bitcast.3), calls=%async_computation | async-start | bytes 327680 | tf_op jit(solution)/shard_map/all_to_all | solution.py:473
  9.6 3.5 %shard_map.101 = (bf16[64,128]{1,0:T(8,128)(2,1)S(1)}, f32[32,512]{1,0:T(8,128)S(1)}, f32[32,256]{1,0:T(8,128)S(1)}, bf16[3,2048,256]{2,1,0:T(8,128)(2,1)S(1)}, bf16[512,896]{1,0:T(8,128)(2,1)}) custom-call(s32[1]{0:T(128)} %bitcast.5.core_ref, s32[1,64]{1,0:T(1,128)} %bitcast.12, s32[1,64]{1,0:T(1,128)} %bitcast.13, bf16[64,512]{1,0:T(8,128)(2,1)} %queries_hbm.5, ...), custom_call_target="tpu_custom_call" | custom-call | flops 67108864 | bytes 8388608 | tf_op jit(solution)/shard_map/pallas_call | solution.py:508
  13.1 1.0 %all-to-all-done = bf16[8,16,640]{2,1,0:T(8,128)(2,1)S(1)} async-done(((bf16[8,16,640]{2,1,0:T(8,128)(2,1)}), bf16[8,16,640]{2,1,0:T(8,128)(2,1)S(1)}, u32[]{:S(2)}, u32[]{:S(2)}) %all-to-all-start) | async-done | bytes 163872 | tf_op jit(solution)/shard_map/all_to_all | solution.py:473
  14.1 4.3 %shard_map.102.after_hbm = bf16[128,640]{1,0:T(8,128)(2,1)} custom-call(s32[4]{0:T(128)} %length_hbm.1, bf16[128,640]{1,0:T(8,128)(2,1)S(1)} %bitcast.10, bf16[3,2048,256]{2,1,0:T(8,128)(2,1)S(1)} %get-tuple-element.21.early_ref, bf16[4,2,2048,256]{3,2,1,0:T(8,128)(2,1)} %cache_hbm.4), custom_call_target="tpu_custom_call" | custom-call | tf_op jit(solution)/shard_map/pallas_call | solution.py:537
  18.4 5.3 %all-to-all-start.1 = ((bf16[8,16,640]{2,1,0:T(8,128)(2,1)}), bf16[8,16,640]{2,1,0:T(8,128)(2,1)S(1)}, u32[]{:S(2)}, u32[]{:S(2)}) async-start(bf16[8,16,640]{2,1,0:T(8,128)(2,1)} %bitcast.7), calls=%async_computation.1 | async-start | bytes 327680 | tf_op jit(solution)/shard_map/all_to_all | solution.py:473
  23.8 3.0 %shard_map.103 = (f32[32,512]{1,0:T(8,128)S(1)}, f32[32,256]{1,0:T(8,128)S(1)}, bf16[3,512,896]{2,1,0:T(8,128)(2,1)S(1)}) custom-call(s32[1]{0:T(128)} %bitcast.5.core_ref, s32[1,64]{1,0:T(1,128)} %bitcast.14, bf16[64,512]{1,0:T(8,128)(2,1)} %queries_hbm.5, bf16[64,2,64,256]{3,2,1,0:T(8,128)(2,1)} %cache_hbm.5, bf16[512,3584]{1,0:T(8,128)(2,1)} %weight_hbm.3, ...), custom_call_target="tpu_custom_call" | custom-call | flops 67108864 | bytes 5767168 | tf_op jit(solution)/shard_map/pallas_call | solution.py:561
  26.7 0.7 %all-to-all-done.1 = bf16[8,16,640]{2,1,0:T(8,128)(2,1)S(1)} async-done(((bf16[8,16,640]{2,1,0:T(8,128)(2,1)}), bf16[8,16,640]{2,1,0:T(8,128)(2,1)S(1)}, u32[]{:S(2)}, u32[]{:S(2)}) %all-to-all-start.1) | async-done | bytes 163872 | tf_op jit(solution)/shard_map/all_to_all | solution.py:473
  27.4 0.6 %shard_map.104 = (bf16[64,512]{1,0:T(8,128)(2,1)S(1)}, bf16[64,896]{1,0:T(8,128)(2,1)S(1)}) custom-call(bf16[128,640]{1,0:T(8,128)(2,1)S(1)} %bitcast.9, bf16[64,128]{1,0:T(8,128)(2,1)S(1)} %get-tuple-element.22.back_ref, f32[32,512]{1,0:T(8,128)S(1)} %get-tuple-element.23.num_a, f32[32,256]{1,0:T(8,128)S(1)} %get-tuple-element.24.den_a, ...), custom_call_target="tpu_custom_call" | custom-call | tf_op jit(solution)/shard_map/pallas_call | solution.py:426
  28.0 0.0 copy-start
  28.0 0.1 collective-permute-start
  28.1 0.0 copy-start.2
  28.1 0.0 copy-start.1
  28.1 0.3 shard_map.107
  28.4 0.5 %collective-permute-start.2 = (bf16[64,896]{1,0:T(8,128)(2,1)S(1)}, bf16[64,896]{1,0:T(8,128)(2,1)S(1)}, u32[]{:S(2)}, u32[]{:S(2)}) collective-permute-start(bf16[64,896]{1,0:T(8,128)(2,1)S(1)} %shard_map.107), channel_id=1, source_target_pairs={{0,1},{1,0},{2,3},{3,2},{4,5},{5,4},{6,7},{7,6},{8,9},{9,8},{10,11... | collective-permute-start | bytes 344072 | tf_op jit(solution)/shard_map/ppermute | solution.py:479
  28.9 0.3 shard_map.105.own_ref
  29.2 0.2 collective-permute-done.got_ref
  29.4 1.6 %collective-permute-start.1 = (bf16[64,896]{1,0:T(8,128)(2,1)S(1)}, bf16[64,896]{1,0:T(8,128)(2,1)S(1)}, u32[]{:S(2)}, u32[]{:S(2)}) collective-permute-start(bf16[64,896]{1,0:T(8,128)(2,1)S(1)} %get-tuple-element.31.after_ref), channel_id=1, source_target_pairs={{0,2},{1,3},{2,0},{3,1},{4,6},{5,7},{6,4},{7,5},{8,10},{9,11},{10,... | collective-permute-start | bytes 344072 | tf_op jit(solution)/shard_map/ppermute | solution.py:479
  31.0 0.0 collective-permute-done.2.got_ref
  31.0 0.0 copy-done
  31.0 0.3 shard_map.108
  31.3 0.6 %collective-permute-start.3 = (bf16[64,896]{1,0:T(8,128)(2,1)S(1)}, bf16[64,896]{1,0:T(8,128)(2,1)S(1)}, u32[]{:S(2)}, u32[]{:S(2)}) collective-permute-start(bf16[64,896]{1,0:T(8,128)(2,1)S(1)} %get-tuple-element.34), channel_id=1, source_target_pairs={{0,2},{1,3},{2,0},{3,1},{4,6},{5,7},{6,4},{7,5},{8,10},{9,11},{10,... | collective-permute-start | bytes 344072 | tf_op jit(solution)/shard_map/ppermute | solution.py:479
  31.9 3.6 %collective-permute-done.1.got_a = bf16[64,896]{1,0:T(8,128)(2,1)S(1)} collective-permute-done((bf16[64,896]{1,0:T(8,128)(2,1)S(1)}, bf16[64,896]{1,0:T(8,128)(2,1)S(1)}, u32[]{:S(2)}, u32[]{:S(2)}) %collective-permute-start.1) | collective-permute-done | bytes 114720 | tf_op jit(solution)/shard_map/ppermute | solution.py:479
  35.5 1.7 %collective-permute-done.3.got_b = bf16[64,896]{1,0:T(8,128)(2,1)S(1)} collective-permute-done((bf16[64,896]{1,0:T(8,128)(2,1)S(1)}, bf16[64,896]{1,0:T(8,128)(2,1)S(1)}, u32[]{:S(2)}, u32[]{:S(2)}) %collective-permute-start.3) | collective-permute-done | bytes 114720 | tf_op jit(solution)/shard_map/ppermute | solution.py:479
  37.1 0.1 shard_map.109
  37.2 0.1 collective-permute-start.4
  37.3 0.0 copy-done.2
  37.3 1.2 %collective-permute-done.4.got_ref = f32[64,128]{1,0:T(8,128)S(1)} collective-permute-done((f32[64,128]{1,0:T(8,128)S(1)}, f32[64,128]{1,0:T(8,128)S(1)}, u32[]{:S(2)}, u32[]{:S(2)}) %collective-permute-start.4) | collective-permute-done | bytes 32800 | tf_op jit(solution)/shard_map/ppermute | solution.py:479
  38.5 0.0 copy-done.1
  38.5 0.8 %shard_map.110 = bf16[64,896]{1,0:T(8,128)(2,1)} custom-call(f32[64,896]{1,0:T(8,128)S(1)} %get-tuple-element.35.mine_ref, f32[64,128]{1,0:T(8,128)S(1)} %get-tuple-element.36.square_ref, f32[64,128]{1,0:T(8,128)S(1)} %collective-permute-done.4.got_ref, f32[1,896]{1,0:T(1,128)S(1)} %reshape.39.gain_ref, bf16[64,896]{1,0:T(8,128)(2,1)S(1)} %copy-done.1), custom_call_target="tpu_custom_call" | custom-call | tf_op jit(solution)/shard_map/pallas_call | solution.py:426
  (2 shorter events, 0.0 us)
Async XLA Ops:
  1.8 12.3 %all-to-all-start = ((bf16[8,16,640]{2,1,0:T(8,128)(2,1)}), bf16[8,16,640]{2,1,0:T(8,128)(2,1)S(1)}, u32[]{:S(2)}, u32[]{:S(2)}) async-start(bf16[8,16,640]{2,1,0:T(8,128)(2,1)} %bitcast.3), calls=%async_computation | async-start | bytes 327680 | tf_op jit(solution)/shard_map/all_to_all | solution.py:473
  18.4 8.9 %all-to-all-start.1 = ((bf16[8,16,640]{2,1,0:T(8,128)(2,1)}), bf16[8,16,640]{2,1,0:T(8,128)(2,1)S(1)}, u32[]{:S(2)}, u32[]{:S(2)}) async-start(bf16[8,16,640]{2,1,0:T(8,128)(2,1)} %bitcast.7), calls=%async_computation.1 | async-start | bytes 327680 | tf_op jit(solution)/shard_map/all_to_all | solution.py:473
  28.0 3.0 %copy-start = (bf16[512,896]{1,0:T(8,128)(2,1)S(1)}, bf16[512,896]{1,0:T(8,128)(2,1)}, u32[]{:S(2)}) copy-start(bf16[512,896]{1,0:T(8,128)(2,1)} %get-tuple-element.32.weight_ref) | copy-start | bytes 2752516
  28.0 1.4 %collective-permute-start = (bf16[64,896]{1,0:T(8,128)(2,1)S(1)}, bf16[64,896]{1,0:T(8,128)(2,1)S(1)}, u32[]{:S(2)}, u32[]{:S(2)}) collective-permute-start(bf16[64,896]{1,0:T(8,128)(2,1)S(1)} %get-tuple-element.29), channel_id=1, source_target_pairs={{0,1},{1,0},{2,3},{3,2},{4,5},{5,4},{6,7},{7,6},{8,9},{9,8},{10,11... | collective-permute-start | bytes 344072 | tf_op jit(solution)/shard_map/ppermute | solution.py:479
  28.1 9.2 %copy-start.2 = (f32[896]{0:T(1024)S(1)}, f32[896]{0:T(1024)}, u32[]{:S(2)}) copy-start(f32[896]{0:T(1024)} %param.19) | copy-start | bytes 10756
  28.1 10.4 %copy-start.1 = (bf16[64,896]{1,0:T(8,128)(2,1)S(1)}, bf16[64,896]{1,0:T(8,128)(2,1)}, u32[]{:S(2)}) copy-start(bf16[64,896]{1,0:T(8,128)(2,1)} %hidden_ref.1) | copy-start | bytes 344068
  28.4 2.6 %collective-permute-start.2 = (bf16[64,896]{1,0:T(8,128)(2,1)S(1)}, bf16[64,896]{1,0:T(8,128)(2,1)S(1)}, u32[]{:S(2)}, u32[]{:S(2)}) collective-permute-start(bf16[64,896]{1,0:T(8,128)(2,1)S(1)} %shard_map.107), channel_id=1, source_target_pairs={{0,1},{1,0},{2,3},{3,2},{4,5},{5,4},{6,7},{7,6},{8,9},{9,8},{10,11... | collective-permute-start | bytes 344072 | tf_op jit(solution)/shard_map/ppermute | solution.py:479
  29.4 6.1 %collective-permute-start.1 = (bf16[64,896]{1,0:T(8,128)(2,1)S(1)}, bf16[64,896]{1,0:T(8,128)(2,1)S(1)}, u32[]{:S(2)}, u32[]{:S(2)}) collective-permute-start(bf16[64,896]{1,0:T(8,128)(2,1)S(1)} %get-tuple-element.31.after_ref), channel_id=1, source_target_pairs={{0,2},{1,3},{2,0},{3,1},{4,6},{5,7},{6,4},{7,5},{8,10},{9,11},{10,... | collective-permute-start | bytes 344072 | tf_op jit(solution)/shard_map/ppermute | solution.py:479
  31.3 5.8 %collective-permute-start.3 = (bf16[64,896]{1,0:T(8,128)(2,1)S(1)}, bf16[64,896]{1,0:T(8,128)(2,1)S(1)}, u32[]{:S(2)}, u32[]{:S(2)}) collective-permute-start(bf16[64,896]{1,0:T(8,128)(2,1)S(1)} %get-tuple-element.34), channel_id=1, source_target_pairs={{0,2},{1,3},{2,0},{3,1},{4,6},{5,7},{6,4},{7,5},{8,10},{9,11},{10,... | collective-permute-start | bytes 344072 | tf_op jit(solution)/shard_map/ppermute | solution.py:479
  37.2 1.3 %collective-permute-start.4 = (f32[64,128]{1,0:T(8,128)S(1)}, f32[64,128]{1,0:T(8,128)S(1)}, u32[]{:S(2)}, u32[]{:S(2)}) collective-permute-start(f32[64,128]{1,0:T(8,128)S(1)} %get-tuple-element.36.square_ref), channel_id=1, source_target_pairs={{0,1},{1,0},{2,3},{3,2},{4,5},{5,4},{6,7},{7,6},{8,9},{9,8},{10,11... | collective-permute-start | bytes 98312 | tf_op jit(solution)/shard_map/ppermute | solution.py:479

commit v9 on v8

--- a/solution.py
+++ b/solution.py
@@ -399,17 +399,24 @@
     send_ref[...] = total.astype(bf16)
 
 
-def square_kernel(row_ref, sum_a, got_a, sum_b, got_b, mine_ref, square_ref):
-    part = jnp.zeros(square_ref.shape, f32)
-    totals = []
-    for sum_ref, got_ref in ((sum_a, got_a), (sum_b, got_b)):
-        total = sum_ref[...] + got_ref[...].astype(f32)
-        for k in range(total.shape[1] // 128):
-            piece = total[:, k * 128 : (k + 1) * 128]
-            part = part + piece * piece
-        totals.append(total)
-    square_ref[...] = part
-    mine_ref[...] = jnp.where(row_ref[0] == 0, totals[0], totals[1])
+def squares(total):
+    part = jnp.zeros((total.shape[0], 128), f32)
+    for k in range(total.shape[1] // 128):
+        piece = total[:, k * 128 : (k + 1) * 128]
+        part = part + piece * piece
+    return part
+
+
+def first_square_kernel(sum_ref, got_ref, total_ref, square_ref):
+    total = sum_ref[...] + got_ref[...].astype(f32)
+    total_ref[...] = total
+    square_ref[...] = squares(total)
+
+
+def square_kernel(row_ref, total_ref, first_ref, sum_ref, got_ref, mine_ref, square_ref):
+    total = sum_ref[...] + got_ref[...].astype(f32)
+    square_ref[...] = first_ref[...] + squares(total)
+    mine_ref[...] = jnp.where(row_ref[0] == 0, total_ref[...], total)
 
 
 def final_kernel(features, mine_ref, square_ref, got_ref, gain_ref, hidden_ref, out_ref):
@@ -588,11 +595,9 @@
     far_a = permute(send_a, 2)
     sum_b, send_b = call(last_kernel, [block_f32, block_bf16], [attention, last, got_b, send_a])
     far_b = permute(send_b, 2)
-    mine, square = call(
-        square_kernel,
-        [block_f32, shape((requests, 128), f32)],
-        [far_row, sum_a, far_a, sum_b, far_b],
-    )
+    outs = [block_f32, shape((requests, 128), f32)]
+    total_a, square_a = call(first_square_kernel, outs, [sum_a, far_a])
+    mine, square = call(square_kernel, outs, [far_row, total_a, square_a, sum_b, far_b])
     beside = permute(square, 1)
     return call(
         functools.partial(final_kernel, features),

time: 39.6 us -> 39.6 us (level)
    pallas_call x7 -> x8, Pallas kernels: 2.32 us -> 2.32 us  [call(): pl.pallas_call(kernel, out_shape=outs, in_specs=specs, out_specs=jax.tree...]
where the time goes in v9:
time: 39.6 us; the launch traced here: 39.3 us
  starting transfers between devices  16 us (40%)
  Pallas kernels  15 us (38%)
  waiting for transfers between devices  8.17 us (21%)
    all_to_all x2, starting transfers between devices, exchange(): lax.all_to_all(blocks, 'replica', split_axis=0, concat_axis=0, axis_index...  13.1 us
    ppermute x5, waiting for transfers between devices, permute(): return lax.ppermute(x, 'tensor', [(i, i ^ bit) for i in range(ranks)])  6.56 us
    pallas_call x1, Pallas kernels, shards(): pl.pallas_call(functools.partial(prompt_kernel, chunk, fit, moves), out_s...  4.35 us
    pallas_call x1, Pallas kernels, shards(): pl.pallas_call(functools.partial(early_kernel, capacity, back_again, bloc...  3.49 us
    pallas_call x1, Pallas kernels, shards(): pl.pallas_call(functools.partial(late_kernel, block), out_shape=halves +...  2.96 us
    ppermute x5, starting transfers between devices, permute(): return lax.ppermute(x, 'tensor', [(i, i ^ bit) for i in range(ranks)])  2.84 us
    pallas_call x8, Pallas kernels, call(): pl.pallas_call(kernel, out_shape=outs, in_specs=specs, out_specs=jax.tree...  2.32 us
    pallas_call x1, Pallas kernels, shards(): pl.pallas_call(functools.partial(route_kernel, capacity, there), out_shap...  1.82 us
  transfers between devices with their start and end apart: 7, of which 6 were waited for; matrix products, arithmetic and copies ran while one was open for 0% of the time, Pallas kernels for 19%

profile of v9, /device:TPU:0, one launch (start us, length us, event | category | flops | bytes accessed | tf_op | source)
XLA Modules:
  0.0 39.3 jit_solution(9828253527859145885)
XLA Ops:
  0.0 1.8 %shard_map.100 = bf16[128,640]{1,0:T(8,128)(2,1)} custom-call(s32[1,64]{1,0:T(1,128)} %bitcast.11, s32[1,64]{1,0:T(1,128)} %bitcast.15, bf16[64,512]{1,0:T(8,128)(2,1)} %queries_hbm.5), custom_call_target="tpu_custom_call" | custom-call | tf_op jit(solution)/shard_map/pallas_call | solution.py:489
  1.8 7.8 %all-to-all-start = ((bf16[8,16,640]{2,1,0:T(8,128)(2,1)}), bf16[8,16,640]{2,1,0:T(8,128)(2,1)S(1)}, u32[]{:S(2)}, u32[]{:S(2)}) async-start(bf16[8,16,640]{2,1,0:T(8,128)(2,1)} %bitcast.3), calls=%async_computation | async-start | bytes 327680 | tf_op jit(solution)/shard_map/all_to_all | solution.py:480
  9.7 3.5 %shard_map.101 = (bf16[64,128]{1,0:T(8,128)(2,1)S(1)}, f32[32,512]{1,0:T(8,128)S(1)}, f32[32,256]{1,0:T(8,128)S(1)}, bf16[3,2048,256]{2,1,0:T(8,128)(2,1)S(1)}, bf16[512,896]{1,0:T(8,128)(2,1)}) custom-call(s32[1]{0:T(128)} %bitcast.5.core_ref, s32[1,64]{1,0:T(1,128)} %bitcast.12, s32[1,64]{1,0:T(1,128)} %bitcast.13, bf16[64,512]{1,0:T(8,128)(2,1)} %queries_hbm.5, ...), custom_call_target="tpu_custom_call" | custom-call | flops 67108864 | bytes 8388608 | tf_op jit(solution)/shard_map/pallas_call | solution.py:515
  13.2 0.9 %all-to-all-done = bf16[8,16,640]{2,1,0:T(8,128)(2,1)S(1)} async-done(((bf16[8,16,640]{2,1,0:T(8,128)(2,1)}), bf16[8,16,640]{2,1,0:T(8,128)(2,1)S(1)}, u32[]{:S(2)}, u32[]{:S(2)}) %all-to-all-start) | async-done | bytes 163872 | tf_op jit(solution)/shard_map/all_to_all | solution.py:480
  14.1 4.4 %shard_map.102.after_hbm = bf16[128,640]{1,0:T(8,128)(2,1)} custom-call(s32[4]{0:T(128)} %length_hbm.1, bf16[128,640]{1,0:T(8,128)(2,1)S(1)} %bitcast.10, bf16[3,2048,256]{2,1,0:T(8,128)(2,1)S(1)} %get-tuple-element.23.early_ref, bf16[4,2,2048,256]{3,2,1,0:T(8,128)(2,1)} %cache_hbm.4), custom_call_target="tpu_custom_call" | custom-call | tf_op jit(solution)/shard_map/pallas_call | solution.py:544
  18.5 5.3 %all-to-all-start.1 = ((bf16[8,16,640]{2,1,0:T(8,128)(2,1)}), bf16[8,16,640]{2,1,0:T(8,128)(2,1)S(1)}, u32[]{:S(2)}, u32[]{:S(2)}) async-start(bf16[8,16,640]{2,1,0:T(8,128)(2,1)} %bitcast.7), calls=%async_computation.1 | async-start | bytes 327680 | tf_op jit(solution)/shard_map/all_to_all | solution.py:480
  23.8 3.0 %shard_map.103 = (f32[32,512]{1,0:T(8,128)S(1)}, f32[32,256]{1,0:T(8,128)S(1)}, bf16[3,512,896]{2,1,0:T(8,128)(2,1)S(1)}) custom-call(s32[1]{0:T(128)} %bitcast.5.core_ref, s32[1,64]{1,0:T(1,128)} %bitcast.14, bf16[64,512]{1,0:T(8,128)(2,1)} %queries_hbm.5, bf16[64,2,64,256]{3,2,1,0:T(8,128)(2,1)} %cache_hbm.5, bf16[512,3584]{1,0:T(8,128)(2,1)} %weight_hbm.3, ...), custom_call_target="tpu_custom_call" | custom-call | flops 67108864 | bytes 5767168 | tf_op jit(solution)/shard_map/pallas_call | solution.py:568
  26.8 0.7 %all-to-all-done.1 = bf16[8,16,640]{2,1,0:T(8,128)(2,1)S(1)} async-done(((bf16[8,16,640]{2,1,0:T(8,128)(2,1)}), bf16[8,16,640]{2,1,0:T(8,128)(2,1)S(1)}, u32[]{:S(2)}, u32[]{:S(2)}) %all-to-all-start.1) | async-done | bytes 163872 | tf_op jit(solution)/shard_map/all_to_all | solution.py:480
  27.4 0.6 %shard_map.104 = (bf16[64,512]{1,0:T(8,128)(2,1)S(1)}, bf16[64,896]{1,0:T(8,128)(2,1)S(1)}) custom-call(bf16[128,640]{1,0:T(8,128)(2,1)S(1)} %bitcast.9, bf16[64,128]{1,0:T(8,128)(2,1)S(1)} %get-tuple-element.24.back_ref, f32[32,512]{1,0:T(8,128)S(1)} %get-tuple-element.25.num_a, f32[32,256]{1,0:T(8,128)S(1)} %get-tuple-element.26.den_a, ...), custom_call_target="tpu_custom_call" | custom-call | tf_op jit(solution)/shard_map/pallas_call | solution.py:433
  28.0 0.0 copy-start
  28.0 0.1 collective-permute-start
  28.1 0.0 copy-start.2
  28.1 0.0 copy-start.1
  28.1 0.3 shard_map.108
  28.4 0.5 %collective-permute-start.2 = (bf16[64,896]{1,0:T(8,128)(2,1)S(1)}, bf16[64,896]{1,0:T(8,128)(2,1)S(1)}, u32[]{:S(2)}, u32[]{:S(2)}) collective-permute-start(bf16[64,896]{1,0:T(8,128)(2,1)S(1)} %shard_map.108), channel_id=1, source_target_pairs={{0,1},{1,0},{2,3},{3,2},{4,5},{5,4},{6,7},{7,6},{8,9},{9,8},{10,11... | collective-permute-start | bytes 344072 | tf_op jit(solution)/shard_map/ppermute | solution.py:486
  29.0 0.3 shard_map.105.own_ref
  29.3 0.2 collective-permute-done.got_ref
  29.4 1.6 %collective-permute-start.1 = (bf16[64,896]{1,0:T(8,128)(2,1)S(1)}, bf16[64,896]{1,0:T(8,128)(2,1)S(1)}, u32[]{:S(2)}, u32[]{:S(2)}) collective-permute-start(bf16[64,896]{1,0:T(8,128)(2,1)S(1)} %get-tuple-element.33.after_ref), channel_id=1, source_target_pairs={{0,2},{1,3},{2,0},{3,1},{4,6},{5,7},{6,4},{7,5},{8,10},{9,11},{10,... | collective-permute-start | bytes 344072 | tf_op jit(solution)/shard_map/ppermute | solution.py:486
  31.0 0.0 collective-permute-done.2.got_ref
  31.0 0.0 copy-done
  31.0 0.3 shard_map.109
  31.3 0.6 %collective-permute-start.3 = (bf16[64,896]{1,0:T(8,128)(2,1)S(1)}, bf16[64,896]{1,0:T(8,128)(2,1)S(1)}, u32[]{:S(2)}, u32[]{:S(2)}) collective-permute-start(bf16[64,896]{1,0:T(8,128)(2,1)S(1)} %get-tuple-element.38), channel_id=1, source_target_pairs={{0,2},{1,3},{2,0},{3,1},{4,6},{5,7},{6,4},{7,5},{8,10},{9,11},{10,... | collective-permute-start | bytes 344072 | tf_op jit(solution)/shard_map/ppermute | solution.py:486
  31.9 3.6 %collective-permute-done.1.got_ref = bf16[64,896]{1,0:T(8,128)(2,1)S(1)} collective-permute-done((bf16[64,896]{1,0:T(8,128)(2,1)S(1)}, bf16[64,896]{1,0:T(8,128)(2,1)S(1)}, u32[]{:S(2)}, u32[]{:S(2)}) %collective-permute-start.1) | collective-permute-done | bytes 114720 | tf_op jit(solution)/shard_map/ppermute | solution.py:486
  35.5 1.6 %collective-permute-done.3.got_ref = bf16[64,896]{1,0:T(8,128)(2,1)S(1)} collective-permute-done((bf16[64,896]{1,0:T(8,128)(2,1)S(1)}, bf16[64,896]{1,0:T(8,128)(2,1)S(1)}, u32[]{:S(2)}, u32[]{:S(2)}) %collective-permute-start.3) | collective-permute-done | bytes 114720 | tf_op jit(solution)/shard_map/ppermute | solution.py:486
  37.2 0.1 collective-permute-start.4
  37.3 0.0 copy-done.2
  37.3 1.2 %collective-permute-done.4.got_ref = f32[64,128]{1,0:T(8,128)S(1)} collective-permute-done((f32[64,128]{1,0:T(8,128)S(1)}, f32[64,128]{1,0:T(8,128)S(1)}, u32[]{:S(2)}, u32[]{:S(2)}) %collective-permute-start.4) | collective-permute-done | bytes 32800 | tf_op jit(solution)/shard_map/ppermute | solution.py:486
  38.5 0.0 copy-done.1
  38.5 0.8 %shard_map.111 = bf16[64,896]{1,0:T(8,128)(2,1)} custom-call(f32[64,896]{1,0:T(8,128)S(1)} %get-tuple-element.39.mine_ref, f32[64,128]{1,0:T(8,128)S(1)} %get-tuple-element.40.square_ref, f32[64,128]{1,0:T(8,128)S(1)} %collective-permute-done.4.got_ref, f32[1,896]{1,0:T(1,128)S(1)} %reshape.39.gain_ref, bf16[64,896]{1,0:T(8,128)(2,1)S(1)} %copy-done.1), custom_call_target="tpu_custom_call" | custom-call | tf_op jit(solution)/shard_map/pallas_call | solution.py:433
  (4 shorter events, 0.1 us)
Async XLA Ops:
  1.8 12.3 %all-to-all-start = ((bf16[8,16,640]{2,1,0:T(8,128)(2,1)}), bf16[8,16,640]{2,1,0:T(8,128)(2,1)S(1)}, u32[]{:S(2)}, u32[]{:S(2)}) async-start(bf16[8,16,640]{2,1,0:T(8,128)(2,1)} %bitcast.3), calls=%async_computation | async-start | bytes 327680 | tf_op jit(solution)/shard_map/all_to_all | solution.py:480
  18.5 9.0 %all-to-all-start.1 = ((bf16[8,16,640]{2,1,0:T(8,128)(2,1)}), bf16[8,16,640]{2,1,0:T(8,128)(2,1)S(1)}, u32[]{:S(2)}, u32[]{:S(2)}) async-start(bf16[8,16,640]{2,1,0:T(8,128)(2,1)} %bitcast.7), calls=%async_computation.1 | async-start | bytes 327680 | tf_op jit(solution)/shard_map/all_to_all | solution.py:480
  28.0 3.0 %copy-start = (bf16[512,896]{1,0:T(8,128)(2,1)S(1)}, bf16[512,896]{1,0:T(8,128)(2,1)}, u32[]{:S(2)}) copy-start(bf16[512,896]{1,0:T(8,128)(2,1)} %get-tuple-element.36.weight_ref) | copy-start | bytes 2752516
  28.0 1.4 %collective-permute-start = (bf16[64,896]{1,0:T(8,128)(2,1)S(1)}, bf16[64,896]{1,0:T(8,128)(2,1)S(1)}, u32[]{:S(2)}, u32[]{:S(2)}) collective-permute-start(bf16[64,896]{1,0:T(8,128)(2,1)S(1)} %get-tuple-element.31), channel_id=1, source_target_pairs={{0,1},{1,0},{2,3},{3,2},{4,5},{5,4},{6,7},{7,6},{8,9},{9,8},{10,11... | collective-permute-start | bytes 344072 | tf_op jit(solution)/shard_map/ppermute | solution.py:486
  28.1 9.2 %copy-start.2 = (f32[896]{0:T(1024)S(1)}, f32[896]{0:T(1024)}, u32[]{:S(2)}) copy-start(f32[896]{0:T(1024)} %param.19) | copy-start | bytes 10756
  28.1 10.4 %copy-start.1 = (bf16[64,896]{1,0:T(8,128)(2,1)S(1)}, bf16[64,896]{1,0:T(8,128)(2,1)}, u32[]{:S(2)}) copy-start(bf16[64,896]{1,0:T(8,128)(2,1)} %hidden_ref.1) | copy-start | bytes 344068
  28.4 2.6 %collective-permute-start.2 = (bf16[64,896]{1,0:T(8,128)(2,1)S(1)}, bf16[64,896]{1,0:T(8,128)(2,1)S(1)}, u32[]{:S(2)}, u32[]{:S(2)}) collective-permute-start(bf16[64,896]{1,0:T(8,128)(2,1)S(1)} %shard_map.108), channel_id=1, source_target_pairs={{0,1},{1,0},{2,3},{3,2},{4,5},{5,4},{6,7},{7,6},{8,9},{9,8},{10,11... | collective-permute-start | bytes 344072 | tf_op jit(solution)/shard_map/ppermute | solution.py:486
  29.4 6.1 %collective-permute-start.1 = (bf16[64,896]{1,0:T(8,128)(2,1)S(1)}, bf16[64,896]{1,0:T(8,128)(2,1)S(1)}, u32[]{:S(2)}, u32[]{:S(2)}) collective-permute-start(bf16[64,896]{1,0:T(8,128)(2,1)S(1)} %get-tuple-element.33.after_ref), channel_id=1, source_target_pairs={{0,2},{1,3},{2,0},{3,1},{4,6},{5,7},{6,4},{7,5},{8,10},{9,11},{10,... | collective-permute-start | bytes 344072 | tf_op jit(solution)/shard_map/ppermute | solution.py:486
  31.3 5.8 %collective-permute-start.3 = (bf16[64,896]{1,0:T(8,128)(2,1)S(1)}, bf16[64,896]{1,0:T(8,128)(2,1)S(1)}, u32[]{:S(2)}, u32[]{:S(2)}) collective-permute-start(bf16[64,896]{1,0:T(8,128)(2,1)S(1)} %get-tuple-element.38), channel_id=1, source_target_pairs={{0,2},{1,3},{2,0},{3,1},{4,6},{5,7},{6,4},{7,5},{8,10},{9,11},{10,... | collective-permute-start | bytes 344072 | tf_op jit(solution)/shard_map/ppermute | solution.py:486
  37.2 1.3 %collective-permute-start.4 = (f32[64,128]{1,0:T(8,128)S(1)}, f32[64,128]{1,0:T(8,128)S(1)}, u32[]{:S(2)}, u32[]{:S(2)}) collective-permute-start(f32[64,128]{1,0:T(8,128)S(1)} %get-tuple-element.40.square_ref), channel_id=1, source_target_pairs={{0,1},{1,0},{2,3},{3,2},{4,5},{5,4},{6,7},{7,6},{8,9},{9,8},{10,11... | collective-permute-start | bytes 98312 | tf_op jit(solution)/shard_map/ppermute | solution.py:486

commit v10 on v9

--- a/solution.py
+++ b/solution.py
@@ -61,7 +61,7 @@
     copies = [pltpu.make_async_copy(a, b, sems.at[i]) for i, (a, b) in enumerate(pairs)]
     for copy in copies:
         copy.start()
-    for copy in copies:
+    for copy in copies[:2]:
         copy.wait()
     requests, width = queries_ref.shape
     slots = out_ref.shape[0]
@@ -69,6 +69,7 @@
     earlier = jnp.where((by_row == by_col) & (rows < cols), 1.0, 0.0)
     position = (by_col[:1] * capacity + jnp.sum(earlier, axis=0, keepdims=True)).astype(jnp.int32)
     matches = iota((slots, requests), 0) == position
+    copies[2].wait()
     out_ref[:, :width] = jnp.dot(
         jnp.where(matches, 1.0, 0.0).astype(bf16), queries_ref[...], preferred_element_type=f32
     ).astype(bf16)

time: 39.6 us -> 39.5 us (level)
  no operation moved by 1% of the time
where the time goes in v10:
time: 39.5 us; the launch traced here: 39.2 us
  starting transfers between devices  16 us (41%)
  Pallas kernels  14.9 us (38%)
  waiting for transfers between devices  8.17 us (21%)
    all_to_all x2, starting transfers between devices, exchange(): lax.all_to_all(blocks, 'replica', split_axis=0, concat_axis=0, axis_index...  13.1 us
    ppermute x5, waiting for transfers between devices, permute(): return lax.ppermute(x, 'tensor', [(i, i ^ bit) for i in range(ranks)])  6.56 us
    pallas_call x1, Pallas kernels, shards(): pl.pallas_call(functools.partial(prompt_kernel, chunk, fit, moves), out_s...  4.36 us
    pallas_call x1, Pallas kernels, shards(): pl.pallas_call(functools.partial(early_kernel, capacity, back_again, bloc...  3.49 us
    pallas_call x1, Pallas kernels, shards(): pl.pallas_call(functools.partial(late_kernel, block), out_shape=halves +...  2.96 us
    ppermute x5, starting transfers between devices, permute(): return lax.ppermute(x, 'tensor', [(i, i ^ bit) for i in range(ranks)])  2.84 us
    pallas_call x8, Pallas kernels, call(): pl.pallas_call(kernel, out_shape=outs, in_specs=specs, out_specs=jax.tree...  2.32 us
    pallas_call x1, Pallas kernels, shards(): pl.pallas_call(functools.partial(route_kernel, capacity, there), out_shap...  1.73 us
  transfers between devices with their start and end apart: 7, of which 6 were waited for; matrix products, arithmetic and copies ran while one was open for 0% of the time, Pallas kernels for 19%

profile of v10, /device:TPU:0, one launch (start us, length us, event | category | flops | bytes accessed | tf_op | source)
XLA Modules:
  0.0 39.2 jit_solution(16591254176372364181)
XLA Ops:
  0.0 1.7 %shard_map.100 = bf16[128,640]{1,0:T(8,128)(2,1)} custom-call(s32[1,64]{1,0:T(1,128)} %bitcast.11, s32[1,64]{1,0:T(1,128)} %bitcast.15, bf16[64,512]{1,0:T(8,128)(2,1)} %queries_hbm.5), custom_call_target="tpu_custom_call" | custom-call | tf_op jit(solution)/shard_map/pallas_call | solution.py:490
  1.7 7.8 %all-to-all-start = ((bf16[8,16,640]{2,1,0:T(8,128)(2,1)}), bf16[8,16,640]{2,1,0:T(8,128)(2,1)S(1)}, u32[]{:S(2)}, u32[]{:S(2)}) async-start(bf16[8,16,640]{2,1,0:T(8,128)(2,1)} %bitcast.3), calls=%async_computation | async-start | bytes 327680 | tf_op jit(solution)/shard_map/all_to_all | solution.py:481
  9.6 3.5 %shard_map.101 = (bf16[64,128]{1,0:T(8,128)(2,1)S(1)}, f32[32,512]{1,0:T(8,128)S(1)}, f32[32,256]{1,0:T(8,128)S(1)}, bf16[3,2048,256]{2,1,0:T(8,128)(2,1)S(1)}, bf16[512,896]{1,0:T(8,128)(2,1)}) custom-call(s32[1]{0:T(128)} %bitcast.5.core_ref, s32[1,64]{1,0:T(1,128)} %bitcast.12, s32[1,64]{1,0:T(1,128)} %bitcast.13, bf16[64,512]{1,0:T(8,128)(2,1)} %queries_hbm.5, ...), custom_call_target="tpu_custom_call" | custom-call | flops 67108864 | bytes 8388608 | tf_op jit(solution)/shard_map/pallas_call | solution.py:516
  13.1 0.9 %all-to-all-done = bf16[8,16,640]{2,1,0:T(8,128)(2,1)S(1)} async-done(((bf16[8,16,640]{2,1,0:T(8,128)(2,1)}), bf16[8,16,640]{2,1,0:T(8,128)(2,1)S(1)}, u32[]{:S(2)}, u32[]{:S(2)}) %all-to-all-start) | async-done | bytes 163872 | tf_op jit(solution)/shard_map/all_to_all | solution.py:481
  14.0 4.4 %shard_map.102.after_hbm = bf16[128,640]{1,0:T(8,128)(2,1)} custom-call(s32[4]{0:T(128)} %length_hbm.1, bf16[128,640]{1,0:T(8,128)(2,1)S(1)} %bitcast.10, bf16[3,2048,256]{2,1,0:T(8,128)(2,1)S(1)} %get-tuple-element.23.early_ref, bf16[4,2,2048,256]{3,2,1,0:T(8,128)(2,1)} %cache_hbm.4), custom_call_target="tpu_custom_call" | custom-call | tf_op jit(solution)/shard_map/pallas_call | solution.py:545
  18.4 5.3 %all-to-all-start.1 = ((bf16[8,16,640]{2,1,0:T(8,128)(2,1)}), bf16[8,16,640]{2,1,0:T(8,128)(2,1)S(1)}, u32[]{:S(2)}, u32[]{:S(2)}) async-start(bf16[8,16,640]{2,1,0:T(8,128)(2,1)} %bitcast.7), calls=%async_computation.1 | async-start | bytes 327680 | tf_op jit(solution)/shard_map/all_to_all | solution.py:481
  23.7 3.0 %shard_map.103 = (f32[32,512]{1,0:T(8,128)S(1)}, f32[32,256]{1,0:T(8,128)S(1)}, bf16[3,512,896]{2,1,0:T(8,128)(2,1)S(1)}) custom-call(s32[1]{0:T(128)} %bitcast.5.core_ref, s32[1,64]{1,0:T(1,128)} %bitcast.14, bf16[64,512]{1,0:T(8,128)(2,1)} %queries_hbm.5, bf16[64,2,64,256]{3,2,1,0:T(8,128)(2,1)} %cache_hbm.5, bf16[512,3584]{1,0:T(8,128)(2,1)} %weight_hbm.3, ...), custom_call_target="tpu_custom_call" | custom-call | flops 67108864 | bytes 5767168 | tf_op jit(solution)/shard_map/pallas_call | solution.py:569
  26.7 0.7 %all-to-all-done.1 = bf16[8,16,640]{2,1,0:T(8,128)(2,1)S(1)} async-done(((bf16[8,16,640]{2,1,0:T(8,128)(2,1)}), bf16[8,16,640]{2,1,0:T(8,128)(2,1)S(1)}, u32[]{:S(2)}, u32[]{:S(2)}) %all-to-all-start.1) | async-done | bytes 163872 | tf_op jit(solution)/shard_map/all_to_all | solution.py:481
  27.3 0.6 %shard_map.104 = (bf16[64,512]{1,0:T(8,128)(2,1)S(1)}, bf16[64,896]{1,0:T(8,128)(2,1)S(1)}) custom-call(bf16[128,640]{1,0:T(8,128)(2,1)S(1)} %bitcast.9, bf16[64,128]{1,0:T(8,128)(2,1)S(1)} %get-tuple-element.24.back_ref, f32[32,512]{1,0:T(8,128)S(1)} %get-tuple-element.25.num_a, f32[32,256]{1,0:T(8,128)S(1)} %get-tuple-element.26.den_a, ...), custom_call_target="tpu_custom_call" | custom-call | tf_op jit(solution)/shard_map/pallas_call | solution.py:434
  27.9 0.0 copy-start
  27.9 0.1 collective-permute-start
  28.0 0.0 copy-start.2
  28.0 0.0 copy-start.1
  28.0 0.3 shard_map.108
  28.3 0.5 %collective-permute-start.2 = (bf16[64,896]{1,0:T(8,128)(2,1)S(1)}, bf16[64,896]{1,0:T(8,128)(2,1)S(1)}, u32[]{:S(2)}, u32[]{:S(2)}) collective-permute-start(bf16[64,896]{1,0:T(8,128)(2,1)S(1)} %shard_map.108), channel_id=1, source_target_pairs={{0,1},{1,0},{2,3},{3,2},{4,5},{5,4},{6,7},{7,6},{8,9},{9,8},{10,11... | collective-permute-start | bytes 344072 | tf_op jit(solution)/shard_map/ppermute | solution.py:487
  28.9 0.3 shard_map.105.own_ref
  29.2 0.2 collective-permute-done.got_ref
  29.3 1.6 %collective-permute-start.1 = (bf16[64,896]{1,0:T(8,128)(2,1)S(1)}, bf16[64,896]{1,0:T(8,128)(2,1)S(1)}, u32[]{:S(2)}, u32[]{:S(2)}) collective-permute-start(bf16[64,896]{1,0:T(8,128)(2,1)S(1)} %get-tuple-element.33.after_ref), channel_id=1, source_target_pairs={{0,2},{1,3},{2,0},{3,1},{4,6},{5,7},{6,4},{7,5},{8,10},{9,11},{10,... | collective-permute-start | bytes 344072 | tf_op jit(solution)/shard_map/ppermute | solution.py:487
  30.9 0.0 collective-permute-done.2.got_ref
  30.9 0.0 copy-done
  30.9 0.3 shard_map.109
  31.2 0.6 %collective-permute-start.3 = (bf16[64,896]{1,0:T(8,128)(2,1)S(1)}, bf16[64,896]{1,0:T(8,128)(2,1)S(1)}, u32[]{:S(2)}, u32[]{:S(2)}) collective-permute-start(bf16[64,896]{1,0:T(8,128)(2,1)S(1)} %get-tuple-element.38), channel_id=1, source_target_pairs={{0,2},{1,3},{2,0},{3,1},{4,6},{5,7},{6,4},{7,5},{8,10},{9,11},{10,... | collective-permute-start | bytes 344072 | tf_op jit(solution)/shard_map/ppermute | solution.py:487
  31.8 3.6 %collective-permute-done.1.got_ref = bf16[64,896]{1,0:T(8,128)(2,1)S(1)} collective-permute-done((bf16[64,896]{1,0:T(8,128)(2,1)S(1)}, bf16[64,896]{1,0:T(8,128)(2,1)S(1)}, u32[]{:S(2)}, u32[]{:S(2)}) %collective-permute-start.1) | collective-permute-done | bytes 114720 | tf_op jit(solution)/shard_map/ppermute | solution.py:487
  35.4 1.6 %collective-permute-done.3.got_ref = bf16[64,896]{1,0:T(8,128)(2,1)S(1)} collective-permute-done((bf16[64,896]{1,0:T(8,128)(2,1)S(1)}, bf16[64,896]{1,0:T(8,128)(2,1)S(1)}, u32[]{:S(2)}, u32[]{:S(2)}) %collective-permute-start.3) | collective-permute-done | bytes 114720 | tf_op jit(solution)/shard_map/ppermute | solution.py:487
  37.1 0.1 collective-permute-start.4
  37.2 0.0 copy-done.2
  37.2 1.2 %collective-permute-done.4.got_ref = f32[64,128]{1,0:T(8,128)S(1)} collective-permute-done((f32[64,128]{1,0:T(8,128)S(1)}, f32[64,128]{1,0:T(8,128)S(1)}, u32[]{:S(2)}, u32[]{:S(2)}) %collective-permute-start.4) | collective-permute-done | bytes 32800 | tf_op jit(solution)/shard_map/ppermute | solution.py:487
  38.4 0.0 copy-done.1
  38.4 0.8 %shard_map.111 = bf16[64,896]{1,0:T(8,128)(2,1)} custom-call(f32[64,896]{1,0:T(8,128)S(1)} %get-tuple-element.39.mine_ref, f32[64,128]{1,0:T(8,128)S(1)} %get-tuple-element.40.square_ref, f32[64,128]{1,0:T(8,128)S(1)} %collective-permute-done.4.got_ref, f32[1,896]{1,0:T(1,128)S(1)} %reshape.39.gain_ref, bf16[64,896]{1,0:T(8,128)(2,1)S(1)} %copy-done.1), custom_call_target="tpu_custom_call" | custom-call | tf_op jit(solution)/shard_map/pallas_call | solution.py:434
  (4 shorter events, 0.1 us)
Async XLA Ops:
  1.7 12.3 %all-to-all-start = ((bf16[8,16,640]{2,1,0:T(8,128)(2,1)}), bf16[8,16,640]{2,1,0:T(8,128)(2,1)S(1)}, u32[]{:S(2)}, u32[]{:S(2)}) async-start(bf16[8,16,640]{2,1,0:T(8,128)(2,1)} %bitcast.3), calls=%async_computation | async-start | bytes 327680 | tf_op jit(solution)/shard_map/all_to_all | solution.py:481
  18.4 8.9 %all-to-all-start.1 = ((bf16[8,16,640]{2,1,0:T(8,128)(2,1)}), bf16[8,16,640]{2,1,0:T(8,128)(2,1)S(1)}, u32[]{:S(2)}, u32[]{:S(2)}) async-start(bf16[8,16,640]{2,1,0:T(8,128)(2,1)} %bitcast.7), calls=%async_computation.1 | async-start | bytes 327680 | tf_op jit(solution)/shard_map/all_to_all | solution.py:481
  27.9 3.0 %copy-start = (bf16[512,896]{1,0:T(8,128)(2,1)S(1)}, bf16[512,896]{1,0:T(8,128)(2,1)}, u32[]{:S(2)}) copy-start(bf16[512,896]{1,0:T(8,128)(2,1)} %get-tuple-element.36.weight_ref) | copy-start | bytes 2752516
  27.9 1.4 %collective-permute-start = (bf16[64,896]{1,0:T(8,128)(2,1)S(1)}, bf16[64,896]{1,0:T(8,128)(2,1)S(1)}, u32[]{:S(2)}, u32[]{:S(2)}) collective-permute-start(bf16[64,896]{1,0:T(8,128)(2,1)S(1)} %get-tuple-element.31), channel_id=1, source_target_pairs={{0,1},{1,0},{2,3},{3,2},{4,5},{5,4},{6,7},{7,6},{8,9},{9,8},{10,11... | collective-permute-start | bytes 344072 | tf_op jit(solution)/shard_map/ppermute | solution.py:487
  28.0 9.2 %copy-start.2 = (f32[896]{0:T(1024)S(1)}, f32[896]{0:T(1024)}, u32[]{:S(2)}) copy-start(f32[896]{0:T(1024)} %param.19) | copy-start | bytes 10756
  28.0 10.4 %copy-start.1 = (bf16[64,896]{1,0:T(8,128)(2,1)S(1)}, bf16[64,896]{1,0:T(8,128)(2,1)}, u32[]{:S(2)}) copy-start(bf16[64,896]{1,0:T(8,128)(2,1)} %hidden_ref.1) | copy-start | bytes 344068
  28.3 2.6 %collective-permute-start.2 = (bf16[64,896]{1,0:T(8,128)(2,1)S(1)}, bf16[64,896]{1,0:T(8,128)(2,1)S(1)}, u32[]{:S(2)}, u32[]{:S(2)}) collective-permute-start(bf16[64,896]{1,0:T(8,128)(2,1)S(1)} %shard_map.108), channel_id=1, source_target_pairs={{0,1},{1,0},{2,3},{3,2},{4,5},{5,4},{6,7},{7,6},{8,9},{9,8},{10,11... | collective-permute-start | bytes 344072 | tf_op jit(solution)/shard_map/ppermute | solution.py:487
  29.3 6.1 %collective-permute-start.1 = (bf16[64,896]{1,0:T(8,128)(2,1)S(1)}, bf16[64,896]{1,0:T(8,128)(2,1)S(1)}, u32[]{:S(2)}, u32[]{:S(2)}) collective-permute-start(bf16[64,896]{1,0:T(8,128)(2,1)S(1)} %get-tuple-element.33.after_ref), channel_id=1, source_target_pairs={{0,2},{1,3},{2,0},{3,1},{4,6},{5,7},{6,4},{7,5},{8,10},{9,11},{10,... | collective-permute-start | bytes 344072 | tf_op jit(solution)/shard_map/ppermute | solution.py:487
  31.2 5.8 %collective-permute-start.3 = (bf16[64,896]{1,0:T(8,128)(2,1)S(1)}, bf16[64,896]{1,0:T(8,128)(2,1)S(1)}, u32[]{:S(2)}, u32[]{:S(2)}) collective-permute-start(bf16[64,896]{1,0:T(8,128)(2,1)S(1)} %get-tuple-element.38), channel_id=1, source_target_pairs={{0,2},{1,3},{2,0},{3,1},{4,6},{5,7},{6,4},{7,5},{8,10},{9,11},{10,... | collective-permute-start | bytes 344072 | tf_op jit(solution)/shard_map/ppermute | solution.py:487
  37.1 1.3 %collective-permute-start.4 = (f32[64,128]{1,0:T(8,128)S(1)}, f32[64,128]{1,0:T(8,128)S(1)}, u32[]{:S(2)}, u32[]{:S(2)}) collective-permute-start(f32[64,128]{1,0:T(8,128)S(1)} %get-tuple-element.40.square_ref), channel_id=1, source_target_pairs={{0,1},{1,0},{2,3},{3,2},{4,5},{5,4},{6,7},{7,6},{8,9},{9,8},{10,11... | collective-permute-start | bytes 98312 | tf_op jit(solution)/shard_map/ppermute | solution.py:487
